TPU v7x, 256 devices: a whole 4x4x8 slice. The times are simulated.
256 devices in a mesh: dp: 64 (over z_hi, y, x), tensor: 4 (over z_lo, core).
Axes of the slice: x: 4, y: 4, z: 8 (z_hi: 4, z_lo: 2; z = z_hi * 2 + z_lo), core: 2. Of those that a mesh axis runs over, the one named last changes fastest.
Arguments:
- acts: bfloat16 [65536, 8192], P(('dp', 'tensor')), may hold values from -24 to 24
- grad_out: bfloat16 [65536, 1024], P(('dp', 'tensor')), may hold values from -0.0234375 to 0.0234375
- master: float32 [8192, 1024], P('dp', 'tensor'), may hold values from -0.125 to 0.125
- moment1: float32 [8192, 1024], P('dp', 'tensor'), may hold values from -1.75 to 1.75
- moment2: float32 [8192, 1024], P('dp', 'tensor'), may hold values from 0.0001 to 0.002
Outputs:
- new_master: float32 [8192, 1024], P('dp', 'tensor')
- new_moment1: float32 [8192, 1024], P('dp', 'tensor')
- new_moment2: float32 [8192, 1024], P('dp', 'tensor')
- new_weights: bfloat16 [8192, 1024], P(None, 'tensor')
All inputs are finite; a program needn't handle non-finite values.
Results may differ from a plain program's by a relative error of at most 0.001.
Values may be sent and summed in bfloat16 or wider, within the bound.
No kernel may reach another device: no remote copies, remote signals or barrier semaphores. Data moves between devices by JAX's collectives and lax.ppermute only.
A program may use at most 128 MiB of HBM per device.

v0:
```python
import math

import jax
import jax.numpy as jnp
from jax import lax
from jax.sharding import PartitionSpec as P

first_bias = 1.0 - math.exp(100.0 * math.log(0.9))
second_bias = 1.0 - math.exp(100.0 * math.log(0.999))


def per_device(acts, grad_out, master, moment1, moment2):
    contract = (((0,), (0,)), ((), ()))
    group_acts = lax.all_gather(acts, "tensor", axis=0, tiled=True)
    group_grad = lax.all_to_all(grad_out, "tensor", split_axis=1, concat_axis=0, tiled=True)
    grad = lax.psum_scatter(
        lax.dot_general(group_acts, group_grad, contract, preferred_element_type=jnp.float32),
        "dp",
        scatter_dimension=0,
        tiled=True,
    )
    new_moment1 = 0.9 * moment1 + 0.1 * grad
    new_moment2 = 0.999 * moment2 + 0.001 * grad * grad
    update = new_moment1 / first_bias / (jnp.sqrt(new_moment2 / second_bias) + 1e-08)
    new_master = master - 0.01 * (update + 0.1 * master)
    new_weights = lax.all_gather(new_master.astype(jnp.bfloat16), "dp", axis=0, tiled=True)
    return (new_master, new_moment1, new_moment2, new_weights)


def solution(mesh):
    in_specs = (
        P(("dp", "tensor"), None),
        P(("dp", "tensor"), None),
        P("dp", "tensor"),
        P("dp", "tensor"),
        P("dp", "tensor"),
    )
    out_specs = (P("dp", "tensor"), P("dp", "tensor"), P("dp", "tensor"), P(None, "tensor"))
    return jax.shard_map(
        per_device, mesh=mesh, in_specs=in_specs, out_specs=out_specs, check_vma=False
    )
```

profile of v0, /device:TPU:2, one launch (start us, length us, event | category | flops | bytes accessed | tf_op | source)
XLA Modules:
  0.0 685.2 jit_solution(11875357221226675304)
XLA Ops:
  7.2 0.0 all-gather.3.cloned.1.call-start
  7.2 0.7 all-gather.3.cloned.1.call-update
  7.9 0.0 reduce-scatter.2.cloned.1.call-start
  7.9 1.2 copy.9
  9.2 11.8 %all_to_all.19 = bf16[256,4,256]{0,2,1:T(8,128)(2,1)S(1)} all-to-all(bf16[256,4,256]{0,2,1:T(8,128)(2,1)S(1)} %bitcast.6), channel_id=1, replica_groups=mesh['dp'=64,'tensor'=4] {'tensor'}, dimensions={1} | all-to-all | bytes 1048576 | tf_op jit(solution)/shard_map/all_to_all | solution.py:15
  21.0 0.2 copy.10
  21.2 143.5 %all-gather.3.cloned.1.call-done = bf16[1024,8192]{1,0:T(8,128)(2,1)} async-done(((bf16[256,8192]{1,0:T(8,128)(2,1)}), bf16[1024,8192]{1,0:T(8,128)(2,1)}) %all-gather.3.cloned.1.call-update) | async-done | bytes 16777232 | tf_op jit(solution)/shard_map/all_gather | solution.py:14
  164.8 13.7 %fusion.3 = f32[8192,256]{1,0:T(8,128)} fusion(bf16[1024,8192]{1,0:T(8,128)(2,1)} %all-gather.3.cloned.1.call-done, bf16[1024,256]{1,0:T(8,128)(2,1)S(1)} %bitcast.7), kind=kOutput, calls=%fused_computation.5 | convolution fusion | flops 4294967296 | bytes 25690112 | tf_op jit(solution)/shard_map/dot_general | solution.py:17
  178.5 0.0 copy-start
  178.5 0.0 copy-start.1
  178.5 0.0 copy-start.2
  178.5 0.0 reduce-scatter.2.cloned.1.call-update
  178.5 0.0 all-gather.5.cloned.1.call-start
  178.6 404.0 %reduce-scatter.2.cloned.1.call-done = f32[128,256]{1,0:T(8,128)} async-done(((f32[8192,256]{1,0:T(8,128)}), f32[128,256]{1,0:T(8,128)}) %reduce-scatter.2.cloned.1.call-update) | async-done | bytes 131088 | tf_op jit(solution)/shard_map/reduce_scatter | solution.py:16
  582.6 0.0 copy-done
  582.6 0.0 copy-done.1
  582.6 0.0 copy-done.2
  582.6 1.7 fusion.1
  584.3 0.0 all-gather.5.cloned.1.call-update
  584.4 89.8 %all-gather.5.cloned.1.call-done = bf16[8192,256]{1,0:T(8,128)(2,1)} async-done(((bf16[128,256]{1,0:T(8,128)(2,1)}), bf16[8192,256]{1,0:T(8,128)(2,1)}) %all-gather.5.cloned.1.call-update) | async-done | bytes 4194320 | tf_op jit(solution)/shard_map/all_gather | solution.py:26
  674.2 4.5 copy.12
Async XLA Ops:
  7.2 157.6 %all-gather.3.cloned.1.call-start = ((), (), s32[]{:S(2)}) async-start(), calls=%async_computation.2 | async-start | bytes 20971520 | tf_op jit(solution)/shard_map/all_gather | solution.py:14
  7.9 574.7 %reduce-scatter.2.cloned.1.call-start = ((), (), s32[]{:S(2)}) async-start(), calls=%async_computation.3 | async-start | bytes 8519680 | tf_op jit(solution)/shard_map/reduce_scatter | solution.py:16
  178.5 404.1 %copy-start = (f32[128,256]{1,0:T(8,128)S(1)}, f32[128,256]{1,0:T(8,128)}, u32[]{:S(2)}) copy-start(f32[128,256]{1,0:T(8,128)} %param.7) | copy-start | bytes 393220
  178.5 404.1 %copy-start.1 = (f32[128,256]{1,0:T(8,128)S(1)}, f32[128,256]{1,0:T(8,128)}, u32[]{:S(2)}) copy-start(f32[128,256]{1,0:T(8,128)} %param.8) | copy-start | bytes 393220
  178.5 404.1 %copy-start.2 = (f32[128,256]{1,0:T(8,128)S(1)}, f32[128,256]{1,0:T(8,128)}, u32[]{:S(2)}) copy-start(f32[128,256]{1,0:T(8,128)} %param.9) | copy-start | bytes 393220
  178.5 495.7 %all-gather.5.cloned.1.call-start = ((), (), s32[]{:S(2)}) async-start(), calls=%async_computation.4 | async-start | bytes 4259840 | tf_op jit(solution)/shard_map/all_gather | solution.py:26
Sparse Core Ops, SparseCore 0:
  9.8 154.9 all-gather.2
  178.6 403.9 reduce-scatter.1
  586.5 87.6 all-gather.4
where the time goes:
time: 686 us; the launch traced here: 685 us
  waiting for transfers between devices  638 us (93%)
  between operations  13.8 us (2%)
  matrix products  13.7 us (2%)
  blocking collectives  11.8 us (2%)
    reduce_scatter x1, waiting for transfers between devices, per_device(): lax.psum_scatter(lax.dot_general(group_acts, group_grad, contract, prefer...  404 us
    all_gather x1, waiting for transfers between devices, per_device(): group_acts = lax.all_gather(acts, 'tensor', axis=0, tiled=True)  144 us
    all_gather x1, waiting for transfers between devices, per_device(): lax.all_gather(new_master.astype(jnp.bfloat16), 'dp', axis=0, tiled=True)  89.8 us
    dot_general x1, matrix products, per_device(): lax.dot_general(group_acts, group_grad, contract, preferred_element_type=...  13.7 us
  transfers between devices with their start and end apart: 3, of which 3 were waited for; matrix products, arithmetic and copies ran while one was open for 0% of the time, Pallas kernels for 0%

commit v1 on v0

v1 whole, which is shorter than its diff:
```python
import math

import jax
import jax.numpy as jnp
from jax import lax
from jax.experimental import pallas as pl
from jax.experimental.pallas import tpu as pltpu
from jax.sharding import Mesh
from jax.sharding import PartitionSpec as P

first_bias = 1.0 - math.exp(100.0 * math.log(0.9))
second_bias = 1.0 - math.exp(100.0 * math.log(0.999))

F32, F16, BF16 = jnp.float32, jnp.float16, jnp.bfloat16
LANES = 128


def shift(array, axis, by, size=4):
    return lax.ppermute(array, axis, [(i, (i + by) % size) for i in range(size)])


def other_core(array):
    return lax.ppermute(array, "c", [(0, 1), (1, 0)])


def arrange(acts, where):
    tokens = acts.shape[0]

    def kernel(where_ref, acts_ref, out_ref, sem):
        x, y = where_ref[0], where_ref[1]
        copies = []
        for colour in range(2):
            for first in range(4):
                for second in range(4):
                    kx, ky = (first, second) if colour == 0 else (second, first)
                    for half in range(2):
                        block = (
                            (2 * colour + half) * 16
                            + lax.rem(y + ky, 4) * 4
                            + lax.rem(x + kx, 4)
                        )
                        copies.append(
                            pltpu.make_async_copy(
                                acts_ref.at[
                                    :, pl.ds(pl.multiple_of(block * LANES, LANES), LANES)
                                ],
                                out_ref.at[
                                    colour * 4 + first,
                                    :,
                                    pl.ds((second * 2 + half) * LANES, LANES),
                                ],
                                sem,
                            )
                        )
        for copy in copies:
            copy.start()
        for copy in copies:
            copy.wait()

    return pl.pallas_call(
        kernel,
        out_shape=jax.ShapeDtypeStruct((8, tokens, 1024), acts.dtype),
        in_specs=[
            pl.BlockSpec(memory_space=pltpu.SMEM),
            pl.BlockSpec(memory_space=pl.ANY),
        ],
        out_specs=pl.BlockSpec(memory_space=pl.ANY),
        scratch_shapes=[pltpu.SemaphoreType.DMA],
        cost_estimate=pl.CostEstimate(
            flops=0, bytes_accessed=4 * acts.size, transcendentals=0
        ),
    )(where, acts)


def assemble(pieces, where):
    def kernel(where_ref, *refs):
        ins, out_ref, sem = refs[:8], refs[8], refs[9]
        x, y, zh = where_ref[0], where_ref[1], where_ref[2]
        copies = []
        for colour in range(2):
            for first in range(4):
                for second in range(4):
                    kx, ky = (second, first) if colour == 0 else (first, second)
                    for half in range(2):
                        kz = 2 * colour + half
                        block = (
                            lax.rem(zh + 4 - kz, 4) * 16
                            + lax.rem(y + 4 - ky, 4) * 4
                            + lax.rem(x + 4 - kx, 4)
                        )
                        copies.append(
                            pltpu.make_async_copy(
                                ins[colour * 4 + first].at[
                                    pl.ds((second * 2 + half) * LANES, LANES), :
                                ],
                                out_ref.at[
                                    pl.ds(pl.multiple_of(block * LANES, LANES), LANES), :
                                ],
                                sem,
                            )
                        )
        for copy in copies:
            copy.start()
        for copy in copies:
            copy.wait()

    return pl.pallas_call(
        kernel,
        out_shape=jax.ShapeDtypeStruct((8192, 256), BF16),
        in_specs=[pl.BlockSpec(memory_space=pltpu.SMEM)]
        + [pl.BlockSpec(memory_space=pl.ANY)] * 8,
        out_specs=pl.BlockSpec(memory_space=pl.ANY),
        scratch_shapes=[pltpu.SemaphoreType.DMA],
    )(where, *pieces[0], *pieces[1])


def dot(a, b):
    return lax.dot_general(a, b, (((0,), (0,)), ((), ())), preferred_element_type=F32)


def per_device(acts, grad_out, master, moment1, moment2):
    x, y, zh, core = (lax.axis_index(name) for name in ("x", "y", "zh", "c"))
    where = jnp.stack([x, y, zh]).astype(jnp.int32)

    parts = grad_out.reshape(-1, 2, 2, 256)
    mine = jnp.where(core == 0, parts[:, :, 0], parts[:, :, 1]).reshape(-1, 512)
    theirs = jnp.where(core == 0, parts[:, :, 1], parts[:, :, 0]).reshape(-1, 512)
    peer_grad = other_core(theirs)
    chunks = arrange(acts, where)
    order = (2, 6, 1, 5, 3, 7, 0, 4)
    partial = {}
    for i in order:
        peer = other_core(chunks[i])
        partial[i] = dot(chunks[i], mine) + dot(peer, peer_grad)

    def reduce(parts_by_distance, axis, scale):
        total = parts_by_distance[0]
        for by in (2, 1, 3):
            sent = (parts_by_distance[by] * scale).astype(F16)
            total = total + shift(sent, axis, by).astype(F32) * (1.0 / scale)
        return total

    sum_x = reduce([partial[k] for k in range(4)], "x", 128.0)
    sum_y = reduce([partial[4 + k] for k in range(4)], "y", 128.0)
    sum_xy = reduce([sum_x[k * 256 : (k + 1) * 256] for k in range(4)], "y", 32.0)
    sum_yx = reduce([sum_y[k * 256 : (k + 1) * 256] for k in range(4)], "x", 32.0)
    level = jnp.concatenate([sum_xy, sum_yx], 0)
    level = (level * 8.0).astype(F16).reshape(4, 128, 2, 256).transpose(0, 2, 1, 3)
    level = lax.all_to_all(level.reshape(8, 128, 256), ("zh", "zl"), 0, 0, tiled=True)
    grad = jnp.sum(level.astype(F32), 0) * 0.125

    new_moment1 = 0.9 * moment1 + 0.1 * grad
    new_moment2 = 0.999 * moment2 + 0.001 * grad * grad
    update = new_moment1 / first_bias / (jnp.sqrt(new_moment2 / second_bias) + 1e-08)
    new_master = master - 0.01 * (update + 0.1 * master)

    own = new_master.astype(BF16)
    z = [own] + [shift(own, "zh", k) for k in (1, 2, 3)]
    first = jnp.concatenate([z[0], z[1]], 0)
    second = jnp.concatenate([z[2], z[3]], 0)
    first = jnp.concatenate([first] + [shift(first, "x", k) for k in (1, 2, 3)], 0)
    second = jnp.concatenate([second] + [shift(second, "y", k) for k in (1, 2, 3)], 0)
    first = [first] + [shift(first, "y", k) for k in (1, 2, 3)]
    second = [second] + [shift(second, "x", k) for k in (1, 2, 3)]
    new_weights = assemble((first, second), where)
    return (new_master, new_moment1, new_moment2, new_weights)


def solution(mesh):
    fine = Mesh(mesh.devices.reshape(4, 4, 4, 2, 2), ("zh", "y", "x", "zl", "c"))
    dp, tensor = ("zh", "y", "x"), ("zl", "c")
    tokens, state = P(dp + tensor, None), P(dp, tensor)
    return jax.shard_map(
        per_device,
        mesh=fine,
        in_specs=(tokens, tokens, state, state, state),
        out_specs=(state, state, state, P(None, tensor)),
        check_vma=False,
    )
```

time: 686 us -> 442 us (0.64)
  waiting for transfers between devices: 638 us -> 77.1 us
  Pallas kernels: 0 us -> 258 us
  starting transfers between devices: 0.12 us -> 58.9 us
  blocking collectives: 11.8 us -> 24.7 us
  between operations: 13.8 us -> 1.25 us
    reduce_scatter x1 -> x0, waiting for transfers between devices: 404 us -> none  [per_device(): lax.psum_scatter(lax.dot_general(group_acts, group_grad, contract, prefer...]
    pallas_call x0 -> x2, Pallas kernels: none -> 258 us  [the longest x1 129 us: assemble(): pl.pallas_call(kernel, out_shape=jax.ShapeDtypeStruct((8192, 256), BF16),...]
    all_gather x2 -> x0, waiting for transfers between devices: 233 us -> none  [the longest x1 144 us: per_device(): group_acts = lax.all_gather(acts, 'tensor', axis=0, tiled=True)]
    ppermute x0 -> x36, waiting for transfers between devices: none -> 77.1 us  [the longest x27 77.1 us: shift(): lax.ppermute(array, axis, [(i, (i + by) % size) for i in range(size)])]
    ppermute x0 -> x36, starting transfers between devices: none -> 58.9 us  [the longest x27 56.5 us: shift(): lax.ppermute(array, axis, [(i, (i + by) % size) for i in range(size)])]
    all_to_all x1, blocking collectives: 11.8 us -> 24.7 us  [per_device(): lax.all_to_all(level.reshape(8, 128, 256), ('zh', 'zl'), 0, 0, tiled=True)]
    dot_general x1 -> x16, matrix products: 13.7 us -> 11.1 us  [dot(): lax.dot_general(a, b, (((0,), (0,)), ((), ())), preferred_element_type=F32)]
  transfers between devices with their start and end apart: 3 -> 36, of which waited for: 3 -> 15; matrix products, arithmetic and copies ran while one was open for 0% -> 3% of each run, Pallas kernels for 0% -> 0%
where the time goes in v1:
time: 442 us; the launch traced here: 441 us
  Pallas kernels  258 us (58%)
  waiting for transfers between devices  77.1 us (17%)
  starting transfers between devices  58.9 us (13%)
  blocking collectives  24.7 us (6%)
  matrix products  11.1 us (3%)
  local copies, waits for them, and re-layouts  6.38 us (1%)
    pallas_call x1, Pallas kernels, assemble(): pl.pallas_call(kernel, out_shape=jax.ShapeDtypeStruct((8192, 256), BF16),...  129 us
    pallas_call x1, Pallas kernels, arrange(): pl.pallas_call(kernel, out_shape=jax.ShapeDtypeStruct((8, tokens, 1024),...  129 us
    ppermute x27, waiting for transfers between devices, shift(): lax.ppermute(array, axis, [(i, (i + by) % size) for i in range(size)])  77.1 us
    ppermute x27, starting transfers between devices, shift(): lax.ppermute(array, axis, [(i, (i + by) % size) for i in range(size)])  56.5 us
    all_to_all x1, blocking collectives, per_device(): lax.all_to_all(level.reshape(8, 128, 256), ('zh', 'zl'), 0, 0, tiled=True)  24.7 us
    dot_general x16, matrix products, dot(): lax.dot_general(a, b, (((0,), (0,)), ((), ())), preferred_element_type=F32)  11.1 us
  transfers between devices with their start and end apart: 36, of which 15 were waited for; matrix products, arithmetic and copies ran while one was open for 3% of the time, Pallas kernels for 0%

profile of v1, /device:TPU:2, one launch (start us, length us, event | category | flops | bytes accessed | tf_op | source)
XLA Modules:
  0.0 441.3 jit_solution(1330793673819437035)
XLA Ops:
  1.3 128.8 %shard_map.84 = bf16[8,256,1024]{2,1,0:T(8,128)(2,1)} custom-call(s32[3]{0:T(128)} %pad_add_fusion.where_ref, bf16[256,8192]{1,0:T(8,128)(2,1)} %acts_ref.1), custom_call_target="tpu_custom_call" | custom-call | bytes 8388608 | tf_op jit(solution)/shard_map/pallas_call | solution.py:60
  130.2 3.8 slice_bitcast_fusion.7
  136.5 1.7 fusion.12
  138.2 1.5 fusion.13
  145.9 2.2 collective-permute-start.3
  149.2 1.9 collective-permute-start.5
  152.5 3.3 collective-permute-start.13
  156.5 17.0 %collective-permute-done.3 = f16[1024,512]{1,0:T(8,128)(2,1)S(1)} collective-permute-done((f16[1024,512]{1,0:T(8,128)(2,1)S(1)}, f16[1024,512]{1,0:T(8,128)(2,1)S(1)}, u32[]{:S(2)}, u32[]{:S(2)}) %collective-permute-start.3) | collective-permute-done | bytes 1048608 | tf_op jit(solution)/shard_map/ppermute | solution.py:19
  173.5 3.0 collective-permute-start.17
  177.5 17.7 %collective-permute-done.5 = f16[1024,512]{1,0:T(8,128)(2,1)S(1)} collective-permute-done((f16[1024,512]{1,0:T(8,128)(2,1)S(1)}, f16[1024,512]{1,0:T(8,128)(2,1)S(1)}, u32[]{:S(2)}, u32[]{:S(2)}) %collective-permute-start.5) | collective-permute-done | bytes 1048608 | tf_op jit(solution)/shard_map/ppermute | solution.py:19
  196.2 3.1 collective-permute-start.10
  204.0 1.5 collective-permute-start.18
  205.6 2.7 collective-permute-start.19
  208.6 2.7 collective-permute-start.20
  211.3 3.1 collective-permute-done.9
  214.9 3.4 collective-permute-done.19
  218.9 24.7 %all_to_all.5 = f16[8,128,256]{2,1,0:T(8,128)(2,1)S(1)} all-to-all(f16[8,128,256]{2,1,0:T(8,128)(2,1)S(1)} %bitcast.66), channel_id=1, replica_groups=mesh['zh'=4,'y'=4,'x'=4,'zl'=2,'c'=2] {'zh','zl'}, dimensions={0} | all-to-all | bytes 1048576 | tf_op jit(solution)/shard_map/all_to_all | solution.py:149
  245.1 3.2 collective-permute-start.29
  248.3 4.5 %collective-permute-done.28 = bf16[128,256]{1,0:T(8,128)(2,1)S(1)} collective-permute-done((bf16[128,256]{1,0:T(8,128)(2,1)S(1)}, bf16[128,256]{1,0:T(8,128)(2,1)S(1)}, u32[]{:S(2)}, u32[]{:S(2)}) %collective-permute-start.28) | collective-permute-done | bytes 65568 | tf_op jit(solution)/shard_map/ppermute | solution.py:19
  252.8 2.4 collective-permute-start.30
  255.2 3.0 collective-permute-start.31
  258.2 2.8 collective-permute-start.21
  261.0 1.6 collective-permute-done.31
  262.6 3.4 collective-permute-done.32
  268.2 2.5 collective-permute-start.23
  270.7 2.5 collective-permute-start.24
  273.2 10.8 %collective-permute-done.22 = bf16[256,256]{1,0:T(8,128)(2,1)S(1)} collective-permute-done((bf16[256,256]{1,0:T(8,128)(2,1)S(1)}, bf16[256,256]{1,0:T(8,128)(2,1)S(1)}, u32[]{:S(2)}, u32[]{:S(2)}) %collective-permute-start.22) | collective-permute-done | bytes 131104 | tf_op jit(solution)/shard_map/ppermute | solution.py:19
  284.1 10.9 %collective-permute-start.35 = (bf16[1024,256]{1,0:T(8,128)(2,1)S(1)}, bf16[1024,256]{1,0:T(8,128)(2,1)S(1)}, u32[]{:S(2)}, u32[]{:S(2)}) collective-permute-start(bf16[1024,256]{1,0:T(8,128)(2,1)S(1)} %constant_dynamic-update-slice_fusion.7.refs_4_), channel_id=1, source_target_pairs={{0,12},{4,0},{8,4},{12,8},{1,13},{5,1},{9,5},{13,9},{2,14},{6,2},{... | collective-permute-start | bytes 1572872 | tf_op jit(solution)/shard_map/ppermute | solution.py:19
  295.2 2.5 collective-permute-start.26
  298.5 3.2 collective-permute-done.35.refs_7_
  301.7 9.5 %collective-permute-done.25.refs_1_ = bf16[1024,256]{1,0:T(8,128)(2,1)S(1)} collective-permute-done((bf16[1024,256]{1,0:T(8,128)(2,1)S(1)}, bf16[1024,256]{1,0:T(8,128)(2,1)S(1)}, u32[]{:S(2)}, u32[]{:S(2)}) %collective-permute-start.25) | collective-permute-done | bytes 524320 | tf_op jit(solution)/shard_map/ppermute | solution.py:19
  312.2 128.9 %shard_map.85 = bf16[8192,256]{1,0:T(8,128)(2,1)} custom-call(s32[3]{0:T(128)} %pad_add_fusion.where_ref, bf16[1024,256]{1,0:T(8,128)(2,1)} %copy-done.1, bf16[1024,256]{1,0:T(8,128)(2,1)} %copy-done.6, bf16[1024,256]{1,0:T(8,128)(2,1)} %copy-done.7, bf16[1024,256]{1,0:T(8,128)(2,1)} %collective-permute-done.27.refs_3_, bf16[1024,256]{1,0:T(8,128)(2,1)} %copy-done.2, ...), custom_call_target="tpu_custom_call" | custom-call | tf_op jit(solution)/shard_map/pallas_call | solution.py:107
  (106 shorter events, 26.3 us)
Async XLA Ops:
  134.0 9.2 %collective-permute-start.2 = (bf16[256,1024]{1,0:T(8,128)(2,1)}, bf16[256,1024]{1,0:T(8,128)(2,1)}, u32[]{:S(2)}, u32[]{:S(2)}) collective-permute-start(bf16[256,1024]{1,0:T(8,128)(2,1)} %get-tuple-element.16), channel_id=1, source_target_pairs={{0,1},{1,0},{2,3},{3,2},{4,5},{5,4},{6,7},{7,6},{8,9},{9,8},{10,11... | collective-permute-start | bytes 1572872 | tf_op jit(solution)/shard_map/ppermute | solution.py:23
  135.3 7.4 %collective-permute-start.1 = (bf16[256,512]{0,1:T(8,128)(2,1)S(1)}, bf16[256,512]{0,1:T(8,128)(2,1)S(1)}, u32[]{:S(2)}, u32[]{:S(2)}) collective-permute-start(bf16[256,512]{0,1:T(8,128)(2,1)S(1)} %bitcast.67), channel_id=1, source_target_pairs={{0,1},{1,0},{2,3},{3,2},{4,5},{5,4},{6,7},{7,6},{8,9},{9,8},{10,11... | collective-permute-start | bytes 786440 | tf_op jit(solution)/shard_map/ppermute | solution.py:23
  135.9 9.0 %collective-permute-start.4 = (bf16[256,1024]{1,0:T(8,128)(2,1)}, bf16[256,1024]{1,0:T(8,128)(2,1)S(1)}, u32[]{:S(2)}, u32[]{:S(2)}) collective-permute-start(bf16[256,1024]{1,0:T(8,128)(2,1)} %get-tuple-element.15), channel_id=1, source_target_pairs={{0,1},{1,0},{2,3},{3,2},{4,5},{5,4},{6,7},{7,6},{8,9},{9,8},{10,11... | collective-permute-start | bytes 1572872 | tf_op jit(solution)/shard_map/ppermute | solution.py:23
  136.0 9.9 %collective-permute-start.6 = (bf16[256,1024]{1,0:T(8,128)(2,1)}, bf16[256,1024]{1,0:T(8,128)(2,1)S(1)}, u32[]{:S(2)}, u32[]{:S(2)}) collective-permute-start(bf16[256,1024]{1,0:T(8,128)(2,1)} %get-tuple-element.14), channel_id=1, source_target_pairs={{0,1},{1,0},{2,3},{3,2},{4,5},{5,4},{6,7},{7,6},{8,9},{9,8},{10,11... | collective-permute-start | bytes 1572872 | tf_op jit(solution)/shard_map/ppermute | solution.py:23
  136.4 16.1 %collective-permute-start = (bf16[256,1024]{1,0:T(8,128)(2,1)S(1)}, bf16[256,1024]{1,0:T(8,128)(2,1)S(1)}, u32[]{:S(2)}, u32[]{:S(2)}) collective-permute-start(bf16[256,1024]{1,0:T(8,128)(2,1)S(1)} %get-tuple-element.9), channel_id=1, source_target_pairs={{0,1},{1,0},{2,3},{3,2},{4,5},{5,4},{6,7},{7,6},{8,9},{9,8},{10,11... | collective-permute-start | bytes 1572872 | tf_op jit(solution)/shard_map/ppermute | solution.py:23
  145.9 27.6 %collective-permute-start.3 = (f16[1024,512]{1,0:T(8,128)(2,1)S(1)}, f16[1024,512]{1,0:T(8,128)(2,1)S(1)}, u32[]{:S(2)}, u32[]{:S(2)}) collective-permute-start(f16[1024,512]{1,0:T(8,128)(2,1)S(1)} %multiply_convert_fusion.5), channel_id=1, source_target_pairs={{0,8},{4,12},{8,0},{12,4},{1,9},{5,13},{9,1},{13,5},{2,10},{6,14},... | collective-permute-start | bytes 3145736 | tf_op jit(solution)/shard_map/ppermute | solution.py:19
  148.6 7.2 %collective-permute-start.11 = (bf16[256,1024]{1,0:T(8,128)(2,1)S(1)}, bf16[256,1024]{1,0:T(8,128)(2,1)S(1)}, u32[]{:S(2)}, u32[]{:S(2)}) collective-permute-start(bf16[256,1024]{1,0:T(8,128)(2,1)S(1)} %get-tuple-element.13), channel_id=1, source_target_pairs={{0,1},{1,0},{2,3},{3,2},{4,5},{5,4},{6,7},{7,6},{8,9},{9,8},{10,11... | collective-permute-start | bytes 1572872 | tf_op jit(solution)/shard_map/ppermute | solution.py:23
  149.2 46.0 %collective-permute-start.5 = (f16[1024,512]{1,0:T(8,128)(2,1)S(1)}, f16[1024,512]{1,0:T(8,128)(2,1)S(1)}, u32[]{:S(2)}, u32[]{:S(2)}) collective-permute-start(f16[1024,512]{1,0:T(8,128)(2,1)S(1)} %multiply_convert_fusion.4), channel_id=1, source_target_pairs={{0,4},{4,8},{8,12},{12,0},{1,5},{5,9},{9,13},{13,1},{2,6},{6,10},{... | collective-permute-start | bytes 3145736 | tf_op jit(solution)/shard_map/ppermute | solution.py:19
  151.1 44.1 %collective-permute-start.7 = (f16[1024,512]{1,0:T(8,128)(2,1)S(1)}, f16[1024,512]{1,0:T(8,128)(2,1)S(1)}, u32[]{:S(2)}, u32[]{:S(2)}) collective-permute-start(f16[1024,512]{1,0:T(8,128)(2,1)S(1)} %multiply_convert_fusion.3), channel_id=1, source_target_pairs={{0,12},{4,0},{8,4},{12,8},{1,13},{5,1},{9,5},{13,9},{2,14},{6,2},{... | collective-permute-start | bytes 3145736 | tf_op jit(solution)/shard_map/ppermute | solution.py:19
  152.5 47.4 %collective-permute-start.13 = (f16[1024,512]{1,0:T(8,128)(2,1)S(1)}, f16[1024,512]{1,0:T(8,128)(2,1)S(1)}, u32[]{:S(2)}, u32[]{:S(2)}) collective-permute-start(f16[1024,512]{1,0:T(8,128)(2,1)S(1)} %multiply_convert_fusion.2), channel_id=1, source_target_pairs={{0,32},{16,48},{32,0},{48,16},{1,33},{17,49},{33,1},{49,17},{2,34}... | collective-permute-start | bytes 3145736 | tf_op jit(solution)/shard_map/ppermute | solution.py:19
  155.8 46.0 %collective-permute-start.15 = (f16[1024,512]{1,0:T(8,128)(2,1)S(1)}, f16[1024,512]{1,0:T(8,128)(2,1)S(1)}, u32[]{:S(2)}, u32[]{:S(2)}) collective-permute-start(f16[1024,512]{1,0:T(8,128)(2,1)S(1)} %multiply_convert_fusion.1), channel_id=1, source_target_pairs={{0,16},{16,32},{32,48},{48,0},{1,17},{17,33},{33,49},{49,1},{2,18}... | collective-permute-start | bytes 3145736 | tf_op jit(solution)/shard_map/ppermute | solution.py:19
  173.5 29.5 %collective-permute-start.17 = (f16[1024,512]{1,0:T(8,128)(2,1)S(1)}, f16[1024,512]{1,0:T(8,128)(2,1)S(1)}, u32[]{:S(2)}, u32[]{:S(2)}) collective-permute-start(f16[1024,512]{1,0:T(8,128)(2,1)S(1)} %multiply_convert_fusion), channel_id=1, source_target_pairs={{0,48},{16,0},{32,16},{48,32},{1,49},{17,1},{33,17},{49,33},{2,50}... | collective-permute-start | bytes 3145736 | tf_op jit(solution)/shard_map/ppermute | solution.py:19
  196.2 12.4 %collective-permute-start.10 = (f16[256,512]{1,0:T(8,128)(2,1)S(1)}, f16[256,512]{1,0:T(8,128)(2,1)S(1)}, u32[]{:S(2)}, u32[]{:S(2)}) collective-permute-start(f16[256,512]{1,0:T(8,128)(2,1)S(1)} %get-tuple-element.18), channel_id=1, source_target_pairs={{0,48},{16,0},{32,16},{48,32},{1,49},{17,1},{33,17},{49,33},{2,50}... | collective-permute-start | bytes 786440 | tf_op jit(solution)/shard_map/ppermute | solution.py:19
  199.3 12.0 %collective-permute-start.8 = (f16[256,512]{1,0:T(8,128)(2,1)S(1)}, f16[256,512]{1,0:T(8,128)(2,1)S(1)}, u32[]{:S(2)}, u32[]{:S(2)}) collective-permute-start(f16[256,512]{1,0:T(8,128)(2,1)S(1)} %get-tuple-element.17), channel_id=1, source_target_pairs={{0,32},{16,48},{32,0},{48,16},{1,33},{17,49},{33,1},{49,17},{2,34}... | collective-permute-start | bytes 786440 | tf_op jit(solution)/shard_map/ppermute | solution.py:19
  199.9 14.4 %collective-permute-start.9 = (f16[256,512]{1,0:T(8,128)(2,1)S(1)}, f16[256,512]{1,0:T(8,128)(2,1)S(1)}, u32[]{:S(2)}, u32[]{:S(2)}) collective-permute-start(f16[256,512]{1,0:T(8,128)(2,1)S(1)} %get-tuple-element.19), channel_id=1, source_target_pairs={{0,16},{16,32},{32,48},{48,0},{1,17},{17,33},{33,49},{49,1},{2,18}... | collective-permute-start | bytes 786440 | tf_op jit(solution)/shard_map/ppermute | solution.py:19
  204.0 10.8 %collective-permute-start.18 = (f16[256,512]{1,0:T(8,128)(2,1)S(1)}, f16[256,512]{1,0:T(8,128)(2,1)S(1)}, u32[]{:S(2)}, u32[]{:S(2)}) collective-permute-start(f16[256,512]{1,0:T(8,128)(2,1)S(1)} %get-tuple-element.20), channel_id=1, source_target_pairs={{0,8},{4,12},{8,0},{12,4},{1,9},{5,13},{9,1},{13,5},{2,10},{6,14},... | collective-permute-start | bytes 786440 | tf_op jit(solution)/shard_map/ppermute | solution.py:19
  205.6 12.7 %collective-permute-start.19 = (f16[256,512]{1,0:T(8,128)(2,1)S(1)}, f16[256,512]{1,0:T(8,128)(2,1)S(1)}, u32[]{:S(2)}, u32[]{:S(2)}) collective-permute-start(f16[256,512]{1,0:T(8,128)(2,1)S(1)} %get-tuple-element.22), channel_id=1, source_target_pairs={{0,4},{4,8},{8,12},{12,0},{1,5},{5,9},{9,13},{13,1},{2,6},{6,10},{... | collective-permute-start | bytes 786440 | tf_op jit(solution)/shard_map/ppermute | solution.py:19
  208.6 9.6 %collective-permute-start.20 = (f16[256,512]{1,0:T(8,128)(2,1)S(1)}, f16[256,512]{1,0:T(8,128)(2,1)S(1)}, u32[]{:S(2)}, u32[]{:S(2)}) collective-permute-start(f16[256,512]{1,0:T(8,128)(2,1)S(1)} %get-tuple-element.21), channel_id=1, source_target_pairs={{0,12},{4,0},{8,4},{12,8},{1,13},{5,1},{9,5},{13,9},{2,14},{6,2},{... | collective-permute-start | bytes 786440 | tf_op jit(solution)/shard_map/ppermute | solution.py:19
  244.5 8.3 %collective-permute-start.28 = (bf16[128,256]{1,0:T(8,128)(2,1)S(1)}, bf16[128,256]{1,0:T(8,128)(2,1)S(1)}, u32[]{:S(2)}, u32[]{:S(2)}) collective-permute-start(bf16[128,256]{1,0:T(8,128)(2,1)S(1)} %get-tuple-element.5), channel_id=1, source_target_pairs={{0,128},{64,192},{128,0},{192,64},{1,129},{65,193},{129,1},{193,65... | collective-permute-start | bytes 196616 | tf_op jit(solution)/shard_map/ppermute | solution.py:19
  245.1 7.7 %collective-permute-start.29 = (bf16[128,256]{1,0:T(8,128)(2,1)S(1)}, bf16[128,256]{1,0:T(8,128)(2,1)S(1)}, u32[]{:S(2)}, u32[]{:S(2)}) collective-permute-start(bf16[128,256]{1,0:T(8,128)(2,1)S(1)} %get-tuple-element.5), channel_id=1, source_target_pairs={{0,192},{64,0},{128,64},{192,128},{1,193},{65,1},{129,65},{193,129... | collective-permute-start | bytes 196616 | tf_op jit(solution)/shard_map/ppermute | solution.py:19
  252.8 8.2 %collective-permute-start.30 = (bf16[256,256]{1,0:T(8,128)(2,1)S(1)}, bf16[256,256]{1,0:T(8,128)(2,1)S(1)}, u32[]{:S(2)}, u32[]{:S(2)}) collective-permute-start(bf16[256,256]{1,0:T(8,128)(2,1)S(1)} %get-tuple-element.25), channel_id=1, source_target_pairs={{0,16},{16,32},{32,48},{48,0},{1,17},{17,33},{33,49},{49,1},{2,18}... | collective-permute-start | bytes 393224 | tf_op jit(solution)/shard_map/ppermute | solution.py:19
  255.2 7.3 %collective-permute-start.31 = (bf16[256,256]{1,0:T(8,128)(2,1)S(1)}, bf16[256,256]{1,0:T(8,128)(2,1)S(1)}, u32[]{:S(2)}, u32[]{:S(2)}) collective-permute-start(bf16[256,256]{1,0:T(8,128)(2,1)S(1)} %get-tuple-element.25), channel_id=1, source_target_pairs={{0,32},{16,48},{32,0},{48,16},{1,33},{17,49},{33,1},{49,17},{2,34}... | collective-permute-start | bytes 393224 | tf_op jit(solution)/shard_map/ppermute | solution.py:19
  258.2 8.9 %collective-permute-start.21 = (bf16[128,256]{1,0:T(8,128)(2,1)S(1)}, bf16[128,256]{1,0:T(8,128)(2,1)S(1)}, u32[]{:S(2)}, u32[]{:S(2)}) collective-permute-start(bf16[128,256]{1,0:T(8,128)(2,1)S(1)} %get-tuple-element.5), channel_id=1, source_target_pairs={{0,64},{64,128},{128,192},{192,0},{1,65},{65,129},{129,193},{193,1... | collective-permute-start | bytes 196616 | tf_op jit(solution)/shard_map/ppermute | solution.py:19
  266.0 31.7 %collective-permute-start.33 = (bf16[1024,256]{1,0:T(8,128)(2,1)S(1)}, bf16[1024,256]{1,0:T(8,128)(2,1)S(1)}, u32[]{:S(2)}, u32[]{:S(2)}) collective-permute-start(bf16[1024,256]{1,0:T(8,128)(2,1)S(1)} %constant_dynamic-update-slice_fusion.7.refs_4_), channel_id=1, source_target_pairs={{0,4},{4,8},{8,12},{12,0},{1,5},{5,9},{9,13},{13,1},{2,6},{6,10},{... | collective-permute-start | bytes 1572872 | tf_op jit(solution)/shard_map/ppermute | solution.py:19
  267.2 16.9 %collective-permute-start.22 = (bf16[256,256]{1,0:T(8,128)(2,1)S(1)}, bf16[256,256]{1,0:T(8,128)(2,1)S(1)}, u32[]{:S(2)}, u32[]{:S(2)}) collective-permute-start(bf16[256,256]{1,0:T(8,128)(2,1)S(1)} %pad_maximum_fusion), channel_id=1, source_target_pairs={{0,4},{4,8},{8,12},{12,0},{1,5},{5,9},{9,13},{13,1},{2,6},{6,10},{... | collective-permute-start | bytes 393224 | tf_op jit(solution)/shard_map/ppermute | solution.py:19
  268.2 26.8 %collective-permute-start.23 = (bf16[256,256]{1,0:T(8,128)(2,1)S(1)}, bf16[256,256]{1,0:T(8,128)(2,1)S(1)}, u32[]{:S(2)}, u32[]{:S(2)}) collective-permute-start(bf16[256,256]{1,0:T(8,128)(2,1)S(1)} %pad_maximum_fusion), channel_id=1, source_target_pairs={{0,8},{4,12},{8,0},{12,4},{1,9},{5,13},{9,1},{13,5},{2,10},{6,14},... | collective-permute-start | bytes 393224 | tf_op jit(solution)/shard_map/ppermute | solution.py:19
  270.7 24.4 %collective-permute-start.24 = (bf16[256,256]{1,0:T(8,128)(2,1)S(1)}, bf16[256,256]{1,0:T(8,128)(2,1)S(1)}, u32[]{:S(2)}, u32[]{:S(2)}) collective-permute-start(bf16[256,256]{1,0:T(8,128)(2,1)S(1)} %pad_maximum_fusion), channel_id=1, source_target_pairs={{0,12},{4,0},{8,4},{12,8},{1,13},{5,1},{9,5},{13,9},{2,14},{6,2},{... | collective-permute-start | bytes 393224 | tf_op jit(solution)/shard_map/ppermute | solution.py:19
  273.2 25.3 %collective-permute-start.34 = (bf16[1024,256]{1,0:T(8,128)(2,1)S(1)}, bf16[1024,256]{1,0:T(8,128)(2,1)S(1)}, u32[]{:S(2)}, u32[]{:S(2)}) collective-permute-start(bf16[1024,256]{1,0:T(8,128)(2,1)S(1)} %constant_dynamic-update-slice_fusion.7.refs_4_), channel_id=1, source_target_pairs={{0,8},{4,12},{8,0},{12,4},{1,9},{5,13},{9,1},{13,5},{2,10},{6,14},... | collective-permute-start | bytes 1572872 | tf_op jit(solution)/shard_map/ppermute | solution.py:19
  284.1 17.6 %collective-permute-start.35 = (bf16[1024,256]{1,0:T(8,128)(2,1)S(1)}, bf16[1024,256]{1,0:T(8,128)(2,1)S(1)}, u32[]{:S(2)}, u32[]{:S(2)}) collective-permute-start(bf16[1024,256]{1,0:T(8,128)(2,1)S(1)} %constant_dynamic-update-slice_fusion.7.refs_4_), channel_id=1, source_target_pairs={{0,12},{4,0},{8,4},{12,8},{1,13},{5,1},{9,5},{13,9},{2,14},{6,2},{... | collective-permute-start | bytes 1572872 | tf_op jit(solution)/shard_map/ppermute | solution.py:19
  295.1 16.1 %collective-permute-start.25 = (bf16[1024,256]{1,0:T(8,128)(2,1)S(1)}, bf16[1024,256]{1,0:T(8,128)(2,1)S(1)}, u32[]{:S(2)}, u32[]{:S(2)}) collective-permute-start(bf16[1024,256]{1,0:T(8,128)(2,1)S(1)} %constant_dynamic-update-slice_fusion.refs_0_), channel_id=1, source_target_pairs={{0,16},{16,32},{32,48},{48,0},{1,17},{17,33},{33,49},{49,1},{2,18}... | collective-permute-start | bytes 1572872 | tf_op jit(solution)/shard_map/ppermute | solution.py:19
  295.2 16.0 %collective-permute-start.26 = (bf16[1024,256]{1,0:T(8,128)(2,1)S(1)}, bf16[1024,256]{1,0:T(8,128)(2,1)S(1)}, u32[]{:S(2)}, u32[]{:S(2)}) collective-permute-start(bf16[1024,256]{1,0:T(8,128)(2,1)S(1)} %constant_dynamic-update-slice_fusion.refs_0_), channel_id=1, source_target_pairs={{0,32},{16,48},{32,0},{48,16},{1,33},{17,49},{33,1},{49,17},{2,34}... | collective-permute-start | bytes 1572872 | tf_op jit(solution)/shard_map/ppermute | solution.py:19
  297.7 14.5 %collective-permute-start.27 = (bf16[1024,256]{1,0:T(8,128)(2,1)S(1)}, bf16[1024,256]{1,0:T(8,128)(2,1)}, u32[]{:S(2)}, u32[]{:S(2)}) collective-permute-start(bf16[1024,256]{1,0:T(8,128)(2,1)S(1)} %constant_dynamic-update-slice_fusion.refs_0_), channel_id=1, source_target_pairs={{0,48},{16,0},{32,16},{48,32},{1,49},{17,1},{33,17},{49,33},{2,50}... | collective-permute-start | bytes 1572872 | tf_op jit(solution)/shard_map/ppermute | solution.py:19
  (15 other events, 205.5 us)

commit v2 on v0

v2 whole, which is shorter than its diff:
```python
import math

import jax
import jax.numpy as jnp
from jax import lax
from jax.experimental import pallas as pl
from jax.experimental.pallas import tpu as pltpu
from jax.sharding import Mesh
from jax.sharding import PartitionSpec as P

first_bias = 1.0 - math.exp(100.0 * math.log(0.9))
second_bias = 1.0 - math.exp(100.0 * math.log(0.999))

F32, F16, BF16 = jnp.float32, jnp.float16, jnp.bfloat16
BLOCK = 128
VMEM = pltpu.CompilerParams(vmem_limit_bytes=32 * 2**20)

FIRST, SECOND = ("x", "y"), ("y", "x")
NEAR, NEXT = (1, 3), (3, 1)


def swap(array, axis, by):
    pairs = [(2 * i + c, 2 * (i ^ by[c]) + c) for i in range(4) for c in range(2)]
    return lax.ppermute(array, (axis, "c"), pairs)


def other_core(array):
    return lax.ppermute(array, "c", [(0, 1), (1, 0)])


def order(core):
    return 0, 3 - 2 * core, 1 + 2 * core, 2


def owner(part, first, second, x, y):
    x_by, y_by = (first, second) if part == 0 else (second, first)
    return lax.bitwise_xor(y, y_by) * 4 + lax.bitwise_xor(x, x_by)


def other_rows(acts, where):
    half = acts.shape[1] // 4

    def kernel(where_ref, acts_ref, out_ref):
        for part in range(2):
            start = pl.multiple_of((2 * part + 1 - where_ref[3]) * half, half)
            out_ref[:, part * half : (part + 1) * half] = acts_ref[:, pl.ds(start, half)]

    vmem = pl.BlockSpec(memory_space=pltpu.VMEM)
    return pl.pallas_call(
        kernel,
        out_shape=jax.ShapeDtypeStruct((acts.shape[0], 2 * half), acts.dtype),
        in_specs=[pl.BlockSpec(memory_space=pltpu.SMEM), vmem],
        out_specs=vmem,
        compiler_params=VMEM,
        cost_estimate=pl.CostEstimate(
            flops=0, bytes_accessed=2 * acts.size, transcendentals=0
        ),
    )(where, acts)


def arrange(acts, peer, where, sent):
    tokens = acts.shape[0]

    def kernel(where_ref, acts_ref, peer_ref, *out_refs):
        x, y, core = where_ref[0], where_ref[1], where_ref[3]
        distances = order(core)
        for part in range(2):
            for i in range(2):
                for j in range(4):
                    out_ref, place = out_refs[2 * part + i], slice(j * BLOCK, (j + 1) * BLOCK)
                    block = owner(part, distances[2 * sent + i], distances[j], x, y)
                    own = ((2 * part + core) * 16 + block) * BLOCK
                    out_ref[:tokens, place] = acts_ref[:, pl.ds(pl.multiple_of(own, BLOCK), BLOCK)]
                    other = (part * 16 + block) * BLOCK
                    out_ref[tokens:, place] = peer_ref[:, pl.ds(pl.multiple_of(other, BLOCK), BLOCK)]

    out = jax.ShapeDtypeStruct((2 * tokens, 4 * BLOCK), acts.dtype)
    vmem = pl.BlockSpec(memory_space=pltpu.VMEM)
    outs = pl.pallas_call(
        kernel,
        out_shape=[out] * 4,
        in_specs=[pl.BlockSpec(memory_space=pltpu.SMEM), vmem, vmem],
        out_specs=[vmem] * 4,
        compiler_params=VMEM,
        cost_estimate=pl.CostEstimate(
            flops=0, bytes_accessed=16 * out.size, transcendentals=0
        ),
    )(where, acts, peer)
    return [outs[:2], outs[2:]]


def place(pieces, where, half, into=None):
    def kernel(where_ref, *refs):
        ins, out_ref, sem = refs[:2], refs[-2], refs[-1]
        x, y, zh, core = (where_ref[i] for i in range(4))
        distances = (0, 1 + 2 * core, 3 - 2 * core, 2)
        copies = []
        for part in range(2):
            for i in range(2):
                for j in range(4):
                    for k in range(2):
                        block = lax.bitwise_xor(zh, 2 * part + k) * 16
                        block += owner(part, distances[2 * half + i], distances[j], x, y)
                        copies.append(
                            pltpu.make_async_copy(
                                ins[part].at[pl.ds((i * 8 + j * 2 + k) * BLOCK, BLOCK), :],
                                out_ref.at[pl.ds(pl.multiple_of(block * BLOCK, BLOCK), BLOCK), :],
                                sem,
                            )
                        )
        for copy in copies:
            copy.start()
        for copy in copies:
            copy.wait()

    anywhere = pl.BlockSpec(memory_space=pl.ANY)
    return pl.pallas_call(
        kernel,
        out_shape=jax.ShapeDtypeStruct((8192, 256), BF16),
        in_specs=[pl.BlockSpec(memory_space=pltpu.SMEM)]
        + [pl.BlockSpec(memory_space=pltpu.VMEM)] * 2
        + [anywhere] * (into is not None),
        out_specs=anywhere,
        scratch_shapes=[pltpu.SemaphoreType.DMA],
        input_output_aliases={} if into is None else {3: 0},
        compiler_params=VMEM,
        cost_estimate=pl.CostEstimate(
            flops=0, bytes_accessed=8 * 2**20, transcendentals=0
        ),
    )(where, *pieces, *(() if into is None else (into,)))


def dot(a, b):
    return lax.dot_general(a, b, (((0,), (0,)), ((), ())), preferred_element_type=F32)


def received(array, swapped, scale):
    return swapped((array * scale).astype(F16)).astype(F32) * (1.0 / scale)


def per_device(acts, grad_out, master, moment1, moment2):
    x, y, zh, zl, core = (lax.axis_index(name) for name in ("x", "y", "zh", "zl", "c"))
    where = jnp.stack([x, y, zh, core]).astype(jnp.int32)
    parts = range(2)

    chip_grad = jnp.concatenate([grad_out, other_core(grad_out)], 0)
    peer = other_core(other_rows(acts, where))

    far_grad = [swap(chip_grad, FIRST[p], NEAR) for p in parts]
    sent = arrange(acts, peer, where, 1)
    far_acts = [[None, None], [None, None]]
    for i in (1, 0):
        for p in parts:
            far_acts[p][i] = swap(sent[p][i], FIRST[p], NEAR)
    kept = arrange(acts, peer, where, 0)

    def partial(p, i):
        return dot(kept[p][i], chip_grad) + dot(far_acts[p][i], far_grad[p])

    passed = [partial(p, 1) for p in parts]
    late = [received(passed[p][256:], lambda v: swap(v, FIRST[p], NEXT), 64.0) for p in parts]
    soon = [received(passed[p][:256], lambda v: swap(v, FIRST[p], NEXT), 64.0) for p in parts]
    own = [partial(p, 0) for p in parts]
    level = [
        own[p][:256] + soon[p] + received(own[p][256:] + late[p], lambda v: swap(v, SECOND[p], NEAR), 32.0)
        for p in parts
    ]
    level = [
        level[p][:128] + received(level[p][128:], lambda v: swap(v, SECOND[p], NEXT), 16.0)
        for p in parts
    ]

    both = jnp.concatenate(level, 0)
    low, high = both[:, :512], both[:, 512:]
    pairs = [
        (2 * z + c, 2 * (z ^ 1 if c == 0 else ((z + 1) ^ 1) - 1 & 7) + c)
        for z in range(8)
        for c in range(2)
    ]
    level = jnp.where(zl == 0, low, high) + received(
        jnp.where(zl == 0, high, low), lambda v: lax.ppermute(v, ("zh", "zl", "c"), pairs), 8.0
    )
    grad = 0.0
    for j in (1, 0):
        rows = jnp.where(lax.bitwise_xor(zh // 2, j) == 0, level[:128], level[128:])
        for k in (1, 0):
            block = jnp.where(lax.bitwise_xor(zh % 2, k) == 0, rows[:, :256], rows[:, 256:])
            pairs = [
                (2 * z + c, 2 * (c + 2 * ((z // 2) ^ j)) + ((z % 2) ^ k))
                for z in range(4)
                for c in range(2)
            ]
            grad = grad + lax.ppermute(block, ("zh", "c"), pairs)

    new_moment1 = 0.9 * moment1 + 0.1 * grad
    new_moment2 = 0.999 * moment2 + 0.001 * grad * grad
    update = new_moment1 / first_bias / (jnp.sqrt(new_moment2 / second_bias) + 1e-08)
    new_master = master - 0.01 * (update + 0.1 * master)

    own = new_master.astype(BF16)
    z = [own] + [
        lax.ppermute(own, "zh", [(i, i ^ k) for i in range(4)]) for k in (1, 2, 3)
    ]
    pieces = [jnp.concatenate(z[:2], 0), jnp.concatenate(z[2:], 0)]
    for axes, by in ((SECOND, NEAR), (SECOND, NEXT), (FIRST, NEAR)):
        pieces = [jnp.concatenate([pieces[p], swap(pieces[p], axes[p], by)], 0) for p in parts]
    last = [swap(pieces[p], FIRST[p], NEXT) for p in parts]
    new_weights = place(last, where, 1, place(pieces, where, 0))
    return (new_master, new_moment1, new_moment2, new_weights)


def solution(mesh):
    fine = Mesh(mesh.devices.reshape(4, 4, 4, 2, 2), ("zh", "y", "x", "zl", "c"))
    dp, tensor = ("zh", "y", "x"), ("zl", "c")
    tokens, state = P(dp + tensor, None), P(dp, tensor)
    return jax.shard_map(
        per_device,
        mesh=fine,
        in_specs=(tokens, tokens, state, state, state),
        out_specs=(state, state, state, P(None, tensor)),
        check_vma=False,
    )
```

time: 686 us -> 164 us (0.24)
  the two profiles are of different devices: /device:TPU:2 before, /device:TPU:216 now
where the time goes in v2:
time: 164 us
  waiting for transfers between devices  103 us (63%)
  starting transfers between devices  40.8 us (25%)
  Pallas kernels  6.59 us (4%)
  matrix products  5.83 us (4%)
  other arithmetic  3.78 us (2%)
  local copies, waits for them, and re-layouts  2.68 us (2%)
    ppermute x22, waiting for transfers between devices, swap(): return lax.ppermute(array, (axis, 'c'), pairs)  81.7 us
    ppermute x22, starting transfers between devices, swap(): return lax.ppermute(array, (axis, 'c'), pairs)  24.6 us
    ppermute x4, starting transfers between devices, per_device(): grad = grad + lax.ppermute(block, ('zh', 'c'), pairs)  8.2 us
    ppermute x3, starting transfers between devices, per_device(): lax.ppermute(own, 'zh', [(i, i ^ k) for i in range(4)])  6.51 us
    ppermute x1, waiting for transfers between devices, per_device(): lax.ppermute(v, ('zh', 'zl', 'c'), pairs)  6.28 us
    dot_general x8, matrix products, dot(): lax.dot_general(a, b, (((0,), (0,)), ((), ())), preferred_element_type=F32)  5.83 us
    ppermute x4, waiting for transfers between devices, per_device(): grad = grad + lax.ppermute(block, ('zh', 'c'), pairs)  5.67 us
    ppermute x3, waiting for transfers between devices, per_device(): lax.ppermute(own, 'zh', [(i, i ^ k) for i in range(4)])  5.51 us
  transfers between devices with their start and end apart: 32, of which 20 were waited for; matrix products, arithmetic and copies ran while one was open for 5% of the time, Pallas kernels for 2%

profile of v2, /device:TPU:216, one launch (start us, length us, event | category | flops | bytes accessed | tf_op | source)
XLA Modules:
  0.0 164.3 jit_solution(6989721595479952987)
XLA Ops:
  0.7 2.2 %copy-done = bf16[256,8192]{1,0:T(8,128)(2,1)S(1)} copy-done((bf16[256,8192]{1,0:T(8,128)(2,1)S(1)}, bf16[256,8192]{1,0:T(8,128)(2,1)}, u32[]{:S(2)}) %copy-start) | copy-done | bytes 4194328
  4.2 4.4 %collective-permute-done.1 = bf16[256,1024]{1,0:T(8,128)(2,1)S(1)} collective-permute-done((bf16[256,1024]{1,0:T(8,128)(2,1)S(1)}, bf16[256,1024]{1,0:T(8,128)(2,1)S(1)}, u32[]{:S(2)}, u32[]{:S(2)}) %collective-permute-start.1) | collective-permute-done | bytes 524320 | tf_op jit(solution)/shard_map/ppermute | solution.py:28
  16.6 6.9 %collective-permute-done.10 = bf16[512,1024]{1,0:T(8,128)(2,1)S(1)} collective-permute-done((bf16[512,1024]{1,0:T(8,128)(2,1)S(1)}, bf16[512,1024]{1,0:T(8,128)(2,1)S(1)}, u32[]{:S(2)}, u32[]{:S(2)}) %collective-permute-start.10) | collective-permute-done | bytes 1048608 | tf_op jit(solution)/shard_map/ppermute | solution.py:24
  24.3 4.9 %collective-permute-done.11 = bf16[512,512]{1,0:T(8,128)(2,1)S(1)} collective-permute-done((bf16[512,512]{1,0:T(8,128)(2,1)S(1)}, bf16[512,512]{1,0:T(8,128)(2,1)S(1)}, u32[]{:S(2)}, u32[]{:S(2)}) %collective-permute-start.11) | collective-permute-done | bytes 524320 | tf_op jit(solution)/shard_map/ppermute | solution.py:24
  31.2 3.0 %collective-permute-start.13 = (f16[256,1024]{1,0:T(8,128)(2,1)S(1)}, f16[256,1024]{1,0:T(8,128)(2,1)S(1)}, u32[]{:S(2)}, u32[]{:S(2)}) collective-permute-start(f16[256,1024]{1,0:T(8,128)(2,1)S(1)} %get-tuple-element.28), channel_id=1, source_target_pairs={{0,48},{1,17},{16,32},{17,1},{32,16},{33,49},{48,0},{49,33},{2,50}... | collective-permute-start | bytes 1572872 | tf_op jit(solution)/shard_map/ppermute | solution.py:24
  34.2 3.8 %collective-permute-done.4 = bf16[512,512]{1,0:T(8,128)(2,1)S(1)} collective-permute-done((bf16[512,512]{1,0:T(8,128)(2,1)S(1)}, bf16[512,512]{1,0:T(8,128)(2,1)S(1)}, u32[]{:S(2)}, u32[]{:S(2)}) %collective-permute-start.4) | collective-permute-done | bytes 524320 | tf_op jit(solution)/shard_map/ppermute | solution.py:24
  39.7 2.8 %collective-permute-start.5 = (f16[256,1024]{1,0:T(8,128)(2,1)S(1)}, f16[256,1024]{1,0:T(8,128)(2,1)S(1)}, u32[]{:S(2)}, u32[]{:S(2)}) collective-permute-start(f16[256,1024]{1,0:T(8,128)(2,1)S(1)} %get-tuple-element.25), channel_id=1, source_target_pairs={{0,12},{1,5},{4,8},{5,1},{8,4},{9,13},{12,0},{13,9},{2,14},{3,7},{... | collective-permute-start | bytes 1572872 | tf_op jit(solution)/shard_map/ppermute | solution.py:24
  45.3 1.7 %collective-permute-done.13 = f16[256,1024]{1,0:T(8,128)(2,1)S(1)} collective-permute-done((f16[256,1024]{1,0:T(8,128)(2,1)S(1)}, f16[256,1024]{1,0:T(8,128)(2,1)S(1)}, u32[]{:S(2)}, u32[]{:S(2)}) %collective-permute-start.13) | collective-permute-done | bytes 524320 | tf_op jit(solution)/shard_map/ppermute | solution.py:24
  47.2 1.6 collective-permute-start.14
  49.5 11.9 %collective-permute-done.6 = f16[256,1024]{1,0:T(8,128)(2,1)S(1)} collective-permute-done((f16[256,1024]{1,0:T(8,128)(2,1)S(1)}, f16[256,1024]{1,0:T(8,128)(2,1)S(1)}, u32[]{:S(2)}, u32[]{:S(2)}) %collective-permute-start.6) | collective-permute-done | bytes 524320 | tf_op jit(solution)/shard_map/ppermute | solution.py:24
  62.8 2.8 %collective-permute-start.15 = (f16[128,1024]{1,0:T(8,128)(2,1)S(1)}, f16[128,1024]{1,0:T(8,128)(2,1)S(1)}, u32[]{:S(2)}, u32[]{:S(2)}) collective-permute-start(f16[128,1024]{1,0:T(8,128)(2,1)S(1)} %fusion.11), channel_id=1, source_target_pairs={{0,12},{1,5},{4,8},{5,1},{8,4},{9,13},{12,0},{13,9},{2,14},{3,7},{... | collective-permute-start | bytes 786440 | tf_op jit(solution)/shard_map/ppermute | solution.py:24
  65.6 5.3 %collective-permute-done.7 = f16[256,1024]{1,0:T(8,128)(2,1)S(1)} collective-permute-done((f16[256,1024]{1,0:T(8,128)(2,1)S(1)}, f16[256,1024]{1,0:T(8,128)(2,1)S(1)}, u32[]{:S(2)}, u32[]{:S(2)}) %collective-permute-start.7) | collective-permute-done | bytes 524320 | tf_op jit(solution)/shard_map/ppermute | solution.py:24
  72.2 7.5 %collective-permute-done.8 = f16[128,1024]{1,0:T(8,128)(2,1)S(1)} collective-permute-done((f16[128,1024]{1,0:T(8,128)(2,1)}, f16[128,1024]{1,0:T(8,128)(2,1)S(1)}, u32[]{:S(2)}, u32[]{:S(2)}) %collective-permute-start.8) | collective-permute-done | bytes 262176 | tf_op jit(solution)/shard_map/ppermute | solution.py:24
  81.0 6.3 %collective-permute-done.16 = f16[256,512]{1,0:T(8,128)(2,1)S(1)} collective-permute-done((f16[256,512]{1,0:T(8,128)(2,1)S(1)}, f16[256,512]{1,0:T(8,128)(2,1)S(1)}, u32[]{:S(2)}, u32[]{:S(2)}) %collective-permute-start.16) | collective-permute-done | bytes 262176 | tf_op jit(solution)/shard_map/ppermute | solution.py:181
  87.7 4.1 %collective-permute-start.17 = (f32[128,256]{1,0:T(8,128)S(1)}, f32[128,256]{1,0:T(8,128)S(1)}, u32[]{:S(2)}, u32[]{:S(2)}) collective-permute-start(f32[128,256]{1,0:T(8,128)S(1)} %get-tuple-element.32), channel_id=1, source_target_pairs={{0,129},{1,193},{64,128},{65,192},{128,1},{129,65},{192,0},{193,64... | collective-permute-start | bytes 393224 | tf_op jit(solution)/shard_map/ppermute | solution.py:193
  91.8 2.1 %collective-permute-start.19 = (f32[128,256]{1,0:T(8,128)S(1)}, f32[128,256]{1,0:T(8,128)S(1)}, u32[]{:S(2)}, u32[]{:S(2)}) collective-permute-start(f32[128,256]{1,0:T(8,128)S(1)} %get-tuple-element.33), channel_id=1, source_target_pairs={{0,1},{1,65},{64,0},{65,64},{128,129},{129,193},{192,128},{193,192... | collective-permute-start | bytes 393224 | tf_op jit(solution)/shard_map/ppermute | solution.py:193
  93.9 1.9 %collective-permute-start.20 = (f32[128,256]{1,0:T(8,128)S(1)}, f32[128,256]{1,0:T(8,128)S(1)}, u32[]{:S(2)}, u32[]{:S(2)}) collective-permute-start(f32[128,256]{1,0:T(8,128)S(1)} %get-tuple-element.34), channel_id=1, source_target_pairs={{0,0},{1,64},{64,1},{65,65},{128,128},{129,192},{192,129},{193,193... | collective-permute-start | bytes 393224 | tf_op jit(solution)/shard_map/ppermute | solution.py:193
  95.8 5.1 %collective-permute-done.18 = f32[128,256]{1,0:T(8,128)S(1)} collective-permute-done((f32[128,256]{1,0:T(8,128)S(1)}, f32[128,256]{1,0:T(8,128)S(1)}, u32[]{:S(2)}, u32[]{:S(2)}) %collective-permute-start.18) | collective-permute-done | bytes 131104 | tf_op jit(solution)/shard_map/ppermute | solution.py:193
  102.3 3.1 %collective-permute-start.26 = (bf16[128,256]{1,0:T(8,128)(2,1)S(1)}, bf16[128,256]{1,0:T(8,128)(2,1)S(1)}, u32[]{:S(2)}, u32[]{:S(2)}) collective-permute-start(bf16[128,256]{1,0:T(8,128)(2,1)S(1)} %get-tuple-element.21), channel_id=1, source_target_pairs={{0,128},{64,192},{128,0},{192,64},{1,129},{65,193},{129,1},{193,65... | collective-permute-start | bytes 196616 | tf_op jit(solution)/shard_map/ppermute | solution.py:202
  105.3 2.4 %collective-permute-start.27 = (bf16[128,256]{1,0:T(8,128)(2,1)S(1)}, bf16[128,256]{1,0:T(8,128)(2,1)S(1)}, u32[]{:S(2)}, u32[]{:S(2)}) collective-permute-start(bf16[128,256]{1,0:T(8,128)(2,1)S(1)} %get-tuple-element.21), channel_id=1, source_target_pairs={{0,192},{64,128},{128,64},{192,0},{1,193},{65,129},{129,65},{193,1... | collective-permute-start | bytes 196616 | tf_op jit(solution)/shard_map/ppermute | solution.py:202
  108.8 2.2 %collective-permute-done.26 = bf16[128,256]{1,0:T(8,128)(2,1)S(1)} collective-permute-done((bf16[128,256]{1,0:T(8,128)(2,1)S(1)}, bf16[128,256]{1,0:T(8,128)(2,1)S(1)}, u32[]{:S(2)}, u32[]{:S(2)}) %collective-permute-start.26) | collective-permute-done | bytes 65568 | tf_op jit(solution)/shard_map/ppermute | solution.py:202
  111.0 3.3 %collective-permute-done.27 = bf16[128,256]{1,0:T(8,128)(2,1)S(1)} collective-permute-done((bf16[128,256]{1,0:T(8,128)(2,1)S(1)}, bf16[128,256]{1,0:T(8,128)(2,1)S(1)}, u32[]{:S(2)}, u32[]{:S(2)}) %collective-permute-start.27) | collective-permute-done | bytes 65568 | tf_op jit(solution)/shard_map/ppermute | solution.py:202
  115.2 4.1 %collective-permute-done.28 = bf16[256,256]{1,0:T(8,128)(2,1)S(1)} collective-permute-done((bf16[256,256]{1,0:T(8,128)(2,1)S(1)}, bf16[256,256]{1,0:T(8,128)(2,1)S(1)}, u32[]{:S(2)}, u32[]{:S(2)}) %collective-permute-start.28) | collective-permute-done | bytes 131104 | tf_op jit(solution)/shard_map/ppermute | solution.py:24
  119.4 3.1 %collective-permute-start.29 = (bf16[512,256]{1,0:T(8,128)(2,1)S(1)}, bf16[512,256]{1,0:T(8,128)(2,1)S(1)}, u32[]{:S(2)}, u32[]{:S(2)}) collective-permute-start(bf16[512,256]{1,0:T(8,128)(2,1)S(1)} %pad_maximum_fusion.4), channel_id=1, source_target_pairs={{0,12},{1,5},{4,8},{5,1},{8,4},{9,13},{12,0},{13,9},{2,14},{3,7},{... | collective-permute-start | bytes 786440 | tf_op jit(solution)/shard_map/ppermute | solution.py:24
  123.3 3.9 %collective-permute-done.29 = bf16[512,256]{1,0:T(8,128)(2,1)S(1)} collective-permute-done((bf16[512,256]{1,0:T(8,128)(2,1)S(1)}, bf16[512,256]{1,0:T(8,128)(2,1)S(1)}, u32[]{:S(2)}, u32[]{:S(2)}) %collective-permute-start.29) | collective-permute-done | bytes 262176 | tf_op jit(solution)/shard_map/ppermute | solution.py:24
  127.5 5.5 %collective-permute-done.23 = bf16[512,256]{1,0:T(8,128)(2,1)S(1)} collective-permute-done((bf16[512,256]{1,0:T(8,128)(2,1)S(1)}, bf16[512,256]{1,0:T(8,128)(2,1)S(1)}, u32[]{:S(2)}, u32[]{:S(2)}) %collective-permute-start.23) | collective-permute-done | bytes 262176 | tf_op jit(solution)/shard_map/ppermute | solution.py:24
  133.2 3.4 %collective-permute-done.30 = bf16[1024,256]{1,0:T(8,128)(2,1)S(1)} collective-permute-done((bf16[1024,256]{1,0:T(8,128)(2,1)S(1)}, bf16[1024,256]{1,0:T(8,128)(2,1)S(1)}, u32[]{:S(2)}, u32[]{:S(2)}) %collective-permute-start.30) | collective-permute-done | bytes 524320 | tf_op jit(solution)/shard_map/ppermute | solution.py:24
  137.5 8.6 %collective-permute-done.24 = bf16[1024,256]{1,0:T(8,128)(2,1)S(1)} collective-permute-done((bf16[1024,256]{1,0:T(8,128)(2,1)S(1)}, bf16[1024,256]{1,0:T(8,128)(2,1)S(1)}, u32[]{:S(2)}, u32[]{:S(2)}) %collective-permute-start.24) | collective-permute-done | bytes 524320 | tf_op jit(solution)/shard_map/ppermute | solution.py:24
  146.3 1.8 %shard_map.87.refs_2_ = bf16[8192,256]{1,0:T(8,128)(2,1)} custom-call(s32[4]{0:T(128)S(1)} %pad_add_fusion.where_ref, bf16[2048,256]{1,0:T(8,128)(2,1)S(1)} %constant_dynamic-update-slice_fusion.2.refs_0_, bf16[2048,256]{1,0:T(8,128)(2,1)S(1)} %constant_dynamic-update-slice_fusion.7.refs_1_), custom_call_target="tpu_custom_call" | custom-call | bytes 8388608 | tf_op jit(solution)/shard_map/pallas_call | solution.py:117
  148.1 4.6 %collective-permute-done.31.refs_1_ = bf16[2048,256]{1,0:T(8,128)(2,1)S(1)} collective-permute-done((bf16[2048,256]{1,0:T(8,128)(2,1)S(1)}, bf16[2048,256]{1,0:T(8,128)(2,1)S(1)}, u32[]{:S(2)}, u32[]{:S(2)}) %collective-permute-start.31) | collective-permute-done | bytes 1048608 | tf_op jit(solution)/shard_map/ppermute | solution.py:24
  152.7 9.5 %collective-permute-done.25.refs_0_ = bf16[2048,256]{1,0:T(8,128)(2,1)S(1)} collective-permute-done((bf16[2048,256]{1,0:T(8,128)(2,1)S(1)}, bf16[2048,256]{1,0:T(8,128)(2,1)S(1)}, u32[]{:S(2)}, u32[]{:S(2)}) %collective-permute-start.25) | collective-permute-done | bytes 1048608 | tf_op jit(solution)/shard_map/ppermute | solution.py:24
  162.3 1.8 %shard_map.88 = bf16[8192,256]{1,0:T(8,128)(2,1)} custom-call(s32[4]{0:T(128)S(1)} %pad_add_fusion.where_ref, bf16[2048,256]{1,0:T(8,128)(2,1)S(1)} %collective-permute-done.25.refs_0_, bf16[2048,256]{1,0:T(8,128)(2,1)S(1)} %collective-permute-done.31.refs_1_, bf16[8192,256]{1,0:T(8,128)(2,1)} %shard_map.87.refs_2_), custom_call_target="tpu_custom_call", output_to_operand_aliasing={{}: (3, {})} | custom-call | bytes 8388608 | tf_op jit(solution)/shard_map/pallas_call | solution.py:117
  (89 shorter events, 27.5 us)
Async XLA Ops:
  3.6 5.9 %collective-permute-start = (bf16[256,4096]{1,0:T(8,128)(2,1)S(1)}, bf16[256,4096]{1,0:T(8,128)(2,1)S(1)}, u32[]{:S(2)}, u32[]{:S(2)}) collective-permute-start(bf16[256,4096]{1,0:T(8,128)(2,1)S(1)} %shard_map.84), channel_id=1, source_target_pairs={{0,1},{1,0},{2,3},{3,2},{4,5},{5,4},{6,7},{7,6},{8,9},{9,8},{10,11... | collective-permute-start | bytes 6291464 | tf_op jit(solution)/shard_map/ppermute | solution.py:28
  3.9 4.6 %collective-permute-start.1 = (bf16[256,1024]{1,0:T(8,128)(2,1)S(1)}, bf16[256,1024]{1,0:T(8,128)(2,1)S(1)}, u32[]{:S(2)}, u32[]{:S(2)}) collective-permute-start(bf16[256,1024]{1,0:T(8,128)(2,1)S(1)} %copy-done.1), channel_id=1, source_target_pairs={{0,1},{1,0},{2,3},{3,2},{4,5},{5,4},{6,7},{7,6},{8,9},{9,8},{10,11... | collective-permute-start | bytes 1572872 | tf_op jit(solution)/shard_map/ppermute | solution.py:28
  8.6 14.9 %collective-permute-start.10 = (bf16[512,1024]{1,0:T(8,128)(2,1)S(1)}, bf16[512,1024]{1,0:T(8,128)(2,1)S(1)}, u32[]{:S(2)}, u32[]{:S(2)}) collective-permute-start(bf16[512,1024]{1,0:T(8,128)(2,1)S(1)} %constant_dynamic-update-slice_fusion), channel_id=1, source_target_pairs={{0,16},{1,49},{16,0},{17,33},{32,48},{33,17},{48,32},{49,1},{2,18}... | collective-permute-start | bytes 3145736 | tf_op jit(solution)/shard_map/ppermute | solution.py:24
  10.6 18.5 %collective-permute-start.11 = (bf16[512,512]{1,0:T(8,128)(2,1)S(1)}, bf16[512,512]{1,0:T(8,128)(2,1)S(1)}, u32[]{:S(2)}, u32[]{:S(2)}) collective-permute-start(bf16[512,512]{1,0:T(8,128)(2,1)S(1)} %get-tuple-element.19), channel_id=1, source_target_pairs={{0,16},{1,49},{16,0},{17,33},{32,48},{33,17},{48,32},{49,1},{2,18}... | collective-permute-start | bytes 1572872 | tf_op jit(solution)/shard_map/ppermute | solution.py:24
  12.0 19.2 %collective-permute-start.3 = (bf16[512,1024]{1,0:T(8,128)(2,1)S(1)}, bf16[512,1024]{1,0:T(8,128)(2,1)S(1)}, u32[]{:S(2)}, u32[]{:S(2)}) collective-permute-start(bf16[512,1024]{1,0:T(8,128)(2,1)S(1)} %constant_dynamic-update-slice_fusion), channel_id=1, source_target_pairs={{0,4},{1,13},{4,0},{5,9},{8,12},{9,5},{12,8},{13,1},{2,6},{3,15},{... | collective-permute-start | bytes 3145736 | tf_op jit(solution)/shard_map/ppermute | solution.py:24
  13.4 30.4 %collective-permute-start.2 = (bf16[512,512]{1,0:T(8,128)(2,1)S(1)}, bf16[512,512]{1,0:T(8,128)(2,1)S(1)}, u32[]{:S(2)}, u32[]{:S(2)}) collective-permute-start(bf16[512,512]{1,0:T(8,128)(2,1)S(1)} %get-tuple-element.13), channel_id=1, source_target_pairs={{0,4},{1,13},{4,0},{5,9},{8,12},{9,5},{12,8},{13,1},{2,6},{3,15},{... | collective-permute-start | bytes 1572872 | tf_op jit(solution)/shard_map/ppermute | solution.py:24
  14.0 24.0 %collective-permute-start.4 = (bf16[512,512]{1,0:T(8,128)(2,1)S(1)}, bf16[512,512]{1,0:T(8,128)(2,1)S(1)}, u32[]{:S(2)}, u32[]{:S(2)}) collective-permute-start(bf16[512,512]{1,0:T(8,128)(2,1)S(1)} %get-tuple-element.15), channel_id=1, source_target_pairs={{0,4},{1,13},{4,0},{5,9},{8,12},{9,5},{12,8},{13,1},{2,6},{3,15},{... | collective-permute-start | bytes 1572872 | tf_op jit(solution)/shard_map/ppermute | solution.py:24
  23.5 19.1 %collective-permute-start.9 = (bf16[512,512]{1,0:T(8,128)(2,1)S(1)}, bf16[512,512]{1,0:T(8,128)(2,1)S(1)}, u32[]{:S(2)}, u32[]{:S(2)}) collective-permute-start(bf16[512,512]{1,0:T(8,128)(2,1)S(1)} %get-tuple-element.17), channel_id=1, source_target_pairs={{0,16},{1,49},{16,0},{17,33},{32,48},{33,17},{48,32},{49,1},{2,18}... | collective-permute-start | bytes 1572872 | tf_op jit(solution)/shard_map/ppermute | solution.py:24
  30.9 31.6 %collective-permute-start.12 = (f16[256,1024]{1,0:T(8,128)(2,1)S(1)}, f16[256,1024]{1,0:T(8,128)(2,1)S(1)}, u32[]{:S(2)}, u32[]{:S(2)}) collective-permute-start(f16[256,1024]{1,0:T(8,128)(2,1)S(1)} %get-tuple-element.27), channel_id=1, source_target_pairs={{0,48},{1,17},{16,32},{17,1},{32,16},{33,49},{48,0},{49,33},{2,50}... | collective-permute-start | bytes 1572872 | tf_op jit(solution)/shard_map/ppermute | solution.py:24
  31.2 15.8 %collective-permute-start.13 = (f16[256,1024]{1,0:T(8,128)(2,1)S(1)}, f16[256,1024]{1,0:T(8,128)(2,1)S(1)}, u32[]{:S(2)}, u32[]{:S(2)}) collective-permute-start(f16[256,1024]{1,0:T(8,128)(2,1)S(1)} %get-tuple-element.28), channel_id=1, source_target_pairs={{0,48},{1,17},{16,32},{17,1},{32,16},{33,49},{48,0},{49,33},{2,50}... | collective-permute-start | bytes 1572872 | tf_op jit(solution)/shard_map/ppermute | solution.py:24
  39.7 25.9 %collective-permute-start.5 = (f16[256,1024]{1,0:T(8,128)(2,1)S(1)}, f16[256,1024]{1,0:T(8,128)(2,1)S(1)}, u32[]{:S(2)}, u32[]{:S(2)}) collective-permute-start(f16[256,1024]{1,0:T(8,128)(2,1)S(1)} %get-tuple-element.25), channel_id=1, source_target_pairs={{0,12},{1,5},{4,8},{5,1},{8,4},{9,13},{12,0},{13,9},{2,14},{3,7},{... | collective-permute-start | bytes 1572872 | tf_op jit(solution)/shard_map/ppermute | solution.py:24
  42.6 18.8 %collective-permute-start.6 = (f16[256,1024]{1,0:T(8,128)(2,1)S(1)}, f16[256,1024]{1,0:T(8,128)(2,1)S(1)}, u32[]{:S(2)}, u32[]{:S(2)}) collective-permute-start(f16[256,1024]{1,0:T(8,128)(2,1)S(1)} %get-tuple-element.26), channel_id=1, source_target_pairs={{0,12},{1,5},{4,8},{5,1},{8,4},{9,13},{12,0},{13,9},{2,14},{3,7},{... | collective-permute-start | bytes 1572872 | tf_op jit(solution)/shard_map/ppermute | solution.py:24
  47.2 15.3 %collective-permute-start.14 = (f16[256,1024]{1,0:T(8,128)(2,1)S(1)}, f16[256,1024]{1,0:T(8,128)(2,1)S(1)}, u32[]{:S(2)}, u32[]{:S(2)}) collective-permute-start(f16[256,1024]{1,0:T(8,128)(2,1)S(1)} %fusion.2), channel_id=1, source_target_pairs={{0,4},{1,13},{4,0},{5,9},{8,12},{9,5},{12,8},{13,1},{2,6},{3,15},{... | collective-permute-start | bytes 1572872 | tf_op jit(solution)/shard_map/ppermute | solution.py:24
  61.6 9.3 %collective-permute-start.7 = (f16[256,1024]{1,0:T(8,128)(2,1)S(1)}, f16[256,1024]{1,0:T(8,128)(2,1)S(1)}, u32[]{:S(2)}, u32[]{:S(2)}) collective-permute-start(f16[256,1024]{1,0:T(8,128)(2,1)S(1)} %fusion.7), channel_id=1, source_target_pairs={{0,16},{1,49},{16,0},{17,33},{32,48},{33,17},{48,32},{49,1},{2,18}... | collective-permute-start | bytes 1572872 | tf_op jit(solution)/shard_map/ppermute | solution.py:24
  62.8 9.4 %collective-permute-start.15 = (f16[128,1024]{1,0:T(8,128)(2,1)S(1)}, f16[128,1024]{1,0:T(8,128)(2,1)S(1)}, u32[]{:S(2)}, u32[]{:S(2)}) collective-permute-start(f16[128,1024]{1,0:T(8,128)(2,1)S(1)} %fusion.11), channel_id=1, source_target_pairs={{0,12},{1,5},{4,8},{5,1},{8,4},{9,13},{12,0},{13,9},{2,14},{3,7},{... | collective-permute-start | bytes 786440 | tf_op jit(solution)/shard_map/ppermute | solution.py:24
  71.9 7.8 %collective-permute-start.8 = (f16[128,1024]{1,0:T(8,128)(2,1)}, f16[128,1024]{1,0:T(8,128)(2,1)S(1)}, u32[]{:S(2)}, u32[]{:S(2)}) collective-permute-start(f16[128,1024]{1,0:T(8,128)(2,1)} %fusion.12), channel_id=1, source_target_pairs={{0,48},{1,17},{16,32},{17,1},{32,16},{33,49},{48,0},{49,33},{2,50}... | collective-permute-start | bytes 786440 | tf_op jit(solution)/shard_map/ppermute | solution.py:24
  79.9 7.4 %collective-permute-start.16 = (f16[256,512]{1,0:T(8,128)(2,1)S(1)}, f16[256,512]{1,0:T(8,128)(2,1)S(1)}, u32[]{:S(2)}, u32[]{:S(2)}) collective-permute-start(f16[256,512]{1,0:T(8,128)(2,1)S(1)} %multiply_convert_fusion), channel_id=1, source_target_pairs={{0,2},{1,195},{2,0},{3,65},{64,66},{65,3},{66,64},{67,129},{128,13... | collective-permute-start | bytes 786440 | tf_op jit(solution)/shard_map/ppermute | solution.py:181
  87.6 13.3 %collective-permute-start.18 = (f32[128,256]{1,0:T(8,128)S(1)}, f32[128,256]{1,0:T(8,128)S(1)}, u32[]{:S(2)}, u32[]{:S(2)}) collective-permute-start(f32[128,256]{1,0:T(8,128)S(1)} %get-tuple-element.31), channel_id=1, source_target_pairs={{0,128},{1,192},{64,129},{65,193},{128,0},{129,64},{192,1},{193,65... | collective-permute-start | bytes 393224 | tf_op jit(solution)/shard_map/ppermute | solution.py:193
  87.7 13.2 %collective-permute-start.17 = (f32[128,256]{1,0:T(8,128)S(1)}, f32[128,256]{1,0:T(8,128)S(1)}, u32[]{:S(2)}, u32[]{:S(2)}) collective-permute-start(f32[128,256]{1,0:T(8,128)S(1)} %get-tuple-element.32), channel_id=1, source_target_pairs={{0,129},{1,193},{64,128},{65,192},{128,1},{129,65},{192,0},{193,64... | collective-permute-start | bytes 393224 | tf_op jit(solution)/shard_map/ppermute | solution.py:193
  91.8 9.1 %collective-permute-start.19 = (f32[128,256]{1,0:T(8,128)S(1)}, f32[128,256]{1,0:T(8,128)S(1)}, u32[]{:S(2)}, u32[]{:S(2)}) collective-permute-start(f32[128,256]{1,0:T(8,128)S(1)} %get-tuple-element.33), channel_id=1, source_target_pairs={{0,1},{1,65},{64,0},{65,64},{128,129},{129,193},{192,128},{193,192... | collective-permute-start | bytes 393224 | tf_op jit(solution)/shard_map/ppermute | solution.py:193
  93.9 7.6 %collective-permute-start.20 = (f32[128,256]{1,0:T(8,128)S(1)}, f32[128,256]{1,0:T(8,128)S(1)}, u32[]{:S(2)}, u32[]{:S(2)}) collective-permute-start(f32[128,256]{1,0:T(8,128)S(1)} %get-tuple-element.34), channel_id=1, source_target_pairs={{0,0},{1,64},{64,1},{65,65},{128,128},{129,192},{192,129},{193,193... | collective-permute-start | bytes 393224 | tf_op jit(solution)/shard_map/ppermute | solution.py:193
  102.3 8.7 %collective-permute-start.26 = (bf16[128,256]{1,0:T(8,128)(2,1)S(1)}, bf16[128,256]{1,0:T(8,128)(2,1)S(1)}, u32[]{:S(2)}, u32[]{:S(2)}) collective-permute-start(bf16[128,256]{1,0:T(8,128)(2,1)S(1)} %get-tuple-element.21), channel_id=1, source_target_pairs={{0,128},{64,192},{128,0},{192,64},{1,129},{65,193},{129,1},{193,65... | collective-permute-start | bytes 196616 | tf_op jit(solution)/shard_map/ppermute | solution.py:202
  105.3 9.0 %collective-permute-start.27 = (bf16[128,256]{1,0:T(8,128)(2,1)S(1)}, bf16[128,256]{1,0:T(8,128)(2,1)S(1)}, u32[]{:S(2)}, u32[]{:S(2)}) collective-permute-start(bf16[128,256]{1,0:T(8,128)(2,1)S(1)} %get-tuple-element.21), channel_id=1, source_target_pairs={{0,192},{64,128},{128,64},{192,0},{1,193},{65,129},{129,65},{193,1... | collective-permute-start | bytes 196616 | tf_op jit(solution)/shard_map/ppermute | solution.py:202
  107.7 6.7 %collective-permute-start.21 = (bf16[128,256]{1,0:T(8,128)(2,1)S(1)}, bf16[128,256]{1,0:T(8,128)(2,1)S(1)}, u32[]{:S(2)}, u32[]{:S(2)}) collective-permute-start(bf16[128,256]{1,0:T(8,128)(2,1)S(1)} %get-tuple-element.21), channel_id=1, source_target_pairs={{0,64},{64,0},{128,192},{192,128},{1,65},{65,1},{129,193},{193,129... | collective-permute-start | bytes 196616 | tf_op jit(solution)/shard_map/ppermute | solution.py:202
  114.3 5.1 %collective-permute-start.28 = (bf16[256,256]{1,0:T(8,128)(2,1)S(1)}, bf16[256,256]{1,0:T(8,128)(2,1)S(1)}, u32[]{:S(2)}, u32[]{:S(2)}) collective-permute-start(bf16[256,256]{1,0:T(8,128)(2,1)S(1)} %pad_maximum_fusion.6), channel_id=1, source_target_pairs={{0,4},{1,13},{4,0},{5,9},{8,12},{9,5},{12,8},{13,1},{2,6},{3,15},{... | collective-permute-start | bytes 393224 | tf_op jit(solution)/shard_map/ppermute | solution.py:24
  114.5 8.0 %collective-permute-start.22 = (bf16[256,256]{1,0:T(8,128)(2,1)S(1)}, bf16[256,256]{1,0:T(8,128)(2,1)S(1)}, u32[]{:S(2)}, u32[]{:S(2)}) collective-permute-start(bf16[256,256]{1,0:T(8,128)(2,1)S(1)} %pad_maximum_fusion.5), channel_id=1, source_target_pairs={{0,16},{1,49},{16,0},{17,33},{32,48},{33,17},{48,32},{49,1},{2,18}... | collective-permute-start | bytes 393224 | tf_op jit(solution)/shard_map/ppermute | solution.py:24
  119.4 7.9 %collective-permute-start.29 = (bf16[512,256]{1,0:T(8,128)(2,1)S(1)}, bf16[512,256]{1,0:T(8,128)(2,1)S(1)}, u32[]{:S(2)}, u32[]{:S(2)}) collective-permute-start(bf16[512,256]{1,0:T(8,128)(2,1)S(1)} %pad_maximum_fusion.4), channel_id=1, source_target_pairs={{0,12},{1,5},{4,8},{5,1},{8,4},{9,13},{12,0},{13,9},{2,14},{3,7},{... | collective-permute-start | bytes 786440 | tf_op jit(solution)/shard_map/ppermute | solution.py:24
  122.5 10.5 %collective-permute-start.23 = (bf16[512,256]{1,0:T(8,128)(2,1)S(1)}, bf16[512,256]{1,0:T(8,128)(2,1)S(1)}, u32[]{:S(2)}, u32[]{:S(2)}) collective-permute-start(bf16[512,256]{1,0:T(8,128)(2,1)S(1)} %pad_maximum_fusion.3), channel_id=1, source_target_pairs={{0,48},{1,17},{16,32},{17,1},{32,16},{33,49},{48,0},{49,33},{2,50}... | collective-permute-start | bytes 786440 | tf_op jit(solution)/shard_map/ppermute | solution.py:24
  127.3 9.3 %collective-permute-start.30 = (bf16[1024,256]{1,0:T(8,128)(2,1)S(1)}, bf16[1024,256]{1,0:T(8,128)(2,1)S(1)}, u32[]{:S(2)}, u32[]{:S(2)}) collective-permute-start(bf16[1024,256]{1,0:T(8,128)(2,1)S(1)} %pad_maximum_fusion.2), channel_id=1, source_target_pairs={{0,16},{1,49},{16,0},{17,33},{32,48},{33,17},{48,32},{49,1},{2,18}... | collective-permute-start | bytes 1572872 | tf_op jit(solution)/shard_map/ppermute | solution.py:24
  133.0 13.1 %collective-permute-start.24 = (bf16[1024,256]{1,0:T(8,128)(2,1)S(1)}, bf16[1024,256]{1,0:T(8,128)(2,1)S(1)}, u32[]{:S(2)}, u32[]{:S(2)}) collective-permute-start(bf16[1024,256]{1,0:T(8,128)(2,1)S(1)} %pad_maximum_fusion.1), channel_id=1, source_target_pairs={{0,4},{1,13},{4,0},{5,9},{8,12},{9,5},{12,8},{13,1},{2,6},{3,15},{... | collective-permute-start | bytes 1572872 | tf_op jit(solution)/shard_map/ppermute | solution.py:24
  136.6 16.1 %collective-permute-start.31 = (bf16[2048,256]{1,0:T(8,128)(2,1)S(1)}, bf16[2048,256]{1,0:T(8,128)(2,1)S(1)}, u32[]{:S(2)}, u32[]{:S(2)}) collective-permute-start(bf16[2048,256]{1,0:T(8,128)(2,1)S(1)} %constant_dynamic-update-slice_fusion.7.refs_1_), channel_id=1, source_target_pairs={{0,48},{1,17},{16,32},{17,1},{32,16},{33,49},{48,0},{49,33},{2,50}... | collective-permute-start | bytes 3145736 | tf_op jit(solution)/shard_map/ppermute | solution.py:24
  146.2 16.1 %collective-permute-start.25 = (bf16[2048,256]{1,0:T(8,128)(2,1)S(1)}, bf16[2048,256]{1,0:T(8,128)(2,1)S(1)}, u32[]{:S(2)}, u32[]{:S(2)}) collective-permute-start(bf16[2048,256]{1,0:T(8,128)(2,1)S(1)} %constant_dynamic-update-slice_fusion.2.refs_0_), channel_id=1, source_target_pairs={{0,12},{1,5},{4,8},{5,1},{8,4},{9,13},{12,0},{13,9},{2,14},{3,7},{... | collective-permute-start | bytes 3145736 | tf_op jit(solution)/shard_map/ppermute | solution.py:24
  (5 other events, 67.9 us)

commit v3 on v2

v3 whole, which is shorter than its diff:
```python
import math

import jax
import jax.numpy as jnp
from jax import lax
from jax.experimental import pallas as pl
from jax.experimental.pallas import tpu as pltpu
from jax.sharding import Mesh
from jax.sharding import PartitionSpec as P

first_bias = 1.0 - math.exp(100.0 * math.log(0.9))
second_bias = 1.0 - math.exp(100.0 * math.log(0.999))

F32, F16, BF16 = jnp.float32, jnp.float16, jnp.bfloat16
BLOCK = 128
VMEM = pltpu.CompilerParams(vmem_limit_bytes=32 * 2**20)

FIRST, SECOND = ("x", "y"), ("y", "x")
NEAR, NEXT = (1, 3), (3, 1)


def swap(array, axis, by, cross=False):
    pairs = [(2 * i + (c ^ cross), 2 * (i ^ by[c]) + c) for i in range(4) for c in range(2)]
    return lax.ppermute(array, (axis, "c"), pairs)


def other_core(array):
    return lax.ppermute(array, "c", [(0, 1), (1, 0)])


def order(core):
    return 0, 3 - 2 * core, 1 + 2 * core, 2


def owner(part, first, second, x, y):
    x_by, y_by = (first, second) if part == 0 else (second, first)
    return lax.bitwise_xor(y, y_by) * 4 + lax.bitwise_xor(x, x_by)


def other_rows(acts, where):
    half = acts.shape[1] // 4

    def kernel(where_ref, acts_ref, out_ref):
        for part in range(2):
            start = pl.multiple_of((2 * part + 1 - where_ref[3]) * half, half)
            out_ref[:, part * half : (part + 1) * half] = acts_ref[:, pl.ds(start, half)]

    vmem = pl.BlockSpec(memory_space=pltpu.VMEM)
    return pl.pallas_call(
        kernel,
        out_shape=jax.ShapeDtypeStruct((acts.shape[0], 2 * half), acts.dtype),
        in_specs=[pl.BlockSpec(memory_space=pltpu.SMEM), vmem],
        out_specs=vmem,
        compiler_params=VMEM,
        cost_estimate=pl.CostEstimate(
            flops=0, bytes_accessed=2 * acts.size, transcendentals=0
        ),
    )(where, acts)


def arrange(acts, peer, where, index):
    tokens = acts.shape[0]

    def kernel(where_ref, acts_ref, peer_ref, *out_refs):
        x, y, core = where_ref[0], where_ref[1], where_ref[3]
        distances = order(core)
        for part in range(2):
            for j in range(4):
                out_ref, place = out_refs[part], slice(j * BLOCK, (j + 1) * BLOCK)
                block = owner(part, distances[index], distances[j], x, y)
                own = ((2 * part + core) * 16 + block) * BLOCK
                out_ref[:tokens, place] = acts_ref[:, pl.ds(pl.multiple_of(own, BLOCK), BLOCK)]
                other = (part * 16 + block) * BLOCK
                out_ref[tokens:, place] = peer_ref[:, pl.ds(pl.multiple_of(other, BLOCK), BLOCK)]

    out = jax.ShapeDtypeStruct((2 * tokens, 4 * BLOCK), acts.dtype)
    vmem = pl.BlockSpec(memory_space=pltpu.VMEM)
    return pl.pallas_call(
        kernel,
        out_shape=[out] * 2,
        in_specs=[pl.BlockSpec(memory_space=pltpu.SMEM), vmem, vmem],
        out_specs=[vmem] * 2,
        compiler_params=VMEM,
        cost_estimate=pl.CostEstimate(
            flops=0, bytes_accessed=8 * out.size, transcendentals=0
        ),
    )(where, acts, peer)


def place(pieces, where, firsts, into=None):
    many = len(pieces)

    def kernel(where_ref, *refs):
        ins, out_ref, sem = refs[:many], refs[-2], refs[-1]
        x, y, zh, core = (where_ref[i] for i in range(4))
        distances = (0, 1 + 2 * core, 3 - 2 * core, 2)
        copies = []
        for part in range(2):
            for i, first in enumerate(firsts):
                for j in range(4):
                    for k in range(2):
                        block = lax.bitwise_xor(zh, 2 * part + k) * 16
                        block += owner(part, distances[first], distances[j], x, y)
                        copies.append(
                            pltpu.make_async_copy(
                                ins[part * len(firsts) + i].at[pl.ds((j * 2 + k) * BLOCK, BLOCK), :],
                                out_ref.at[pl.ds(pl.multiple_of(block * BLOCK, BLOCK), BLOCK), :],
                                sem,
                            )
                        )
        for copy in copies:
            copy.start()
        for copy in copies:
            copy.wait()

    anywhere = pl.BlockSpec(memory_space=pl.ANY)
    return pl.pallas_call(
        kernel,
        out_shape=jax.ShapeDtypeStruct((8192, 256), BF16),
        in_specs=[pl.BlockSpec(memory_space=pltpu.SMEM)]
        + [pl.BlockSpec(memory_space=pltpu.VMEM)] * many
        + [anywhere] * (into is not None),
        out_specs=anywhere,
        scratch_shapes=[pltpu.SemaphoreType.DMA],
        input_output_aliases={} if into is None else {1 + many: 0},
        compiler_params=VMEM,
        cost_estimate=pl.CostEstimate(
            flops=0, bytes_accessed=many * 2**20, transcendentals=0
        ),
    )(where, *pieces, *(() if into is None else (into,)))


def dot(a, b):
    return lax.dot_general(a, b, (((0,), (0,)), ((), ())), preferred_element_type=F32)


def received(array, swapped, scale):
    return swapped((array * scale).astype(F16)).astype(F32) * (1.0 / scale)


def per_device(acts, grad_out, master, moment1, moment2):
    x, y, zh, zl, core = (lax.axis_index(name) for name in ("x", "y", "zh", "zl", "c"))
    where = jnp.stack([x, y, zh, core]).astype(jnp.int32)
    parts = range(2)

    far_grad = [
        jnp.concatenate([swap(grad_out, FIRST[p], NEAR), swap(grad_out, FIRST[p], NEAR, True)], 0)
        for p in parts
    ]
    peer = other_core(other_rows(acts, where))
    sent = arrange(acts, peer, where, 3)
    far_acts = [[None, swap(sent[p], FIRST[p], NEAR)] for p in parts]
    grad_out, far_grad = lax.optimization_barrier((grad_out, far_grad))
    chip_grad = jnp.concatenate([grad_out, other_core(grad_out)], 0)
    later, chip_grad = lax.optimization_barrier((where, chip_grad))
    sent = arrange(acts, peer, later, 2)
    for p in parts:
        far_acts[p][0] = swap(sent[p], FIRST[p], NEAR)
    kept = [arrange(acts, peer, where, i) for i in range(2)]

    def partial(p, i):
        return dot(kept[i][p], chip_grad) + dot(far_acts[p][i], far_grad[p])

    passed = [partial(p, 1) for p in parts]
    late = [received(passed[p][256:], lambda v: swap(v, FIRST[p], NEXT), 64.0) for p in parts]
    soon = [received(passed[p][:256], lambda v: swap(v, FIRST[p], NEXT), 64.0) for p in parts]
    own = [partial(p, 0) for p in parts]
    level = []
    for p in parts:
        upper, lower = own[p][256:] + late[p], own[p][:256] + soon[p]
        level.append(
            lower[:128]
            + received(upper[128:], lambda v: swap(v, SECOND[p], (2, 2)), 32.0)
            + received(upper[:128], lambda v: swap(v, SECOND[p], NEAR), 32.0)
            + received(lower[128:], lambda v: swap(v, SECOND[p], NEXT), 32.0)
        )

    grad = 0.0
    for j, l, k in ((1, 1, 1), (1, 1, 0), (1, 0, 1), (1, 0, 0), (0, 1, 1), (0, 1, 0), (0, 0, 1), (0, 0, 0)):
        rows = jnp.where(lax.bitwise_xor(zh // 2, j) == 0, level[0], level[1])
        rows = jnp.where(lax.bitwise_xor(zl, l) == 0, rows[:, :512], rows[:, 512:])
        block = jnp.where(lax.bitwise_xor(zh % 2, k) == 0, rows[:, :256], rows[:, 256:])
        pairs = [
            (4 * z + 2 * a + c, 4 * (c + 2 * ((z // 2) ^ j)) + 2 * (a ^ l) + ((z % 2) ^ k))
            for z in range(4)
            for a in range(2)
            for c in range(2)
        ]
        grad = grad + received(block, lambda v: lax.ppermute(v, ("zh", "zl", "c"), pairs), 8.0)

    new_moment1 = 0.9 * moment1 + 0.1 * grad
    new_moment2 = 0.999 * moment2 + 0.001 * grad * grad
    update = new_moment1 / first_bias / (jnp.sqrt(new_moment2 / second_bias) + 1e-08)
    new_master = master - 0.01 * (update + 0.1 * master)

    own = new_master.astype(BF16)
    z = [own] + [
        lax.ppermute(own, "zh", [(i, i ^ k) for i in range(4)]) for k in (1, 2, 3)
    ]
    pieces = [jnp.concatenate(z[:2], 0), jnp.concatenate(z[2:], 0)]
    pieces = [
        jnp.concatenate([pieces[p]] + [swap(pieces[p], SECOND[p], by) for by in (NEAR, NEXT, (2, 2))], 0)
        for p in parts
    ]
    near = [swap(pieces[p], FIRST[p], NEAR) for p in parts]
    following = [swap(pieces[p], FIRST[p], NEXT) for p in parts]
    last = [swap(near[p], FIRST[p], NEXT) for p in parts]
    first = [array for p in parts for array in (pieces[p], near[p], following[p])]
    new_weights = place(last, where, (3,), place(first, where, (0, 1, 2)))
    return (new_master, new_moment1, new_moment2, new_weights)


def solution(mesh):
    fine = Mesh(mesh.devices.reshape(4, 4, 4, 2, 2), ("zh", "y", "x", "zl", "c"))
    dp, tensor = ("zh", "y", "x"), ("zl", "c")
    tokens, state = P(dp + tensor, None), P(dp, tensor)
    return jax.shard_map(
        per_device,
        mesh=fine,
        in_specs=(tokens, tokens, state, state, state),
        out_specs=(state, state, state, P(None, tensor)),
        check_vma=False,
    )
```

time: 164 us -> 150 us (0.915)
  the two profiles are of different devices: /device:TPU:216 before, /device:TPU:2 now
where the time goes in v3:
time: 150 us; the launch traced here: 148 us
  starting transfers between devices  69.8 us (47%)
  waiting for transfers between devices  55.1 us (37%)
  Pallas kernels  7.66 us (5%)
  matrix products  5.84 us (4%)
  other arithmetic  4.83 us (3%)
  local copies, waits for them, and re-layouts  3.25 us (2%)
    ppermute x30, waiting for transfers between devices, swap(): return lax.ppermute(array, (axis, 'c'), pairs)  48.3 us
    ppermute x30, starting transfers between devices, swap(): return lax.ppermute(array, (axis, 'c'), pairs)  43.7 us
    ppermute x8, starting transfers between devices, per_device(): lax.ppermute(v, ('zh', 'zl', 'c'), pairs)  18.8 us
    ppermute x3, starting transfers between devices, per_device(): lax.ppermute(own, 'zh', [(i, i ^ k) for i in range(4)])  7.14 us
    dot_general x8, matrix products, dot(): lax.dot_general(a, b, (((0,), (0,)), ((), ())), preferred_element_type=F32)  5.84 us
    ppermute x8, waiting for transfers between devices, per_device(): lax.ppermute(v, ('zh', 'zl', 'c'), pairs)  4.52 us
    pallas_call x2, Pallas kernels, place(): pl.pallas_call(kernel, out_shape=jax.ShapeDtypeStruct((8192, 256), BF16),...  3.67 us
    pallas_call x4, Pallas kernels, arrange(): pl.pallas_call(kernel, out_shape=[out] * 2, in_specs=[pl.BlockSpec(memory...  3.3 us
  transfers between devices with their start and end apart: 43, of which 19 were waited for; matrix products, arithmetic and copies ran while one was open for 5% of the time, Pallas kernels for 4%

profile of v3, /device:TPU:2, one launch (start us, length us, event | category | flops | bytes accessed | tf_op | source)
XLA Modules:
  0.0 147.8 jit_solution(2950316700761790627)
XLA Ops:
  0.7 2.2 %copy-done = bf16[256,8192]{1,0:T(8,128)(2,1)S(1)} copy-done((bf16[256,8192]{1,0:T(8,128)(2,1)S(1)}, bf16[256,8192]{1,0:T(8,128)(2,1)}, u32[]{:S(2)}) %copy-start) | copy-done | bytes 4194328
  5.3 1.8 %collective-permute-start.1 = (bf16[256,1024]{1,0:T(8,128)(2,1)S(1)}, bf16[256,1024]{1,0:T(8,128)(2,1)S(1)}, u32[]{:S(2)}, u32[]{:S(2)}) collective-permute-start(bf16[256,1024]{1,0:T(8,128)(2,1)S(1)} %copy-done.1), channel_id=1, source_target_pairs={{0,4},{1,13},{4,0},{5,9},{8,12},{9,5},{12,8},{13,1},{2,6},{3,15},{... | collective-permute-start | bytes 1572872 | tf_op jit(solution)/shard_map/ppermute | solution.py:24
  7.1 1.6 %collective-permute-start.3 = (bf16[256,1024]{1,0:T(8,128)(2,1)S(1)}, bf16[256,1024]{1,0:T(8,128)(2,1)S(1)}, u32[]{:S(2)}, u32[]{:S(2)}) collective-permute-start(bf16[256,1024]{1,0:T(8,128)(2,1)S(1)} %copy-done.1), channel_id=1, source_target_pairs={{0,16},{1,49},{16,0},{17,33},{32,48},{33,17},{48,32},{49,1},{2,18}... | collective-permute-start | bytes 1572872 | tf_op jit(solution)/shard_map/ppermute | solution.py:24
  9.1 8.1 %collective-permute-done.2 = bf16[256,1024]{1,0:T(8,128)(2,1)S(1)} collective-permute-done((bf16[256,1024]{1,0:T(8,128)(2,1)S(1)}, bf16[256,1024]{1,0:T(8,128)(2,1)S(1)}, u32[]{:S(2)}, u32[]{:S(2)}) %collective-permute-start.2) | collective-permute-done | bytes 524320 | tf_op jit(solution)/shard_map/ppermute | solution.py:24
  18.6 2.3 %collective-permute-done.3 = bf16[256,1024]{1,0:T(8,128)(2,1)S(1)} collective-permute-done((bf16[256,1024]{1,0:T(8,128)(2,1)S(1)}, bf16[256,1024]{1,0:T(8,128)(2,1)S(1)}, u32[]{:S(2)}, u32[]{:S(2)}) %collective-permute-start.3) | collective-permute-done | bytes 524320 | tf_op jit(solution)/shard_map/ppermute | solution.py:24
  25.8 1.8 %collective-permute-start.6 = (bf16[512,512]{1,0:T(8,128)(2,1)S(1)}, bf16[512,512]{1,0:T(8,128)(2,1)S(1)}, u32[]{:S(2)}, u32[]{:S(2)}) collective-permute-start(bf16[512,512]{1,0:T(8,128)(2,1)S(1)} %get-tuple-element.21), channel_id=1, source_target_pairs={{0,4},{1,13},{4,0},{5,9},{8,12},{9,5},{12,8},{13,1},{2,6},{3,15},{... | collective-permute-start | bytes 1572872 | tf_op jit(solution)/shard_map/ppermute | solution.py:24
  30.2 2.0 %collective-permute-done.14 = bf16[512,512]{1,0:T(8,128)(2,1)S(1)} collective-permute-done((bf16[512,512]{1,0:T(8,128)(2,1)S(1)}, bf16[512,512]{1,0:T(8,128)(2,1)S(1)}, u32[]{:S(2)}, u32[]{:S(2)}) %collective-permute-start.14) | collective-permute-done | bytes 524320 | tf_op jit(solution)/shard_map/ppermute | solution.py:24
  33.9 3.1 %collective-permute-start.16 = (f16[256,1024]{1,0:T(8,128)(2,1)S(1)}, f16[256,1024]{1,0:T(8,128)(2,1)S(1)}, u32[]{:S(2)}, u32[]{:S(2)}) collective-permute-start(f16[256,1024]{1,0:T(8,128)(2,1)S(1)} %get-tuple-element.39), channel_id=1, source_target_pairs={{0,48},{1,17},{16,32},{17,1},{32,16},{33,49},{48,0},{49,33},{2,50}... | collective-permute-start | bytes 1572872 | tf_op jit(solution)/shard_map/ppermute | solution.py:24
  44.4 5.6 %collective-permute-done.15 = f16[256,1024]{1,0:T(8,128)(2,1)S(1)} collective-permute-done((f16[256,1024]{1,0:T(8,128)(2,1)S(1)}, f16[256,1024]{1,0:T(8,128)(2,1)S(1)}, u32[]{:S(2)}, u32[]{:S(2)}) %collective-permute-start.15) | collective-permute-done | bytes 524320 | tf_op jit(solution)/shard_map/ppermute | solution.py:24
  51.7 2.1 %collective-permute-start.17 = (f16[128,1024]{1,0:T(8,128)(2,1)S(1)}, f16[128,1024]{1,0:T(8,128)(2,1)}, u32[]{:S(2)}, u32[]{:S(2)}) collective-permute-start(f16[128,1024]{1,0:T(8,128)(2,1)S(1)} %get-tuple-element.45), channel_id=1, source_target_pairs={{0,8},{1,9},{4,12},{5,13},{8,0},{9,1},{12,4},{13,5},{2,10},{3,11},... | collective-permute-start | bytes 786440 | tf_op jit(solution)/shard_map/ppermute | solution.py:24
  55.3 3.1 %collective-permute-start.12 = (f16[128,1024]{1,0:T(8,128)(2,1)S(1)}, f16[128,1024]{1,0:T(8,128)(2,1)}, u32[]{:S(2)}, u32[]{:S(2)}) collective-permute-start(f16[128,1024]{1,0:T(8,128)(2,1)S(1)} %fusion.9), channel_id=1, source_target_pairs={{0,48},{1,17},{16,32},{17,1},{32,16},{33,49},{48,0},{49,33},{2,50}... | collective-permute-start | bytes 786440 | tf_op jit(solution)/shard_map/ppermute | solution.py:24
  58.6 6.4 %collective-permute-done.19 = f16[128,1024]{1,0:T(8,128)(2,1)S(1)} collective-permute-done((f16[128,1024]{1,0:T(8,128)(2,1)S(1)}, f16[128,1024]{1,0:T(8,128)(2,1)S(1)}, u32[]{:S(2)}, u32[]{:S(2)}) %collective-permute-start.19) | collective-permute-done | bytes 262176 | tf_op jit(solution)/shard_map/ppermute | solution.py:24
  65.8 4.9 %collective-permute-done.12 = f16[128,1024]{1,0:T(8,128)(2,1)} collective-permute-done((f16[128,1024]{1,0:T(8,128)(2,1)S(1)}, f16[128,1024]{1,0:T(8,128)(2,1)}, u32[]{:S(2)}, u32[]{:S(2)}) %collective-permute-start.12) | collective-permute-done | bytes 262176 | tf_op jit(solution)/shard_map/ppermute | solution.py:24
  70.6 1.6 %collective-permute-done.11 = f16[128,1024]{1,0:T(8,128)(2,1)} collective-permute-done((f16[128,1024]{1,0:T(8,128)(2,1)S(1)}, f16[128,1024]{1,0:T(8,128)(2,1)}, u32[]{:S(2)}, u32[]{:S(2)}) %collective-permute-start.11) | collective-permute-done | bytes 262176 | tf_op jit(solution)/shard_map/ppermute | solution.py:24
  72.2 1.8 %broadcast_select_fusion.1 = (f32[128,1024]{1,0:T(8,128)S(1)}, f32[128,1024]{1,0:T(8,128)S(1)}) fusion(pred[]{:T(512)S(6)} %eq.23, f16[128,1024]{1,0:T(8,128)(2,1)} %collective-permute-done.12, f16[128,1024]{1,0:T(8,128)(2,1)} %collective-permute-done.11, f16[128,1024]{1,0:T(8,128)(2,1)} %collective-permute-done.10, f32[256,1024]{1,0:T(8,128)S(1)} %get-tuple-element.42, ...), kind=kLoop, calls=%fused_computation.38 | loop fusion | flops 2621440 | bytes 3670018 | tf_op jit(solution)/shard_map/jit(_where)/select_n | solution.py:180
  76.4 2.9 %collective-permute-start.26 = (f16[128,256]{1,0:T(8,128)(2,1)S(1)}, f16[128,256]{1,0:T(8,128)(2,1)S(1)}, u32[]{:S(2)}, u32[]{:S(2)}) collective-permute-start(f16[128,256]{1,0:T(8,128)(2,1)S(1)} %get-tuple-element.59), channel_id=1, source_target_pairs={{0,1},{1,65},{2,3},{3,67},{64,0},{65,64},{66,2},{67,66},{128,129},... | collective-permute-start | bytes 196616 | tf_op jit(solution)/shard_map/ppermute | solution.py:189
  80.1 7.4 %collective-permute-start.22 = (f16[128,256]{1,0:T(8,128)(2,1)S(1)}, f16[128,256]{1,0:T(8,128)(2,1)S(1)}, u32[]{:S(2)}, u32[]{:S(2)}) collective-permute-start(f16[128,256]{1,0:T(8,128)(2,1)S(1)} %get-tuple-element.55), channel_id=1, source_target_pairs={{0,129},{1,193},{2,131},{3,195},{64,128},{65,192},{66,130},{67,194... | collective-permute-start | bytes 196616 | tf_op jit(solution)/shard_map/ppermute | solution.py:189
  88.1 5.0 %collective-permute-start.21 = (f16[128,256]{1,0:T(8,128)(2,1)S(1)}, f16[128,256]{1,0:T(8,128)(2,1)S(1)}, u32[]{:S(2)}, u32[]{:S(2)}) collective-permute-start(f16[128,256]{1,0:T(8,128)(2,1)S(1)} %get-tuple-element.54), channel_id=1, source_target_pairs={{0,130},{1,194},{2,128},{3,192},{64,131},{65,195},{66,129},{67,193... | collective-permute-start | bytes 196616 | tf_op jit(solution)/shard_map/ppermute | solution.py:189
  93.1 2.8 %collective-permute-done.23 = f16[128,256]{1,0:T(8,128)(2,1)S(1)} collective-permute-done((f16[128,256]{1,0:T(8,128)(2,1)S(1)}, f16[128,256]{1,0:T(8,128)(2,1)S(1)}, u32[]{:S(2)}, u32[]{:S(2)}) %collective-permute-start.23) | collective-permute-done | bytes 65568 | tf_op jit(solution)/shard_map/ppermute | solution.py:189
  96.0 1.7 %collective-permute-done.21 = f16[128,256]{1,0:T(8,128)(2,1)S(1)} collective-permute-done((f16[128,256]{1,0:T(8,128)(2,1)S(1)}, f16[128,256]{1,0:T(8,128)(2,1)S(1)}, u32[]{:S(2)}, u32[]{:S(2)}) %collective-permute-start.21) | collective-permute-done | bytes 65568 | tf_op jit(solution)/shard_map/ppermute | solution.py:189
  98.5 3.6 %collective-permute-start.28 = (bf16[128,256]{1,0:T(8,128)(2,1)S(1)}, bf16[128,256]{1,0:T(8,128)(2,1)S(1)}, u32[]{:S(2)}, u32[]{:S(2)}) collective-permute-start(bf16[128,256]{1,0:T(8,128)(2,1)S(1)} %get-tuple-element.31), channel_id=1, source_target_pairs={{0,64},{64,0},{128,192},{192,128},{1,65},{65,1},{129,193},{193,129... | collective-permute-start | bytes 196616 | tf_op jit(solution)/shard_map/ppermute | solution.py:198
  102.1 2.6 %collective-permute-start.34 = (bf16[128,256]{1,0:T(8,128)(2,1)S(1)}, bf16[128,256]{1,0:T(8,128)(2,1)S(1)}, u32[]{:S(2)}, u32[]{:S(2)}) collective-permute-start(bf16[128,256]{1,0:T(8,128)(2,1)S(1)} %get-tuple-element.31), channel_id=1, source_target_pairs={{0,128},{64,192},{128,0},{192,64},{1,129},{65,193},{129,1},{193,65... | collective-permute-start | bytes 196616 | tf_op jit(solution)/shard_map/ppermute | solution.py:198
  105.7 2.5 %collective-permute-start.31 = (bf16[256,256]{1,0:T(8,128)(2,1)S(1)}, bf16[256,256]{1,0:T(8,128)(2,1)S(1)}, u32[]{:S(2)}, u32[]{:S(2)}) collective-permute-start(bf16[256,256]{1,0:T(8,128)(2,1)S(1)} %pad_maximum_fusion.3), channel_id=1, source_target_pairs={{0,32},{1,33},{16,48},{17,49},{32,0},{33,1},{48,16},{49,17},{2,34}... | collective-permute-start | bytes 393224 | tf_op jit(solution)/shard_map/ppermute | solution.py:24
  109.6 2.1 %collective-permute-done.34 = bf16[128,256]{1,0:T(8,128)(2,1)S(1)} collective-permute-done((bf16[128,256]{1,0:T(8,128)(2,1)S(1)}, bf16[128,256]{1,0:T(8,128)(2,1)S(1)}, u32[]{:S(2)}, u32[]{:S(2)}) %collective-permute-start.34) | collective-permute-done | bytes 65568 | tf_op jit(solution)/shard_map/ppermute | solution.py:198
  113.2 2.4 %collective-permute-start.37 = (bf16[256,256]{1,0:T(8,128)(2,1)S(1)}, bf16[256,256]{1,0:T(8,128)(2,1)S(1)}, u32[]{:S(2)}, u32[]{:S(2)}) collective-permute-start(bf16[256,256]{1,0:T(8,128)(2,1)S(1)} %get-tuple-element.61), channel_id=1, source_target_pairs={{0,12},{1,5},{4,8},{5,1},{8,4},{9,13},{12,0},{13,9},{2,14},{3,7},{... | collective-permute-start | bytes 393224 | tf_op jit(solution)/shard_map/ppermute | solution.py:24
  115.7 1.9 %collective-permute-start.36 = (bf16[256,256]{1,0:T(8,128)(2,1)S(1)}, bf16[256,256]{1,0:T(8,128)(2,1)S(1)}, u32[]{:S(2)}, u32[]{:S(2)}) collective-permute-start(bf16[256,256]{1,0:T(8,128)(2,1)S(1)} %get-tuple-element.61), channel_id=1, source_target_pairs={{0,4},{1,13},{4,0},{5,9},{8,12},{9,5},{12,8},{13,1},{2,6},{3,15},{... | collective-permute-start | bytes 393224 | tf_op jit(solution)/shard_map/ppermute | solution.py:24
  118.2 2.6 %collective-permute-done.36 = bf16[256,256]{1,0:T(8,128)(2,1)S(1)} collective-permute-done((bf16[256,256]{1,0:T(8,128)(2,1)S(1)}, bf16[256,256]{1,0:T(8,128)(2,1)S(1)}, u32[]{:S(2)}, u32[]{:S(2)}) %collective-permute-start.36) | collective-permute-done | bytes 131104 | tf_op jit(solution)/shard_map/ppermute | solution.py:24
  122.7 2.9 %collective-permute-start.42 = (bf16[1024,256]{1,0:T(8,128)(2,1)S(1)}, bf16[1024,256]{1,0:T(8,128)(2,1)S(1)}, u32[]{:S(2)}, u32[]{:S(2)}) collective-permute-start(bf16[1024,256]{1,0:T(8,128)(2,1)S(1)} %constant_dynamic-update-slice_fusion.7.refs_3_), channel_id=1, source_target_pairs={{0,48},{1,17},{16,32},{17,1},{32,16},{33,49},{48,0},{49,33},{2,50}... | collective-permute-start | bytes 1572872 | tf_op jit(solution)/shard_map/ppermute | solution.py:24
  128.4 4.9 %collective-permute-done.39.refs_4_ = bf16[1024,256]{1,0:T(8,128)(2,1)S(1)} collective-permute-done((bf16[1024,256]{1,0:T(8,128)(2,1)S(1)}, bf16[1024,256]{1,0:T(8,128)(2,1)S(1)}, u32[]{:S(2)}, u32[]{:S(2)}) %collective-permute-start.39) | collective-permute-done | bytes 524320 | tf_op jit(solution)/shard_map/ppermute | solution.py:24
  133.3 5.6 %collective-permute-start.40 = (bf16[1024,256]{1,0:T(8,128)(2,1)S(1)}, bf16[1024,256]{1,0:T(8,128)(2,1)S(1)}, u32[]{:S(2)}, u32[]{:S(2)}) collective-permute-start(bf16[1024,256]{1,0:T(8,128)(2,1)S(1)} %collective-permute-done.39.refs_4_), channel_id=1, source_target_pairs={{0,48},{1,17},{16,32},{17,1},{32,16},{33,49},{48,0},{49,33},{2,50}... | collective-permute-start | bytes 1572872 | tf_op jit(solution)/shard_map/ppermute | solution.py:24
  138.9 2.2 %shard_map.89.refs_2_ = bf16[8192,256]{1,0:T(8,128)(2,1)} custom-call(s32[4]{0:T(128)S(1)} %pad_add_fusion.where_ref, bf16[1024,256]{1,0:T(8,128)(2,1)S(1)} %constant_dynamic-update-slice_fusion.refs_0_, bf16[1024,256]{1,0:T(8,128)(2,1)S(1)} %collective-permute-done.32.refs_1_, bf16[1024,256]{1,0:T(8,128)(2,1)S(1)} %collective-permute-done.41.refs_2_, ...), custom_call_target="tpu_custom_call" | custom-call | bytes 6291456 | tf_op jit(solution)/shard_map/pallas_call | solution.py:117
  141.1 5.0 %collective-permute-done.40.refs_1_ = bf16[1024,256]{1,0:T(8,128)(2,1)S(1)} collective-permute-done((bf16[1024,256]{1,0:T(8,128)(2,1)S(1)}, bf16[1024,256]{1,0:T(8,128)(2,1)S(1)}, u32[]{:S(2)}, u32[]{:S(2)}) %collective-permute-start.40) | collective-permute-done | bytes 524320 | tf_op jit(solution)/shard_map/ppermute | solution.py:24
  (110 shorter events, 40.2 us)
Async XLA Ops:
  3.6 18.5 %collective-permute-start = (bf16[256,4096]{1,0:T(8,128)(2,1)S(1)}, bf16[256,4096]{1,0:T(8,128)(2,1)S(1)}, u32[]{:S(2)}, u32[]{:S(2)}) collective-permute-start(bf16[256,4096]{1,0:T(8,128)(2,1)S(1)} %shard_map.84), channel_id=1, source_target_pairs={{0,1},{1,0},{2,3},{3,2},{4,5},{5,4},{6,7},{7,6},{8,9},{9,8},{10,11... | collective-permute-start | bytes 6291464 | tf_op jit(solution)/shard_map/ppermute | solution.py:28
  3.9 13.2 %collective-permute-start.2 = (bf16[256,1024]{1,0:T(8,128)(2,1)S(1)}, bf16[256,1024]{1,0:T(8,128)(2,1)S(1)}, u32[]{:S(2)}, u32[]{:S(2)}) collective-permute-start(bf16[256,1024]{1,0:T(8,128)(2,1)S(1)} %copy-done.1), channel_id=1, source_target_pairs={{1,4},{0,13},{5,0},{4,9},{9,12},{8,5},{13,8},{12,1},{3,6},{2,15},{... | collective-permute-start | bytes 1572872 | tf_op jit(solution)/shard_map/ppermute | solution.py:24
  5.3 13.3 %collective-permute-start.1 = (bf16[256,1024]{1,0:T(8,128)(2,1)S(1)}, bf16[256,1024]{1,0:T(8,128)(2,1)S(1)}, u32[]{:S(2)}, u32[]{:S(2)}) collective-permute-start(bf16[256,1024]{1,0:T(8,128)(2,1)S(1)} %copy-done.1), channel_id=1, source_target_pairs={{0,4},{1,13},{4,0},{5,9},{8,12},{9,5},{12,8},{13,1},{2,6},{3,15},{... | collective-permute-start | bytes 1572872 | tf_op jit(solution)/shard_map/ppermute | solution.py:24
  7.1 13.8 %collective-permute-start.3 = (bf16[256,1024]{1,0:T(8,128)(2,1)S(1)}, bf16[256,1024]{1,0:T(8,128)(2,1)S(1)}, u32[]{:S(2)}, u32[]{:S(2)}) collective-permute-start(bf16[256,1024]{1,0:T(8,128)(2,1)S(1)} %copy-done.1), channel_id=1, source_target_pairs={{0,16},{1,49},{16,0},{17,33},{32,48},{33,17},{48,32},{49,1},{2,18}... | collective-permute-start | bytes 1572872 | tf_op jit(solution)/shard_map/ppermute | solution.py:24
  8.7 13.2 %collective-permute-start.4 = (bf16[256,1024]{1,0:T(8,128)(2,1)S(1)}, bf16[256,1024]{1,0:T(8,128)(2,1)S(1)}, u32[]{:S(2)}, u32[]{:S(2)}) collective-permute-start(bf16[256,1024]{1,0:T(8,128)(2,1)S(1)} %copy-done.1), channel_id=1, source_target_pairs={{1,16},{0,49},{17,0},{16,33},{33,48},{32,17},{49,32},{48,1},{3,18}... | collective-permute-start | bytes 1572872 | tf_op jit(solution)/shard_map/ppermute | solution.py:24
  24.5 12.7 %collective-permute-start.7 = (bf16[512,512]{1,0:T(8,128)(2,1)S(1)}, bf16[512,512]{1,0:T(8,128)(2,1)S(1)}, u32[]{:S(2)}, u32[]{:S(2)}) collective-permute-start(bf16[512,512]{1,0:T(8,128)(2,1)S(1)} %get-tuple-element.24), channel_id=1, source_target_pairs={{0,4},{1,13},{4,0},{5,9},{8,12},{9,5},{12,8},{13,1},{2,6},{3,15},{... | collective-permute-start | bytes 1572872 | tf_op jit(solution)/shard_map/ppermute | solution.py:24
  25.8 16.8 %collective-permute-start.6 = (bf16[512,512]{1,0:T(8,128)(2,1)S(1)}, bf16[512,512]{1,0:T(8,128)(2,1)S(1)}, u32[]{:S(2)}, u32[]{:S(2)}) collective-permute-start(bf16[512,512]{1,0:T(8,128)(2,1)S(1)} %get-tuple-element.21), channel_id=1, source_target_pairs={{0,4},{1,13},{4,0},{5,9},{8,12},{9,5},{12,8},{13,1},{2,6},{3,15},{... | collective-permute-start | bytes 1572872 | tf_op jit(solution)/shard_map/ppermute | solution.py:24
  27.6 12.6 %collective-permute-start.13 = (bf16[512,512]{1,0:T(8,128)(2,1)S(1)}, bf16[512,512]{1,0:T(8,128)(2,1)S(1)}, u32[]{:S(2)}, u32[]{:S(2)}) collective-permute-start(bf16[512,512]{1,0:T(8,128)(2,1)S(1)} %get-tuple-element.26), channel_id=1, source_target_pairs={{0,16},{1,49},{16,0},{17,33},{32,48},{33,17},{48,32},{49,1},{2,18}... | collective-permute-start | bytes 1572872 | tf_op jit(solution)/shard_map/ppermute | solution.py:24
  33.9 10.5 %collective-permute-start.16 = (f16[256,1024]{1,0:T(8,128)(2,1)S(1)}, f16[256,1024]{1,0:T(8,128)(2,1)S(1)}, u32[]{:S(2)}, u32[]{:S(2)}) collective-permute-start(f16[256,1024]{1,0:T(8,128)(2,1)S(1)} %get-tuple-element.39), channel_id=1, source_target_pairs={{0,48},{1,17},{16,32},{17,1},{32,16},{33,49},{48,0},{49,33},{2,50}... | collective-permute-start | bytes 1572872 | tf_op jit(solution)/shard_map/ppermute | solution.py:24
  37.0 13.0 %collective-permute-start.15 = (f16[256,1024]{1,0:T(8,128)(2,1)S(1)}, f16[256,1024]{1,0:T(8,128)(2,1)S(1)}, u32[]{:S(2)}, u32[]{:S(2)}) collective-permute-start(f16[256,1024]{1,0:T(8,128)(2,1)S(1)} %get-tuple-element.40), channel_id=1, source_target_pairs={{0,48},{1,17},{16,32},{17,1},{32,16},{33,49},{48,0},{49,33},{2,50}... | collective-permute-start | bytes 1572872 | tf_op jit(solution)/shard_map/ppermute | solution.py:24
  39.0 15.9 %collective-permute-start.9 = (f16[256,1024]{1,0:T(8,128)(2,1)S(1)}, f16[256,1024]{1,0:T(8,128)(2,1)S(1)}, u32[]{:S(2)}, u32[]{:S(2)}) collective-permute-start(f16[256,1024]{1,0:T(8,128)(2,1)S(1)} %get-tuple-element.43), channel_id=1, source_target_pairs={{0,12},{1,5},{4,8},{5,1},{8,4},{9,13},{12,0},{13,9},{2,14},{3,7},{... | collective-permute-start | bytes 1572872 | tf_op jit(solution)/shard_map/ppermute | solution.py:24
  40.2 14.7 %collective-permute-start.8 = (f16[256,1024]{1,0:T(8,128)(2,1)S(1)}, f16[256,1024]{1,0:T(8,128)(2,1)S(1)}, u32[]{:S(2)}, u32[]{:S(2)}) collective-permute-start(f16[256,1024]{1,0:T(8,128)(2,1)S(1)} %get-tuple-element.44), channel_id=1, source_target_pairs={{0,12},{1,5},{4,8},{5,1},{8,4},{9,13},{12,0},{13,9},{2,14},{3,7},{... | collective-permute-start | bytes 1572872 | tf_op jit(solution)/shard_map/ppermute | solution.py:24
  50.5 14.6 %collective-permute-start.19 = (f16[128,1024]{1,0:T(8,128)(2,1)S(1)}, f16[128,1024]{1,0:T(8,128)(2,1)S(1)}, u32[]{:S(2)}, u32[]{:S(2)}) collective-permute-start(f16[128,1024]{1,0:T(8,128)(2,1)S(1)} %fusion.4), channel_id=1, source_target_pairs={{0,12},{1,5},{4,8},{5,1},{8,4},{9,13},{12,0},{13,9},{2,14},{3,7},{... | collective-permute-start | bytes 786440 | tf_op jit(solution)/shard_map/ppermute | solution.py:24
  51.7 14.0 %collective-permute-start.17 = (f16[128,1024]{1,0:T(8,128)(2,1)S(1)}, f16[128,1024]{1,0:T(8,128)(2,1)}, u32[]{:S(2)}, u32[]{:S(2)}) collective-permute-start(f16[128,1024]{1,0:T(8,128)(2,1)S(1)} %get-tuple-element.45), channel_id=1, source_target_pairs={{0,8},{1,9},{4,12},{5,13},{8,0},{9,1},{12,4},{13,5},{2,10},{3,11},... | collective-permute-start | bytes 786440 | tf_op jit(solution)/shard_map/ppermute | solution.py:24
  53.8 11.9 %collective-permute-start.18 = (f16[128,1024]{1,0:T(8,128)(2,1)S(1)}, f16[128,1024]{1,0:T(8,128)(2,1)}, u32[]{:S(2)}, u32[]{:S(2)}) collective-permute-start(f16[128,1024]{1,0:T(8,128)(2,1)S(1)} %get-tuple-element.46), channel_id=1, source_target_pairs={{0,4},{1,13},{4,0},{5,9},{8,12},{9,5},{12,8},{13,1},{2,6},{3,15},{... | collective-permute-start | bytes 786440 | tf_op jit(solution)/shard_map/ppermute | solution.py:24
  55.3 15.3 %collective-permute-start.12 = (f16[128,1024]{1,0:T(8,128)(2,1)S(1)}, f16[128,1024]{1,0:T(8,128)(2,1)}, u32[]{:S(2)}, u32[]{:S(2)}) collective-permute-start(f16[128,1024]{1,0:T(8,128)(2,1)S(1)} %fusion.9), channel_id=1, source_target_pairs={{0,48},{1,17},{16,32},{17,1},{32,16},{33,49},{48,0},{49,33},{2,50}... | collective-permute-start | bytes 786440 | tf_op jit(solution)/shard_map/ppermute | solution.py:24
  58.5 12.1 %collective-permute-start.10 = (f16[128,1024]{1,0:T(8,128)(2,1)S(1)}, f16[128,1024]{1,0:T(8,128)(2,1)}, u32[]{:S(2)}, u32[]{:S(2)}) collective-permute-start(f16[128,1024]{1,0:T(8,128)(2,1)S(1)} %get-tuple-element.47), channel_id=1, source_target_pairs={{0,32},{1,33},{16,48},{17,49},{32,0},{33,1},{48,16},{49,17},{2,34}... | collective-permute-start | bytes 786440 | tf_op jit(solution)/shard_map/ppermute | solution.py:24
  74.2 13.3 %collective-permute-start.24 = (f16[128,256]{1,0:T(8,128)(2,1)S(1)}, f16[128,256]{1,0:T(8,128)(2,1)S(1)}, u32[]{:S(2)}, u32[]{:S(2)}) collective-permute-start(f16[128,256]{1,0:T(8,128)(2,1)S(1)} %get-tuple-element.57), channel_id=1, source_target_pairs={{0,3},{1,67},{2,1},{3,65},{64,2},{65,66},{66,0},{67,64},{128,131},... | collective-permute-start | bytes 196616 | tf_op jit(solution)/shard_map/ppermute | solution.py:189
  75.0 12.8 %collective-permute-start.25 = (f16[128,256]{1,0:T(8,128)(2,1)S(1)}, f16[128,256]{1,0:T(8,128)(2,1)S(1)}, u32[]{:S(2)}, u32[]{:S(2)}) collective-permute-start(f16[128,256]{1,0:T(8,128)(2,1)S(1)} %get-tuple-element.58), channel_id=1, source_target_pairs={{0,2},{1,66},{2,0},{3,64},{64,3},{65,67},{66,1},{67,65},{128,130},... | collective-permute-start | bytes 196616 | tf_op jit(solution)/shard_map/ppermute | solution.py:189
  76.4 11.7 %collective-permute-start.26 = (f16[128,256]{1,0:T(8,128)(2,1)S(1)}, f16[128,256]{1,0:T(8,128)(2,1)S(1)}, u32[]{:S(2)}, u32[]{:S(2)}) collective-permute-start(f16[128,256]{1,0:T(8,128)(2,1)S(1)} %get-tuple-element.59), channel_id=1, source_target_pairs={{0,1},{1,65},{2,3},{3,67},{64,0},{65,64},{66,2},{67,66},{128,129},... | collective-permute-start | bytes 196616 | tf_op jit(solution)/shard_map/ppermute | solution.py:189
  79.3 13.8 %collective-permute-start.27 = (f16[128,256]{1,0:T(8,128)(2,1)S(1)}, f16[128,256]{1,0:T(8,128)(2,1)S(1)}, u32[]{:S(2)}, u32[]{:S(2)}) collective-permute-start(f16[128,256]{1,0:T(8,128)(2,1)S(1)} %get-tuple-element.60), channel_id=1, source_target_pairs={{0,0},{1,64},{2,2},{3,66},{64,1},{65,65},{66,3},{67,67},{128,128},... | collective-permute-start | bytes 196616 | tf_op jit(solution)/shard_map/ppermute | solution.py:189
  80.1 13.0 %collective-permute-start.22 = (f16[128,256]{1,0:T(8,128)(2,1)S(1)}, f16[128,256]{1,0:T(8,128)(2,1)S(1)}, u32[]{:S(2)}, u32[]{:S(2)}) collective-permute-start(f16[128,256]{1,0:T(8,128)(2,1)S(1)} %get-tuple-element.55), channel_id=1, source_target_pairs={{0,129},{1,193},{2,131},{3,195},{64,128},{65,192},{66,130},{67,194... | collective-permute-start | bytes 196616 | tf_op jit(solution)/shard_map/ppermute | solution.py:189
  88.1 9.5 %collective-permute-start.21 = (f16[128,256]{1,0:T(8,128)(2,1)S(1)}, f16[128,256]{1,0:T(8,128)(2,1)S(1)}, u32[]{:S(2)}, u32[]{:S(2)}) collective-permute-start(f16[128,256]{1,0:T(8,128)(2,1)S(1)} %get-tuple-element.54), channel_id=1, source_target_pairs={{0,130},{1,194},{2,128},{3,192},{64,131},{65,195},{66,129},{67,193... | collective-permute-start | bytes 196616 | tf_op jit(solution)/shard_map/ppermute | solution.py:189
  102.1 9.6 %collective-permute-start.34 = (bf16[128,256]{1,0:T(8,128)(2,1)S(1)}, bf16[128,256]{1,0:T(8,128)(2,1)S(1)}, u32[]{:S(2)}, u32[]{:S(2)}) collective-permute-start(bf16[128,256]{1,0:T(8,128)(2,1)S(1)} %get-tuple-element.31), channel_id=1, source_target_pairs={{0,128},{64,192},{128,0},{192,64},{1,129},{65,193},{129,1},{193,65... | collective-permute-start | bytes 196616 | tf_op jit(solution)/shard_map/ppermute | solution.py:198
  105.7 12.0 %collective-permute-start.31 = (bf16[256,256]{1,0:T(8,128)(2,1)S(1)}, bf16[256,256]{1,0:T(8,128)(2,1)S(1)}, u32[]{:S(2)}, u32[]{:S(2)}) collective-permute-start(bf16[256,256]{1,0:T(8,128)(2,1)S(1)} %pad_maximum_fusion.3), channel_id=1, source_target_pairs={{0,32},{1,33},{16,48},{17,49},{32,0},{33,1},{48,16},{49,17},{2,34}... | collective-permute-start | bytes 393224 | tf_op jit(solution)/shard_map/ppermute | solution.py:24
  108.2 9.4 %collective-permute-start.30 = (bf16[256,256]{1,0:T(8,128)(2,1)S(1)}, bf16[256,256]{1,0:T(8,128)(2,1)S(1)}, u32[]{:S(2)}, u32[]{:S(2)}) collective-permute-start(bf16[256,256]{1,0:T(8,128)(2,1)S(1)} %pad_maximum_fusion.3), channel_id=1, source_target_pairs={{0,48},{1,17},{16,32},{17,1},{32,16},{33,49},{48,0},{49,33},{2,50}... | collective-permute-start | bytes 393224 | tf_op jit(solution)/shard_map/ppermute | solution.py:24
  112.0 9.8 %collective-permute-start.38 = (bf16[256,256]{1,0:T(8,128)(2,1)S(1)}, bf16[256,256]{1,0:T(8,128)(2,1)S(1)}, u32[]{:S(2)}, u32[]{:S(2)}) collective-permute-start(bf16[256,256]{1,0:T(8,128)(2,1)S(1)} %get-tuple-element.61), channel_id=1, source_target_pairs={{0,8},{1,9},{4,12},{5,13},{8,0},{9,1},{12,4},{13,5},{2,10},{3,11},... | collective-permute-start | bytes 393224 | tf_op jit(solution)/shard_map/ppermute | solution.py:24
  121.8 11.4 %collective-permute-start.39 = (bf16[1024,256]{1,0:T(8,128)(2,1)S(1)}, bf16[1024,256]{1,0:T(8,128)(2,1)S(1)}, u32[]{:S(2)}, u32[]{:S(2)}) collective-permute-start(bf16[1024,256]{1,0:T(8,128)(2,1)S(1)} %constant_dynamic-update-slice_fusion.7.refs_3_), channel_id=1, source_target_pairs={{0,16},{1,49},{16,0},{17,33},{32,48},{33,17},{48,32},{49,1},{2,18}... | collective-permute-start | bytes 1572872 | tf_op jit(solution)/shard_map/ppermute | solution.py:24
  121.9 17.0 %collective-permute-start.41 = (bf16[1024,256]{1,0:T(8,128)(2,1)S(1)}, bf16[1024,256]{1,0:T(8,128)(2,1)S(1)}, u32[]{:S(2)}, u32[]{:S(2)}) collective-permute-start(bf16[1024,256]{1,0:T(8,128)(2,1)S(1)} %constant_dynamic-update-slice_fusion.refs_0_), channel_id=1, source_target_pairs={{0,12},{1,5},{4,8},{5,1},{8,4},{9,13},{12,0},{13,9},{2,14},{3,7},{... | collective-permute-start | bytes 1572872 | tf_op jit(solution)/shard_map/ppermute | solution.py:24
  122.7 16.2 %collective-permute-start.42 = (bf16[1024,256]{1,0:T(8,128)(2,1)S(1)}, bf16[1024,256]{1,0:T(8,128)(2,1)S(1)}, u32[]{:S(2)}, u32[]{:S(2)}) collective-permute-start(bf16[1024,256]{1,0:T(8,128)(2,1)S(1)} %constant_dynamic-update-slice_fusion.7.refs_3_), channel_id=1, source_target_pairs={{0,48},{1,17},{16,32},{17,1},{32,16},{33,49},{48,0},{49,33},{2,50}... | collective-permute-start | bytes 1572872 | tf_op jit(solution)/shard_map/ppermute | solution.py:24
  126.9 14.2 %collective-permute-start.33 = (bf16[1024,256]{1,0:T(8,128)(2,1)S(1)}, bf16[1024,256]{1,0:T(8,128)(2,1)S(1)}, u32[]{:S(2)}, u32[]{:S(2)}) collective-permute-start(bf16[1024,256]{1,0:T(8,128)(2,1)S(1)} %collective-permute-done.32.refs_1_), channel_id=1, source_target_pairs={{0,12},{1,5},{4,8},{5,1},{8,4},{9,13},{12,0},{13,9},{2,14},{3,7},{... | collective-permute-start | bytes 1572872 | tf_op jit(solution)/shard_map/ppermute | solution.py:24
  133.3 12.8 %collective-permute-start.40 = (bf16[1024,256]{1,0:T(8,128)(2,1)S(1)}, bf16[1024,256]{1,0:T(8,128)(2,1)S(1)}, u32[]{:S(2)}, u32[]{:S(2)}) collective-permute-start(bf16[1024,256]{1,0:T(8,128)(2,1)S(1)} %collective-permute-done.39.refs_4_), channel_id=1, source_target_pairs={{0,48},{1,17},{16,32},{17,1},{32,16},{33,49},{48,0},{49,33},{2,50}... | collective-permute-start | bytes 1572872 | tf_op jit(solution)/shard_map/ppermute | solution.py:24
  (17 other events, 153.8 us)

commit v4 on v3

v4 whole, which is shorter than its diff:
```python
import math

import jax
import jax.numpy as jnp
from jax import lax
from jax.experimental import pallas as pl
from jax.experimental.pallas import tpu as pltpu
from jax.sharding import Mesh
from jax.sharding import PartitionSpec as P

first_bias = 1.0 - math.exp(100.0 * math.log(0.9))
second_bias = 1.0 - math.exp(100.0 * math.log(0.999))

F32, F16, BF16 = jnp.float32, jnp.float16, jnp.bfloat16
BLOCK = 128
VMEM = pltpu.CompilerParams(vmem_limit_bytes=32 * 2**20)

FIRST, SECOND = ("x", "y"), ("y", "x")
NEAR, NEXT = (1, 3), (3, 1)
GATHER_NEAR, GATHER_NEXT = NEAR, NEXT


def swap(array, axis, by):
    pairs = [(2 * i + c, 2 * (i ^ by[c]) + c) for i in range(4) for c in range(2)]
    return lax.ppermute(array, (axis, "c"), pairs)


def other_core(array):
    return lax.ppermute(array, "c", [(0, 1), (1, 0)])


def order(core):
    return 0, 3 - 2 * core, 1 + 2 * core, 2


def owner(part, first, second, x, y):
    x_by, y_by = (first, second) if part == 0 else (second, first)
    return lax.bitwise_xor(y, y_by) * 4 + lax.bitwise_xor(x, x_by)


def other_rows(acts, where):
    half = acts.shape[1] // 4

    def kernel(where_ref, acts_ref, out_ref, sem):
        copies = []
        for part in range(2):
            start = pl.multiple_of((2 * part + 1 - where_ref[3]) * half, half)
            copies.append(
                pltpu.make_async_copy(
                    acts_ref.at[:, pl.ds(start, half)],
                    out_ref.at[:, pl.ds(part * half, half)],
                    sem.at[part],
                )
            )
        for copy in copies:
            copy.start()
        for copy in copies:
            copy.wait()

    return pl.pallas_call(
        kernel,
        out_shape=jax.ShapeDtypeStruct((acts.shape[0], 2 * half), acts.dtype),
        in_specs=[
            pl.BlockSpec(memory_space=pltpu.SMEM),
            pl.BlockSpec(memory_space=pltpu.HBM),
        ],
        out_specs=pl.BlockSpec(memory_space=pltpu.VMEM),
        scratch_shapes=[pltpu.SemaphoreType.DMA((2,))],
        compiler_params=pltpu.CompilerParams(vmem_limit_bytes=58 * 2**20),
        cost_estimate=pl.CostEstimate(
            flops=0, bytes_accessed=2 * acts.size, transcendentals=0
        ),
    )(where, acts)


def arrange(acts, peer, where, index):
    tokens = acts.shape[0]

    def kernel(where_ref, acts_ref, peer_ref, *out_refs):
        x, y, core = where_ref[0], where_ref[1], where_ref[3]
        distances = order(core)
        for part in range(2):
            for j in range(4):
                out_ref, place = out_refs[part], slice(j * BLOCK, (j + 1) * BLOCK)
                block = owner(part, distances[index], distances[j], x, y)
                own = ((2 * part + core) * 16 + block) * BLOCK
                out_ref[:tokens, place] = acts_ref[:, pl.ds(pl.multiple_of(own, BLOCK), BLOCK)]
                other = (part * 16 + block) * BLOCK
                out_ref[tokens:, place] = peer_ref[:, pl.ds(pl.multiple_of(other, BLOCK), BLOCK)]

    out = jax.ShapeDtypeStruct((2 * tokens, 4 * BLOCK), acts.dtype)
    vmem = pl.BlockSpec(memory_space=pltpu.VMEM)
    return pl.pallas_call(
        kernel,
        out_shape=[out] * 2,
        in_specs=[pl.BlockSpec(memory_space=pltpu.SMEM), vmem, vmem],
        out_specs=[vmem] * 2,
        compiler_params=VMEM,
        cost_estimate=pl.CostEstimate(
            flops=0, bytes_accessed=8 * out.size, transcendentals=0
        ),
    )(where, acts, peer)


def place(pieces, where, parts, firsts, into=None):
    many = len(pieces)

    def kernel(where_ref, *refs):
        ins, out_ref, sem = refs[:many], refs[-2], refs[-1]
        x, y, zh, core = (where_ref[i] for i in range(4))
        distances = (0, GATHER_NEAR[0] + (GATHER_NEAR[1] - GATHER_NEAR[0]) * core, GATHER_NEXT[0] + (GATHER_NEXT[1] - GATHER_NEXT[0]) * core, 2)
        copies = []
        for index, part in enumerate(parts):
            for i, first in enumerate(firsts):
                for j in range(4):
                    for k in range(2):
                        block = lax.bitwise_xor(zh, distances[2 * part + k]) * 16
                        block += owner(part, distances[first], distances[j], x, y)
                        copies.append(
                            pltpu.make_async_copy(
                                ins[index * len(firsts) + i].at[pl.ds((j * 2 + k) * BLOCK, BLOCK), :],
                                out_ref.at[pl.ds(pl.multiple_of(block * BLOCK, BLOCK), BLOCK), :],
                                sem,
                            )
                        )
        for copy in copies:
            copy.start()
        for copy in copies:
            copy.wait()

    anywhere = pl.BlockSpec(memory_space=pl.ANY)
    return pl.pallas_call(
        kernel,
        out_shape=jax.ShapeDtypeStruct((8192, 256), BF16),
        in_specs=[pl.BlockSpec(memory_space=pltpu.SMEM)]
        + [pl.BlockSpec(memory_space=pltpu.VMEM)] * many
        + [anywhere] * (into is not None),
        out_specs=anywhere,
        scratch_shapes=[pltpu.SemaphoreType.DMA],
        input_output_aliases={} if into is None else {1 + many: 0},
        compiler_params=VMEM,
        cost_estimate=pl.CostEstimate(
            flops=0, bytes_accessed=many * 2**20, transcendentals=0
        ),
    )(where, *pieces, *(() if into is None else (into,)))


def dot(a, b):
    return lax.dot_general(a, b, (((0,), (0,)), ((), ())), preferred_element_type=F32)


def received(array, swapped, scale):
    return swapped((array * scale).astype(F16)).astype(F32) * (1.0 / scale)


def per_device(acts, grad_out, master, moment1, moment2):
    x, y, zh, zl, core = (lax.axis_index(name) for name in ("x", "y", "zh", "zl", "c"))
    where = jnp.stack([x, y, zh, core]).astype(jnp.int32)
    parts = range(2)

    peer_grad = other_core(grad_out)
    soon_where, peer_grad = lax.optimization_barrier((where, peer_grad))
    chip_grad = jnp.concatenate([grad_out, peer_grad], 0)
    peer = other_core(other_rows(acts, soon_where))

    far_grad = [swap(chip_grad, FIRST[p], NEAR) for p in parts]
    sent, rest = arrange(acts, peer, where, 3), arrange(acts, peer, where, 2)
    kept = [arrange(acts, peer, where, i) for i in range(2)]
    far = [swap(sent[p], FIRST[p], NEAR) for p in parts]
    far, far_grad, rest = lax.optimization_barrier((far, far_grad, rest))
    far_acts = [(swap(rest[p], FIRST[p], NEAR), far[p]) for p in parts]

    near_sums = [[dot(kept[i][p], chip_grad) for i in range(2)] for p in parts]
    near_sums = lax.optimization_barrier(near_sums)

    def partial(p, i):
        return near_sums[p][i] + dot(far_acts[p][i], far_grad[p])

    passed = [
        received(partial(p, 1), lambda v: swap(v, FIRST[p], NEXT), 64.0) for p in parts
    ]
    own = [partial(p, 0) for p in parts]
    upper, lower = [array[256:] for array in passed], [array[:256] for array in passed]
    level = []
    for p in parts:
        far = received(own[p][256:] + upper[p], lambda v: swap(v, SECOND[p], NEAR), 32.0)
        level.append(own[p][:256] + lower[p] + far)
    level = [
        level[p][:128] + received(level[p][128:], lambda v: swap(v, SECOND[p], NEXT), 16.0)
        for p in parts
    ]

    both = jnp.concatenate(level, 0)
    low, high = both[:, :512], both[:, 512:]
    stays, goes = jnp.where(zl == 0, low, high), jnp.where(zl == 0, high, low)

    def by_core(array):
        low, high = array[:, :256], array[:, 256:]
        return jnp.where(core == 0, low, high), jnp.where(core == 0, high, low)

    def along_z(cross):
        pairs = [
            (2 * z + c, 2 * (z ^ 1 if c == 0 else ((z + 1) ^ 1) - 1 & 7) + (c ^ cross))
            for z in range(8)
            for c in range(2)
        ]
        return lambda v: lax.ppermute(v, ("zh", "zl", "c"), pairs)

    straight, crossing = by_core(goes)
    mine, theirs = by_core(stays)
    mine = mine + received(straight, along_z(0), 8.0)
    theirs = other_core(theirs) + received(crossing, along_z(1), 8.0)
    even, odd = jnp.where(core == 0, mine, theirs), jnp.where(core == 0, theirs, mine)
    rows = jnp.concatenate([even[:128], odd[:128], even[128:], odd[128:]], 0)
    block = [
        lax.dynamic_slice_in_dim(rows, lax.bitwise_xor(zh, distance) * BLOCK, BLOCK)
        for distance in order(core)
    ]
    far = swap(jnp.concatenate(block[2:], 0), "zh", NEAR)
    grad = swap(block[1] + far[128:], "zh", NEXT) + (block[0] + far[:128])

    new_moment1 = 0.9 * moment1 + 0.1 * grad
    new_moment2 = 0.999 * moment2 + 0.001 * grad * grad
    update = new_moment1 / first_bias / (jnp.sqrt(new_moment2 / second_bias) + 1e-08)
    new_master = master - 0.01 * (update + 0.1 * master)

    own = new_master.astype(BF16)
    every = (GATHER_NEAR, GATHER_NEXT, (2, 2))
    z = [own] + [swap(own, "zh", by) for by in every]
    pieces = [jnp.concatenate(z[:2], 0), jnp.concatenate(z[2:], 0)]
    far = [swap(pieces[0], SECOND[0], by) for by in every]
    pieces[1], far[0] = lax.optimization_barrier((pieces[1], far[0]))
    pieces[0] = jnp.concatenate([pieces[0]] + far, 0)
    pieces[1] = jnp.concatenate([pieces[1]] + [swap(pieces[1], SECOND[1], by) for by in every], 0)
    near = [swap(pieces[p], FIRST[p], GATHER_NEAR) for p in parts]
    following = [swap(pieces[p], FIRST[p], GATHER_NEXT) for p in parts]
    last = [swap(near[p], FIRST[p], GATHER_NEXT) for p in parts]
    first = [array for p in parts for array in (pieces[p], near[p], following[p])]
    new_weights = place(first, where, parts, (0, 1, 2))
    for p in parts:
        new_weights = place([last[p]], where, (p,), (3,), new_weights)
    return (new_master, new_moment1, new_moment2, new_weights)


def solution(mesh):
    fine = Mesh(mesh.devices.reshape(4, 4, 4, 2, 2), ("zh", "y", "x", "zl", "c"))
    dp, tensor = ("zh", "y", "x"), ("zl", "c")
    tokens, state = P(dp + tensor, None), P(dp, tensor)
    return jax.shard_map(
        per_device,
        mesh=fine,
        in_specs=(tokens, tokens, state, state, state),
        out_specs=(state, state, state, P(None, tensor)),
        check_vma=False,
    )
```

time: 150 us -> 151 us (level); the launches traced: 148 us -> 150 us
  waiting for transfers between devices: 55.1 us -> 80.8 us
  starting transfers between devices: 69.8 us -> 46.5 us
  Pallas kernels: 7.66 us -> 12.2 us
  local copies, waits for them, and re-layouts: 3.25 us -> 0.24 us
    ppermute x11 -> x2, starting transfers between devices: 25.9 us -> 2.19 us  [along_z(): return lambda v: lax.ppermute(v, ('zh', 'zl', 'c'), pairs)]
    ppermute x30 -> x29, waiting for transfers between devices: 48.3 us -> 71.2 us  [swap(): return lax.ppermute(array, (axis, 'c'), pairs)]
    pallas_call x1, Pallas kernels: 0.68 us -> 4.07 us  [other_rows(): pl.pallas_call(kernel, out_shape=jax.ShapeDtypeStruct((acts.shape[0], 2 *...]
    ppermute x2 -> x3, waiting for transfers between devices: 0.01 us -> 3.27 us  [other_core(): return lax.ppermute(array, 'c', [(0, 1), (1, 0)])]
    unnamed x18 -> x19, local copies, waits for them, and re-layouts: 3.22 us -> 0.12 us
    select_n x2 -> x3, other arithmetic: 1.91 us -> 0.25 us  [the longest x1 0.14 us: per_device(): stays, goes = (jnp.where(zl == 0, low, high), jnp.where(zl == 0, high, low))]
    pallas_call x2 -> x3, Pallas kernels: 3.67 us -> 4.84 us  [place(): pl.pallas_call(kernel, out_shape=jax.ShapeDtypeStruct((8192, 256), BF16),...]
    ppermute x11 -> x2, waiting for transfers between devices: 6.87 us -> 6.35 us  [along_z(): return lambda v: lax.ppermute(v, ('zh', 'zl', 'c'), pairs)]
  transfers between devices with their start and end apart: 43 -> 34, of which waited for: 19 -> 24; matrix products, arithmetic and copies ran while one was open for 5% -> 6% of each run, Pallas kernels for 4% -> 5%
where the time goes in v4:
time: 151 us; the launch traced here: 150 us
  waiting for transfers between devices  80.8 us (54%)
  starting transfers between devices  46.5 us (31%)
  Pallas kernels  12.2 us (8%)
  matrix products  5.84 us (4%)
  other arithmetic  3.59 us (2%)
    ppermute x29, waiting for transfers between devices, swap(): return lax.ppermute(array, (axis, 'c'), pairs)  71.2 us
    ppermute x29, starting transfers between devices, swap(): return lax.ppermute(array, (axis, 'c'), pairs)  43.9 us
    ppermute x2, waiting for transfers between devices, along_z(): return lambda v: lax.ppermute(v, ('zh', 'zl', 'c'), pairs)  6.35 us
    dot_general x8, matrix products, dot(): lax.dot_general(a, b, (((0,), (0,)), ((), ())), preferred_element_type=F32)  5.84 us
    pallas_call x3, Pallas kernels, place(): pl.pallas_call(kernel, out_shape=jax.ShapeDtypeStruct((8192, 256), BF16),...  4.84 us
    pallas_call x1, Pallas kernels, other_rows(): pl.pallas_call(kernel, out_shape=jax.ShapeDtypeStruct((acts.shape[0], 2 *...  4.07 us
    pallas_call x4, Pallas kernels, arrange(): pl.pallas_call(kernel, out_shape=[out] * 2, in_specs=[pl.BlockSpec(memory...  3.31 us
    ppermute x3, waiting for transfers between devices, other_core(): return lax.ppermute(array, 'c', [(0, 1), (1, 0)])  3.27 us
  transfers between devices with their start and end apart: 34, of which 24 were waited for; matrix products, arithmetic and copies ran while one was open for 6% of the time, Pallas kernels for 5%

profile of v4, /device:TPU:2, one launch (start us, length us, event | category | flops | bytes accessed | tf_op | source)
XLA Modules:
  0.0 150.5 jit_solution(16270951782799386517)
XLA Ops:
  2.8 4.1 %shard_map.84 = bf16[256,4096]{1,0:T(8,128)(2,1)} custom-call(s32[4]{0:T(128)} %pad_add_fusion.where_ref, bf16[256,8192]{1,0:T(8,128)(2,1)} %acts_ref.9), custom_call_target="tpu_custom_call" | custom-call | bytes 4194304 | tf_op jit(solution)/shard_map/pallas_call | solution.py:60
  7.2 2.4 %collective-permute-start.4 = (bf16[512,1024]{1,0:T(8,128)(2,1)S(1)}, bf16[512,1024]{1,0:T(8,128)(2,1)S(1)}, u32[]{:S(2)}, u32[]{:S(2)}) collective-permute-start(bf16[512,1024]{1,0:T(8,128)(2,1)S(1)} %constant_dynamic-update-slice_fusion), channel_id=1, source_target_pairs={{0,4},{1,13},{4,0},{5,9},{8,12},{9,5},{12,8},{13,1},{2,6},{3,15},{... | collective-permute-start | bytes 3145736 | tf_op jit(solution)/shard_map/ppermute | solution.py:25
  12.2 2.4 %collective-permute-start.2 = (bf16[512,512]{1,0:T(8,128)(2,1)S(1)}, bf16[512,512]{1,0:T(8,128)(2,1)S(1)}, u32[]{:S(2)}, u32[]{:S(2)}) collective-permute-start(bf16[512,512]{1,0:T(8,128)(2,1)S(1)} %get-tuple-element.33), channel_id=1, source_target_pairs={{0,4},{1,13},{4,0},{5,9},{8,12},{9,5},{12,8},{13,1},{2,6},{3,15},{... | collective-permute-start | bytes 1572872 | tf_op jit(solution)/shard_map/ppermute | solution.py:25
  20.0 2.4 %collective-permute-done.4 = bf16[512,1024]{1,0:T(8,128)(2,1)S(1)} collective-permute-done((bf16[512,1024]{1,0:T(8,128)(2,1)S(1)}, bf16[512,1024]{1,0:T(8,128)(2,1)S(1)}, u32[]{:S(2)}, u32[]{:S(2)}) %collective-permute-start.4) | collective-permute-done | bytes 1048608 | tf_op jit(solution)/shard_map/ppermute | solution.py:25
  22.4 2.0 %collective-permute-done.5 = bf16[512,1024]{1,0:T(8,128)(2,1)S(1)} collective-permute-done((bf16[512,1024]{1,0:T(8,128)(2,1)S(1)}, bf16[512,1024]{1,0:T(8,128)(2,1)S(1)}, u32[]{:S(2)}, u32[]{:S(2)}) %collective-permute-start.5) | collective-permute-done | bytes 1048608 | tf_op jit(solution)/shard_map/ppermute | solution.py:25
  24.4 3.6 %collective-permute-done.2 = bf16[512,512]{1,0:T(8,128)(2,1)S(1)} collective-permute-done((bf16[512,512]{1,0:T(8,128)(2,1)S(1)}, bf16[512,512]{1,0:T(8,128)(2,1)S(1)}, u32[]{:S(2)}, u32[]{:S(2)}) %collective-permute-start.2) | collective-permute-done | bytes 524320 | tf_op jit(solution)/shard_map/ppermute | solution.py:25
  28.0 2.0 %collective-permute-done.3 = bf16[512,512]{1,0:T(8,128)(2,1)S(1)} collective-permute-done((bf16[512,512]{1,0:T(8,128)(2,1)S(1)}, bf16[512,512]{1,0:T(8,128)(2,1)S(1)}, u32[]{:S(2)}, u32[]{:S(2)}) %collective-permute-start.3) | collective-permute-done | bytes 524320 | tf_op jit(solution)/shard_map/ppermute | solution.py:25
  34.4 2.3 %collective-permute-start.11 = (f16[512,1024]{1,0:T(8,128)(2,1)S(1)}, f16[512,1024]{1,0:T(8,128)(2,1)S(1)}, u32[]{:S(2)}, u32[]{:S(2)}) collective-permute-start(f16[512,1024]{1,0:T(8,128)(2,1)S(1)} %multiply_convert_fusion), channel_id=1, source_target_pairs={{0,48},{1,17},{16,32},{17,1},{32,16},{33,49},{48,0},{49,33},{2,50}... | collective-permute-start | bytes 3145736 | tf_op jit(solution)/shard_map/ppermute | solution.py:25
  36.7 6.9 %collective-permute-done.6 = bf16[512,512]{1,0:T(8,128)(2,1)S(1)} collective-permute-done((bf16[512,512]{1,0:T(8,128)(2,1)S(1)}, bf16[512,512]{1,0:T(8,128)(2,1)S(1)}, u32[]{:S(2)}, u32[]{:S(2)}) %collective-permute-start.6) | collective-permute-done | bytes 524320 | tf_op jit(solution)/shard_map/ppermute | solution.py:25
  45.5 3.3 %collective-permute-done.7 = f16[512,1024]{1,0:T(8,128)(2,1)S(1)} collective-permute-done((f16[512,1024]{1,0:T(8,128)(2,1)S(1)}, f16[512,1024]{1,0:T(8,128)(2,1)S(1)}, u32[]{:S(2)}, u32[]{:S(2)}) %collective-permute-start.7) | collective-permute-done | bytes 1048608 | tf_op jit(solution)/shard_map/ppermute | solution.py:25
  50.3 4.1 %collective-permute-done.11 = f16[512,1024]{1,0:T(8,128)(2,1)S(1)} collective-permute-done((f16[512,1024]{1,0:T(8,128)(2,1)S(1)}, f16[512,1024]{1,0:T(8,128)(2,1)S(1)}, u32[]{:S(2)}, u32[]{:S(2)}) %collective-permute-start.11) | collective-permute-done | bytes 1048608 | tf_op jit(solution)/shard_map/ppermute | solution.py:25
  55.3 3.5 %collective-permute-done.8 = f16[256,1024]{1,0:T(8,128)(2,1)S(1)} collective-permute-done((f16[256,1024]{1,0:T(8,128)(2,1)S(1)}, f16[256,1024]{1,0:T(8,128)(2,1)S(1)}, u32[]{:S(2)}, u32[]{:S(2)}) %collective-permute-start.8) | collective-permute-done | bytes 524320 | tf_op jit(solution)/shard_map/ppermute | solution.py:25
  59.2 3.0 %collective-permute-start.9 = (f16[128,1024]{1,0:T(8,128)(2,1)S(1)}, f16[128,1024]{1,0:T(8,128)(2,1)S(1)}, u32[]{:S(2)}, u32[]{:S(2)}) collective-permute-start(f16[128,1024]{1,0:T(8,128)(2,1)S(1)} %fusion.8), channel_id=1, source_target_pairs={{0,48},{1,17},{16,32},{17,1},{32,16},{33,49},{48,0},{49,33},{2,50}... | collective-permute-start | bytes 786440 | tf_op jit(solution)/shard_map/ppermute | solution.py:25
  62.2 1.9 %collective-permute-done.12 = f16[256,1024]{1,0:T(8,128)(2,1)S(1)} collective-permute-done((f16[256,1024]{1,0:T(8,128)(2,1)S(1)}, f16[256,1024]{1,0:T(8,128)(2,1)S(1)}, u32[]{:S(2)}, u32[]{:S(2)}) %collective-permute-start.12) | collective-permute-done | bytes 524320 | tf_op jit(solution)/shard_map/ppermute | solution.py:25
  66.9 4.0 %collective-permute-done.13 = f16[128,1024]{1,0:T(8,128)(2,1)S(1)} collective-permute-done((f16[128,1024]{1,0:T(8,128)(2,1)S(1)}, f16[128,1024]{1,0:T(8,128)(2,1)S(1)}, u32[]{:S(2)}, u32[]{:S(2)}) %collective-permute-start.13) | collective-permute-done | bytes 262176 | tf_op jit(solution)/shard_map/ppermute | solution.py:25
  73.5 2.9 %collective-permute-done.14 = f16[256,256]{1,0:T(8,128)(2,1)S(1)} collective-permute-done((f16[256,256]{1,0:T(8,128)(2,1)S(1)}, f16[256,256]{1,0:T(8,128)(2,1)S(1)}, u32[]{:S(2)}, u32[]{:S(2)}) %collective-permute-start.14) | collective-permute-done | bytes 131104 | tf_op jit(solution)/shard_map/ppermute | solution.py:207
  76.4 3.5 %collective-permute-done.16 = f16[256,256]{1,0:T(8,128)(2,1)S(1)} collective-permute-done((f16[256,256]{1,0:T(8,128)(2,1)S(1)}, f16[256,256]{1,0:T(8,128)(2,1)S(1)}, u32[]{:S(2)}, u32[]{:S(2)}) %collective-permute-start.16) | collective-permute-done | bytes 131104 | tf_op jit(solution)/shard_map/ppermute | solution.py:207
  80.9 9.0 %collective-permute-done.17 = f32[256,256]{1,0:T(8,128)S(1)} collective-permute-done((f32[256,256]{1,0:T(8,128)S(1)}, f32[256,256]{1,0:T(8,128)S(1)}, u32[]{:S(2)}, u32[]{:S(2)}) %collective-permute-start.17) | collective-permute-done | bytes 262176 | tf_op jit(solution)/shard_map/ppermute | solution.py:25
  89.9 2.7 %collective-permute-start.18 = (f32[128,256]{1,0:T(8,128)S(1)}, f32[128,256]{1,0:T(8,128)S(1)}, u32[]{:S(2)}, u32[]{:S(2)}) collective-permute-start(f32[128,256]{1,0:T(8,128)S(1)} %slice_add_fusion.7), channel_id=1, source_target_pairs={{0,192},{1,65},{64,128},{65,1},{128,64},{129,193},{192,0},{193,129... | collective-permute-start | bytes 393224 | tf_op jit(solution)/shard_map/ppermute | solution.py:25
  92.6 5.8 %collective-permute-done.18 = f32[128,256]{1,0:T(8,128)S(1)} collective-permute-done((f32[128,256]{1,0:T(8,128)S(1)}, f32[128,256]{1,0:T(8,128)S(1)}, u32[]{:S(2)}, u32[]{:S(2)}) %collective-permute-start.18) | collective-permute-done | bytes 131104 | tf_op jit(solution)/shard_map/ppermute | solution.py:25
  99.9 2.5 %collective-permute-start.19 = (bf16[128,256]{1,0:T(8,128)(2,1)S(1)}, bf16[128,256]{1,0:T(8,128)(2,1)S(1)}, u32[]{:S(2)}, u32[]{:S(2)}) collective-permute-start(bf16[128,256]{1,0:T(8,128)(2,1)S(1)} %get-tuple-element.49), channel_id=1, source_target_pairs={{0,192},{1,65},{64,128},{65,1},{128,64},{129,193},{192,0},{193,129... | collective-permute-start | bytes 196616 | tf_op jit(solution)/shard_map/ppermute | solution.py:25
  102.4 3.4 %collective-permute-start.20 = (bf16[128,256]{1,0:T(8,128)(2,1)S(1)}, bf16[128,256]{1,0:T(8,128)(2,1)S(1)}, u32[]{:S(2)}, u32[]{:S(2)}) collective-permute-start(bf16[128,256]{1,0:T(8,128)(2,1)S(1)} %get-tuple-element.49), channel_id=1, source_target_pairs={{0,128},{1,129},{64,192},{65,193},{128,0},{129,1},{192,64},{193,65... | collective-permute-start | bytes 196616 | tf_op jit(solution)/shard_map/ppermute | solution.py:25
  106.0 2.9 %collective-permute-start.28 = (bf16[256,256]{1,0:T(8,128)(2,1)S(1)}, bf16[256,256]{1,0:T(8,128)(2,1)S(1)}, u32[]{:S(2)}, u32[]{:S(2)}) collective-permute-start(bf16[256,256]{1,0:T(8,128)(2,1)S(1)} %pad_maximum_fusion.4), channel_id=1, source_target_pairs={{0,48},{1,17},{16,32},{17,1},{32,16},{33,49},{48,0},{49,33},{2,50}... | collective-permute-start | bytes 393224 | tf_op jit(solution)/shard_map/ppermute | solution.py:25
  112.2 2.6 %collective-permute-start.23 = (bf16[256,256]{1,0:T(8,128)(2,1)S(1)}, bf16[256,256]{1,0:T(8,128)(2,1)S(1)}, u32[]{:S(2)}, u32[]{:S(2)}) collective-permute-start(bf16[256,256]{1,0:T(8,128)(2,1)S(1)} %pad_maximum_fusion.3), channel_id=1, source_target_pairs={{0,4},{1,13},{4,0},{5,9},{8,12},{9,5},{12,8},{13,1},{2,6},{3,15},{... | collective-permute-start | bytes 393224 | tf_op jit(solution)/shard_map/ppermute | solution.py:25
  117.1 2.0 %collective-permute-start.30 = (bf16[1024,256]{1,0:T(8,128)(2,1)S(1)}, bf16[1024,256]{1,0:T(8,128)(2,1)S(1)}, u32[]{:S(2)}, u32[]{:S(2)}) collective-permute-start(bf16[1024,256]{1,0:T(8,128)(2,1)S(1)} %constant_dynamic-update-slice_fusion.6.refs_0_), channel_id=1, source_target_pairs={{0,4},{1,13},{4,0},{5,9},{8,12},{9,5},{12,8},{13,1},{2,6},{3,15},{... | collective-permute-start | bytes 1572872 | tf_op jit(solution)/shard_map/ppermute | solution.py:25
  119.1 4.2 %collective-permute-done.24 = bf16[256,256]{1,0:T(8,128)(2,1)S(1)} collective-permute-done((bf16[256,256]{1,0:T(8,128)(2,1)S(1)}, bf16[256,256]{1,0:T(8,128)(2,1)S(1)}, u32[]{:S(2)}, u32[]{:S(2)}) %collective-permute-start.24) | collective-permute-done | bytes 131104 | tf_op jit(solution)/shard_map/ppermute | solution.py:25
  125.6 2.1 %collective-permute-start.33 = (bf16[1024,256]{1,0:T(8,128)(2,1)S(1)}, bf16[1024,256]{1,0:T(8,128)(2,1)S(1)}, u32[]{:S(2)}, u32[]{:S(2)}) collective-permute-start(bf16[1024,256]{1,0:T(8,128)(2,1)S(1)} %constant_dynamic-update-slice_fusion.2.refs_3_), channel_id=1, source_target_pairs={{0,48},{1,17},{16,32},{17,1},{32,16},{33,49},{48,0},{49,33},{2,50}... | collective-permute-start | bytes 1572872 | tf_op jit(solution)/shard_map/ppermute | solution.py:25
  127.7 3.0 %collective-permute-done.30.refs_1_ = bf16[1024,256]{1,0:T(8,128)(2,1)S(1)} collective-permute-done((bf16[1024,256]{1,0:T(8,128)(2,1)S(1)}, bf16[1024,256]{1,0:T(8,128)(2,1)S(1)}, u32[]{:S(2)}, u32[]{:S(2)}) %collective-permute-start.30) | collective-permute-done | bytes 524320 | tf_op jit(solution)/shard_map/ppermute | solution.py:25
  131.9 6.7 %collective-permute-done.26.refs_4_ = bf16[1024,256]{1,0:T(8,128)(2,1)S(1)} collective-permute-done((bf16[1024,256]{1,0:T(8,128)(2,1)S(1)}, bf16[1024,256]{1,0:T(8,128)(2,1)S(1)}, u32[]{:S(2)}, u32[]{:S(2)}) %collective-permute-start.26) | collective-permute-done | bytes 524320 | tf_op jit(solution)/shard_map/ppermute | solution.py:25
  138.6 2.4 %collective-permute-start.27 = (bf16[1024,256]{1,0:T(8,128)(2,1)S(1)}, bf16[1024,256]{1,0:T(8,128)(2,1)S(1)}, u32[]{:S(2)}, u32[]{:S(2)}) collective-permute-start(bf16[1024,256]{1,0:T(8,128)(2,1)S(1)} %collective-permute-done.26.refs_4_), channel_id=1, source_target_pairs={{0,48},{1,17},{16,32},{17,1},{32,16},{33,49},{48,0},{49,33},{2,50}... | collective-permute-start | bytes 1572872 | tf_op jit(solution)/shard_map/ppermute | solution.py:25
  140.9 2.2 %shard_map.89.refs_1_ = bf16[8192,256]{1,0:T(8,128)(2,1)} custom-call(s32[4]{0:T(128)S(1)} %copy-done.1, bf16[1024,256]{1,0:T(8,128)(2,1)S(1)} %constant_dynamic-update-slice_fusion.6.refs_0_, bf16[1024,256]{1,0:T(8,128)(2,1)S(1)} %collective-permute-done.30.refs_1_, bf16[1024,256]{1,0:T(8,128)(2,1)S(1)} %collective-permute-done.32.refs_2_, ...), custom_call_target="tpu_custom_call" | custom-call | bytes 6291456 | tf_op jit(solution)/shard_map/pallas_call | solution.py:132
  144.5 4.5 %collective-permute-done.27.refs_0_ = bf16[1024,256]{1,0:T(8,128)(2,1)S(1)} collective-permute-done((bf16[1024,256]{1,0:T(8,128)(2,1)S(1)}, bf16[1024,256]{1,0:T(8,128)(2,1)S(1)}, u32[]{:S(2)}, u32[]{:S(2)}) %collective-permute-start.27) | collective-permute-done | bytes 524320 | tf_op jit(solution)/shard_map/ppermute | solution.py:25
  (97 shorter events, 39.1 us)
Async XLA Ops:
  7.2 15.1 %collective-permute-start.4 = (bf16[512,1024]{1,0:T(8,128)(2,1)S(1)}, bf16[512,1024]{1,0:T(8,128)(2,1)S(1)}, u32[]{:S(2)}, u32[]{:S(2)}) collective-permute-start(bf16[512,1024]{1,0:T(8,128)(2,1)S(1)} %constant_dynamic-update-slice_fusion), channel_id=1, source_target_pairs={{0,4},{1,13},{4,0},{5,9},{8,12},{9,5},{12,8},{13,1},{2,6},{3,15},{... | collective-permute-start | bytes 3145736 | tf_op jit(solution)/shard_map/ppermute | solution.py:25
  9.6 14.8 %collective-permute-start.5 = (bf16[512,1024]{1,0:T(8,128)(2,1)S(1)}, bf16[512,1024]{1,0:T(8,128)(2,1)S(1)}, u32[]{:S(2)}, u32[]{:S(2)}) collective-permute-start(bf16[512,1024]{1,0:T(8,128)(2,1)S(1)} %constant_dynamic-update-slice_fusion), channel_id=1, source_target_pairs={{0,16},{1,49},{16,0},{17,33},{32,48},{33,17},{48,32},{49,1},{2,18}... | collective-permute-start | bytes 3145736 | tf_op jit(solution)/shard_map/ppermute | solution.py:25
  12.2 15.8 %collective-permute-start.2 = (bf16[512,512]{1,0:T(8,128)(2,1)S(1)}, bf16[512,512]{1,0:T(8,128)(2,1)S(1)}, u32[]{:S(2)}, u32[]{:S(2)}) collective-permute-start(bf16[512,512]{1,0:T(8,128)(2,1)S(1)} %get-tuple-element.33), channel_id=1, source_target_pairs={{0,4},{1,13},{4,0},{5,9},{8,12},{9,5},{12,8},{13,1},{2,6},{3,15},{... | collective-permute-start | bytes 1572872 | tf_op jit(solution)/shard_map/ppermute | solution.py:25
  14.6 15.4 %collective-permute-start.3 = (bf16[512,512]{1,0:T(8,128)(2,1)S(1)}, bf16[512,512]{1,0:T(8,128)(2,1)S(1)}, u32[]{:S(2)}, u32[]{:S(2)}) collective-permute-start(bf16[512,512]{1,0:T(8,128)(2,1)S(1)} %get-tuple-element.34), channel_id=1, source_target_pairs={{0,16},{1,49},{16,0},{17,33},{32,48},{33,17},{48,32},{49,1},{2,18}... | collective-permute-start | bytes 1572872 | tf_op jit(solution)/shard_map/ppermute | solution.py:25
  30.0 13.5 %collective-permute-start.6 = (bf16[512,512]{1,0:T(8,128)(2,1)S(1)}, bf16[512,512]{1,0:T(8,128)(2,1)S(1)}, u32[]{:S(2)}, u32[]{:S(2)}) collective-permute-start(bf16[512,512]{1,0:T(8,128)(2,1)S(1)} %get-tuple-element.37), channel_id=1, source_target_pairs={{0,4},{1,13},{4,0},{5,9},{8,12},{9,5},{12,8},{13,1},{2,6},{3,15},{... | collective-permute-start | bytes 1572872 | tf_op jit(solution)/shard_map/ppermute | solution.py:25
  30.9 18.0 %collective-permute-start.7 = (f16[512,1024]{1,0:T(8,128)(2,1)S(1)}, f16[512,1024]{1,0:T(8,128)(2,1)S(1)}, u32[]{:S(2)}, u32[]{:S(2)}) collective-permute-start(f16[512,1024]{1,0:T(8,128)(2,1)S(1)} %multiply_convert_fusion.1), channel_id=1, source_target_pairs={{0,12},{1,5},{4,8},{5,1},{8,4},{9,13},{12,0},{13,9},{2,14},{3,7},{... | collective-permute-start | bytes 3145736 | tf_op jit(solution)/shard_map/ppermute | solution.py:25
  32.1 12.7 %collective-permute-start.10 = (bf16[512,512]{1,0:T(8,128)(2,1)S(1)}, bf16[512,512]{1,0:T(8,128)(2,1)S(1)}, u32[]{:S(2)}, u32[]{:S(2)}) collective-permute-start(bf16[512,512]{1,0:T(8,128)(2,1)S(1)} %get-tuple-element.42), channel_id=1, source_target_pairs={{0,16},{1,49},{16,0},{17,33},{32,48},{33,17},{48,32},{49,1},{2,18}... | collective-permute-start | bytes 1572872 | tf_op jit(solution)/shard_map/ppermute | solution.py:25
  34.4 19.9 %collective-permute-start.11 = (f16[512,1024]{1,0:T(8,128)(2,1)S(1)}, f16[512,1024]{1,0:T(8,128)(2,1)S(1)}, u32[]{:S(2)}, u32[]{:S(2)}) collective-permute-start(f16[512,1024]{1,0:T(8,128)(2,1)S(1)} %multiply_convert_fusion), channel_id=1, source_target_pairs={{0,48},{1,17},{16,32},{17,1},{32,16},{33,49},{48,0},{49,33},{2,50}... | collective-permute-start | bytes 3145736 | tf_op jit(solution)/shard_map/ppermute | solution.py:25
  49.4 9.4 %collective-permute-start.8 = (f16[256,1024]{1,0:T(8,128)(2,1)S(1)}, f16[256,1024]{1,0:T(8,128)(2,1)S(1)}, u32[]{:S(2)}, u32[]{:S(2)}) collective-permute-start(f16[256,1024]{1,0:T(8,128)(2,1)S(1)} %fusion.4), channel_id=1, source_target_pairs={{0,16},{1,49},{16,0},{17,33},{32,48},{33,17},{48,32},{49,1},{2,18}... | collective-permute-start | bytes 1572872 | tf_op jit(solution)/shard_map/ppermute | solution.py:25
  54.8 9.3 %collective-permute-start.12 = (f16[256,1024]{1,0:T(8,128)(2,1)S(1)}, f16[256,1024]{1,0:T(8,128)(2,1)S(1)}, u32[]{:S(2)}, u32[]{:S(2)}) collective-permute-start(f16[256,1024]{1,0:T(8,128)(2,1)S(1)} %fusion.1), channel_id=1, source_target_pairs={{0,4},{1,13},{4,0},{5,9},{8,12},{9,5},{12,8},{13,1},{2,6},{3,15},{... | collective-permute-start | bytes 1572872 | tf_op jit(solution)/shard_map/ppermute | solution.py:25
  59.2 7.7 %collective-permute-start.9 = (f16[128,1024]{1,0:T(8,128)(2,1)S(1)}, f16[128,1024]{1,0:T(8,128)(2,1)S(1)}, u32[]{:S(2)}, u32[]{:S(2)}) collective-permute-start(f16[128,1024]{1,0:T(8,128)(2,1)S(1)} %fusion.8), channel_id=1, source_target_pairs={{0,48},{1,17},{16,32},{17,1},{32,16},{33,49},{48,0},{49,33},{2,50}... | collective-permute-start | bytes 786440 | tf_op jit(solution)/shard_map/ppermute | solution.py:25
  64.4 6.5 %collective-permute-start.13 = (f16[128,1024]{1,0:T(8,128)(2,1)S(1)}, f16[128,1024]{1,0:T(8,128)(2,1)S(1)}, u32[]{:S(2)}, u32[]{:S(2)}) collective-permute-start(f16[128,1024]{1,0:T(8,128)(2,1)S(1)} %fusion.7), channel_id=1, source_target_pairs={{0,12},{1,5},{4,8},{5,1},{8,4},{9,13},{12,0},{13,9},{2,14},{3,7},{... | collective-permute-start | bytes 786440 | tf_op jit(solution)/shard_map/ppermute | solution.py:25
  71.1 8.7 %collective-permute-start.15 = (f32[256,256]{1,0:T(8,128)S(1)}, f32[256,256]{1,0:T(8,128)S(1)}, u32[]{:S(2)}, u32[]{:S(2)}) collective-permute-start(f32[256,256]{1,0:T(8,128)S(1)} %slice_select_fusion), channel_id=1, source_target_pairs={{0,1},{1,0},{2,3},{3,2},{4,5},{5,4},{6,7},{7,6},{8,9},{9,8},{10,11... | collective-permute-start | bytes 786440 | tf_op jit(solution)/shard_map/ppermute | solution.py:29
  71.3 5.1 %collective-permute-start.14 = (f16[256,256]{1,0:T(8,128)(2,1)S(1)}, f16[256,256]{1,0:T(8,128)(2,1)S(1)}, u32[]{:S(2)}, u32[]{:S(2)}) collective-permute-start(f16[256,256]{1,0:T(8,128)(2,1)S(1)} %get-tuple-element.59), channel_id=1, source_target_pairs={{0,2},{1,195},{2,0},{3,65},{64,66},{65,3},{66,64},{67,129},{128,13... | collective-permute-start | bytes 393224 | tf_op jit(solution)/shard_map/ppermute | solution.py:207
  71.8 8.1 %collective-permute-start.16 = (f16[256,256]{1,0:T(8,128)(2,1)S(1)}, f16[256,256]{1,0:T(8,128)(2,1)S(1)}, u32[]{:S(2)}, u32[]{:S(2)}) collective-permute-start(f16[256,256]{1,0:T(8,128)(2,1)S(1)} %get-tuple-element.60), channel_id=1, source_target_pairs={{0,3},{1,194},{2,1},{3,64},{64,67},{65,2},{66,65},{67,128},{128,13... | collective-permute-start | bytes 393224 | tf_op jit(solution)/shard_map/ppermute | solution.py:207
  80.1 9.7 %collective-permute-start.17 = (f32[256,256]{1,0:T(8,128)S(1)}, f32[256,256]{1,0:T(8,128)S(1)}, u32[]{:S(2)}, u32[]{:S(2)}) collective-permute-start(f32[256,256]{1,0:T(8,128)S(1)} %pad_maximum_fusion.2), channel_id=1, source_target_pairs={{0,64},{1,193},{64,0},{65,129},{128,192},{129,65},{192,128},{193,1... | collective-permute-start | bytes 786440 | tf_op jit(solution)/shard_map/ppermute | solution.py:25
  89.9 8.6 %collective-permute-start.18 = (f32[128,256]{1,0:T(8,128)S(1)}, f32[128,256]{1,0:T(8,128)S(1)}, u32[]{:S(2)}, u32[]{:S(2)}) collective-permute-start(f32[128,256]{1,0:T(8,128)S(1)} %slice_add_fusion.7), channel_id=1, source_target_pairs={{0,192},{1,65},{64,128},{65,1},{128,64},{129,193},{192,0},{193,129... | collective-permute-start | bytes 393224 | tf_op jit(solution)/shard_map/ppermute | solution.py:25
  99.3 6.5 %collective-permute-start.21 = (bf16[128,256]{1,0:T(8,128)(2,1)S(1)}, bf16[128,256]{1,0:T(8,128)(2,1)S(1)}, u32[]{:S(2)}, u32[]{:S(2)}) collective-permute-start(bf16[128,256]{1,0:T(8,128)(2,1)S(1)} %get-tuple-element.49), channel_id=1, source_target_pairs={{0,64},{1,193},{64,0},{65,129},{128,192},{129,65},{192,128},{193,1... | collective-permute-start | bytes 196616 | tf_op jit(solution)/shard_map/ppermute | solution.py:25
  99.9 10.4 %collective-permute-start.19 = (bf16[128,256]{1,0:T(8,128)(2,1)S(1)}, bf16[128,256]{1,0:T(8,128)(2,1)S(1)}, u32[]{:S(2)}, u32[]{:S(2)}) collective-permute-start(bf16[128,256]{1,0:T(8,128)(2,1)S(1)} %get-tuple-element.49), channel_id=1, source_target_pairs={{0,192},{1,65},{64,128},{65,1},{128,64},{129,193},{192,0},{193,129... | collective-permute-start | bytes 196616 | tf_op jit(solution)/shard_map/ppermute | solution.py:25
  102.4 8.3 %collective-permute-start.20 = (bf16[128,256]{1,0:T(8,128)(2,1)S(1)}, bf16[128,256]{1,0:T(8,128)(2,1)S(1)}, u32[]{:S(2)}, u32[]{:S(2)}) collective-permute-start(bf16[128,256]{1,0:T(8,128)(2,1)S(1)} %get-tuple-element.49), channel_id=1, source_target_pairs={{0,128},{1,129},{64,192},{65,193},{128,0},{129,1},{192,64},{193,65... | collective-permute-start | bytes 196616 | tf_op jit(solution)/shard_map/ppermute | solution.py:25
  105.8 6.4 %collective-permute-start.22 = (bf16[256,256]{1,0:T(8,128)(2,1)S(1)}, bf16[256,256]{1,0:T(8,128)(2,1)S(1)}, u32[]{:S(2)}, u32[]{:S(2)}) collective-permute-start(bf16[256,256]{1,0:T(8,128)(2,1)S(1)} %pad_maximum_fusion.4), channel_id=1, source_target_pairs={{0,16},{1,49},{16,0},{17,33},{32,48},{33,17},{48,32},{49,1},{2,18}... | collective-permute-start | bytes 393224 | tf_op jit(solution)/shard_map/ppermute | solution.py:25
  106.0 11.0 %collective-permute-start.28 = (bf16[256,256]{1,0:T(8,128)(2,1)S(1)}, bf16[256,256]{1,0:T(8,128)(2,1)S(1)}, u32[]{:S(2)}, u32[]{:S(2)}) collective-permute-start(bf16[256,256]{1,0:T(8,128)(2,1)S(1)} %pad_maximum_fusion.4), channel_id=1, source_target_pairs={{0,48},{1,17},{16,32},{17,1},{32,16},{33,49},{48,0},{49,33},{2,50}... | collective-permute-start | bytes 393224 | tf_op jit(solution)/shard_map/ppermute | solution.py:25
  108.9 8.1 %collective-permute-start.29 = (bf16[256,256]{1,0:T(8,128)(2,1)S(1)}, bf16[256,256]{1,0:T(8,128)(2,1)S(1)}, u32[]{:S(2)}, u32[]{:S(2)}) collective-permute-start(bf16[256,256]{1,0:T(8,128)(2,1)S(1)} %pad_maximum_fusion.4), channel_id=1, source_target_pairs={{0,32},{1,33},{16,48},{17,49},{32,0},{33,1},{48,16},{49,17},{2,34}... | collective-permute-start | bytes 393224 | tf_op jit(solution)/shard_map/ppermute | solution.py:25
  112.2 6.9 %collective-permute-start.23 = (bf16[256,256]{1,0:T(8,128)(2,1)S(1)}, bf16[256,256]{1,0:T(8,128)(2,1)S(1)}, u32[]{:S(2)}, u32[]{:S(2)}) collective-permute-start(bf16[256,256]{1,0:T(8,128)(2,1)S(1)} %pad_maximum_fusion.3), channel_id=1, source_target_pairs={{0,4},{1,13},{4,0},{5,9},{8,12},{9,5},{12,8},{13,1},{2,6},{3,15},{... | collective-permute-start | bytes 393224 | tf_op jit(solution)/shard_map/ppermute | solution.py:25
  114.8 8.5 %collective-permute-start.24 = (bf16[256,256]{1,0:T(8,128)(2,1)S(1)}, bf16[256,256]{1,0:T(8,128)(2,1)S(1)}, u32[]{:S(2)}, u32[]{:S(2)}) collective-permute-start(bf16[256,256]{1,0:T(8,128)(2,1)S(1)} %pad_maximum_fusion.3), channel_id=1, source_target_pairs={{0,12},{1,5},{4,8},{5,1},{8,4},{9,13},{12,0},{13,9},{2,14},{3,7},{... | collective-permute-start | bytes 393224 | tf_op jit(solution)/shard_map/ppermute | solution.py:25
  116.1 7.3 %collective-permute-start.25 = (bf16[256,256]{1,0:T(8,128)(2,1)S(1)}, bf16[256,256]{1,0:T(8,128)(2,1)S(1)}, u32[]{:S(2)}, u32[]{:S(2)}) collective-permute-start(bf16[256,256]{1,0:T(8,128)(2,1)S(1)} %pad_maximum_fusion.3), channel_id=1, source_target_pairs={{0,8},{1,9},{4,12},{5,13},{8,0},{9,1},{12,4},{13,5},{2,10},{3,11},... | collective-permute-start | bytes 393224 | tf_op jit(solution)/shard_map/ppermute | solution.py:25
  117.1 13.6 %collective-permute-start.30 = (bf16[1024,256]{1,0:T(8,128)(2,1)S(1)}, bf16[1024,256]{1,0:T(8,128)(2,1)S(1)}, u32[]{:S(2)}, u32[]{:S(2)}) collective-permute-start(bf16[1024,256]{1,0:T(8,128)(2,1)S(1)} %constant_dynamic-update-slice_fusion.6.refs_0_), channel_id=1, source_target_pairs={{0,4},{1,13},{4,0},{5,9},{8,12},{9,5},{12,8},{13,1},{2,6},{3,15},{... | collective-permute-start | bytes 1572872 | tf_op jit(solution)/shard_map/ppermute | solution.py:25
  123.4 15.2 %collective-permute-start.26 = (bf16[1024,256]{1,0:T(8,128)(2,1)S(1)}, bf16[1024,256]{1,0:T(8,128)(2,1)S(1)}, u32[]{:S(2)}, u32[]{:S(2)}) collective-permute-start(bf16[1024,256]{1,0:T(8,128)(2,1)S(1)} %constant_dynamic-update-slice_fusion.2.refs_3_), channel_id=1, source_target_pairs={{0,16},{1,49},{16,0},{17,33},{32,48},{33,17},{48,32},{49,1},{2,18}... | collective-permute-start | bytes 1572872 | tf_op jit(solution)/shard_map/ppermute | solution.py:25
  124.0 17.0 %collective-permute-start.32 = (bf16[1024,256]{1,0:T(8,128)(2,1)S(1)}, bf16[1024,256]{1,0:T(8,128)(2,1)S(1)}, u32[]{:S(2)}, u32[]{:S(2)}) collective-permute-start(bf16[1024,256]{1,0:T(8,128)(2,1)S(1)} %constant_dynamic-update-slice_fusion.6.refs_0_), channel_id=1, source_target_pairs={{0,12},{1,5},{4,8},{5,1},{8,4},{9,13},{12,0},{13,9},{2,14},{3,7},{... | collective-permute-start | bytes 1572872 | tf_op jit(solution)/shard_map/ppermute | solution.py:25
  125.6 15.3 %collective-permute-start.33 = (bf16[1024,256]{1,0:T(8,128)(2,1)S(1)}, bf16[1024,256]{1,0:T(8,128)(2,1)S(1)}, u32[]{:S(2)}, u32[]{:S(2)}) collective-permute-start(bf16[1024,256]{1,0:T(8,128)(2,1)S(1)} %constant_dynamic-update-slice_fusion.2.refs_3_), channel_id=1, source_target_pairs={{0,48},{1,17},{16,32},{17,1},{32,16},{33,49},{48,0},{49,33},{2,50}... | collective-permute-start | bytes 1572872 | tf_op jit(solution)/shard_map/ppermute | solution.py:25
  130.7 12.4 %collective-permute-start.31 = (bf16[1024,256]{1,0:T(8,128)(2,1)S(1)}, bf16[1024,256]{1,0:T(8,128)(2,1)S(1)}, u32[]{:S(2)}, u32[]{:S(2)}) collective-permute-start(bf16[1024,256]{1,0:T(8,128)(2,1)S(1)} %collective-permute-done.30.refs_1_), channel_id=1, source_target_pairs={{0,12},{1,5},{4,8},{5,1},{8,4},{9,13},{12,0},{13,9},{2,14},{3,7},{... | collective-permute-start | bytes 1572872 | tf_op jit(solution)/shard_map/ppermute | solution.py:25
  138.6 10.4 %collective-permute-start.27 = (bf16[1024,256]{1,0:T(8,128)(2,1)S(1)}, bf16[1024,256]{1,0:T(8,128)(2,1)S(1)}, u32[]{:S(2)}, u32[]{:S(2)}) collective-permute-start(bf16[1024,256]{1,0:T(8,128)(2,1)S(1)} %collective-permute-done.26.refs_4_), channel_id=1, source_target_pairs={{0,48},{1,17},{16,32},{17,1},{32,16},{33,49},{48,0},{49,33},{2,50}... | collective-permute-start | bytes 1572872 | tf_op jit(solution)/shard_map/ppermute | solution.py:25
  (8 other events, 80.9 us)

commit v5 on v4

--- a/solution.py
+++ b/solution.py
@@ -41,32 +41,18 @@
 def other_rows(acts, where):
     half = acts.shape[1] // 4
 
-    def kernel(where_ref, acts_ref, out_ref, sem):
-        copies = []
+    def kernel(where_ref, acts_ref, out_ref):
         for part in range(2):
             start = pl.multiple_of((2 * part + 1 - where_ref[3]) * half, half)
-            copies.append(
-                pltpu.make_async_copy(
-                    acts_ref.at[:, pl.ds(start, half)],
-                    out_ref.at[:, pl.ds(part * half, half)],
-                    sem.at[part],
-                )
-            )
-        for copy in copies:
-            copy.start()
-        for copy in copies:
-            copy.wait()
-
+            out_ref[:, part * half : (part + 1) * half] = acts_ref[:, pl.ds(start, half)]
+
+    vmem = pl.BlockSpec(memory_space=pltpu.VMEM)
     return pl.pallas_call(
         kernel,
         out_shape=jax.ShapeDtypeStruct((acts.shape[0], 2 * half), acts.dtype),
-        in_specs=[
-            pl.BlockSpec(memory_space=pltpu.SMEM),
-            pl.BlockSpec(memory_space=pltpu.HBM),
-        ],
-        out_specs=pl.BlockSpec(memory_space=pltpu.VMEM),
-        scratch_shapes=[pltpu.SemaphoreType.DMA((2,))],
-        compiler_params=pltpu.CompilerParams(vmem_limit_bytes=58 * 2**20),
+        in_specs=[pl.BlockSpec(memory_space=pltpu.SMEM), vmem],
+        out_specs=vmem,
+        compiler_params=VMEM,
         cost_estimate=pl.CostEstimate(
             flops=0, bytes_accessed=2 * acts.size, transcendentals=0
         ),
@@ -158,10 +144,9 @@
     where = jnp.stack([x, y, zh, core]).astype(jnp.int32)
     parts = range(2)
 
-    peer_grad = other_core(grad_out)
-    soon_where, peer_grad = lax.optimization_barrier((where, peer_grad))
+    peer, peer_grad = lax.optimization_barrier((other_rows(acts, where), other_core(grad_out)))
+    peer = other_core(peer)
     chip_grad = jnp.concatenate([grad_out, peer_grad], 0)
-    peer = other_core(other_rows(acts, soon_where))
 
     far_grad = [swap(chip_grad, FIRST[p], NEAR) for p in parts]
     sent, rest = arrange(acts, peer, where, 3), arrange(acts, peer, where, 2)

time: 151 us -> 148 us (0.980)
  Pallas kernels: 12.2 us -> 8.83 us
  local copies, waits for them, and re-layouts: 0.24 us -> 2.42 us
  waiting for transfers between devices: 80.8 us -> 78.9 us
    pallas_call x1, Pallas kernels: 4.07 us -> 0.68 us  [other_rows(): pl.pallas_call(kernel, out_shape=jax.ShapeDtypeStruct((acts.shape[0], 2 *...]
    unnamed x19 -> x17, local copies, waits for them, and re-layouts: 0.12 us -> 2.3 us
    ppermute x3, waiting for transfers between devices: 3.27 us -> 1.35 us  [other_core(): return lax.ppermute(array, 'c', [(0, 1), (1, 0)])]
  transfers between devices with their start and end apart: 34 -> 34, of which waited for: 24 -> 23; matrix products, arithmetic and copies ran while one was open for 6% -> 5% of each run, Pallas kernels for 5% -> 5%
where the time goes in v5:
time: 148 us; the launch traced here: 147 us
  waiting for transfers between devices  78.9 us (53%)
  starting transfers between devices  47 us (32%)
  Pallas kernels  8.83 us (6%)
  matrix products  5.84 us (4%)
  other arithmetic  2.95 us (2%)
  local copies, waits for them, and re-layouts  2.42 us (2%)
    ppermute x29, waiting for transfers between devices, swap(): return lax.ppermute(array, (axis, 'c'), pairs)  71.2 us
    ppermute x29, starting transfers between devices, swap(): return lax.ppermute(array, (axis, 'c'), pairs)  44 us
    ppermute x2, waiting for transfers between devices, along_z(): return lambda v: lax.ppermute(v, ('zh', 'zl', 'c'), pairs)  6.35 us
    dot_general x8, matrix products, dot(): lax.dot_general(a, b, (((0,), (0,)), ((), ())), preferred_element_type=F32)  5.84 us
    pallas_call x3, Pallas kernels, place(): pl.pallas_call(kernel, out_shape=jax.ShapeDtypeStruct((8192, 256), BF16),...  4.84 us
    pallas_call x4, Pallas kernels, arrange(): pl.pallas_call(kernel, out_shape=[out] * 2, in_specs=[pl.BlockSpec(memory...  3.31 us
  transfers between devices with their start and end apart: 34, of which 23 were waited for; matrix products, arithmetic and copies ran while one was open for 5% of the time, Pallas kernels for 5%

profile of v5, /device:TPU:2, one launch (start us, length us, event | category | flops | bytes accessed | tf_op | source)
XLA Modules:
  0.0 147.1 jit_solution(13896758209096120543)
XLA Ops:
  0.8 2.2 %copy-done = bf16[256,8192]{1,0:T(8,128)(2,1)S(1)} copy-done((bf16[256,8192]{1,0:T(8,128)(2,1)S(1)}, bf16[256,8192]{1,0:T(8,128)(2,1)}, u32[]{:S(2)}) %copy-start) | copy-done | bytes 4194328
  4.4 2.4 %collective-permute-start.4 = (bf16[512,1024]{1,0:T(8,128)(2,1)S(1)}, bf16[512,1024]{1,0:T(8,128)(2,1)S(1)}, u32[]{:S(2)}, u32[]{:S(2)}) collective-permute-start(bf16[512,1024]{1,0:T(8,128)(2,1)S(1)} %constant_dynamic-update-slice_fusion), channel_id=1, source_target_pairs={{0,4},{1,13},{4,0},{5,9},{8,12},{9,5},{12,8},{13,1},{2,6},{3,15},{... | collective-permute-start | bytes 3145736 | tf_op jit(solution)/shard_map/ppermute | solution.py:25
  8.9 2.4 %collective-permute-start.2 = (bf16[512,512]{1,0:T(8,128)(2,1)S(1)}, bf16[512,512]{1,0:T(8,128)(2,1)S(1)}, u32[]{:S(2)}, u32[]{:S(2)}) collective-permute-start(bf16[512,512]{1,0:T(8,128)(2,1)S(1)} %get-tuple-element.33), channel_id=1, source_target_pairs={{0,4},{1,13},{4,0},{5,9},{8,12},{9,5},{12,8},{13,1},{2,6},{3,15},{... | collective-permute-start | bytes 1572872 | tf_op jit(solution)/shard_map/ppermute | solution.py:25
  16.7 2.8 %collective-permute-done.4 = bf16[512,1024]{1,0:T(8,128)(2,1)S(1)} collective-permute-done((bf16[512,1024]{1,0:T(8,128)(2,1)S(1)}, bf16[512,1024]{1,0:T(8,128)(2,1)S(1)}, u32[]{:S(2)}, u32[]{:S(2)}) %collective-permute-start.4) | collective-permute-done | bytes 1048608 | tf_op jit(solution)/shard_map/ppermute | solution.py:25
  19.5 2.0 %collective-permute-done.5 = bf16[512,1024]{1,0:T(8,128)(2,1)S(1)} collective-permute-done((bf16[512,1024]{1,0:T(8,128)(2,1)S(1)}, bf16[512,1024]{1,0:T(8,128)(2,1)S(1)}, u32[]{:S(2)}, u32[]{:S(2)}) %collective-permute-start.5) | collective-permute-done | bytes 1048608 | tf_op jit(solution)/shard_map/ppermute | solution.py:25
  21.5 3.6 %collective-permute-done.2 = bf16[512,512]{1,0:T(8,128)(2,1)S(1)} collective-permute-done((bf16[512,512]{1,0:T(8,128)(2,1)S(1)}, bf16[512,512]{1,0:T(8,128)(2,1)S(1)}, u32[]{:S(2)}, u32[]{:S(2)}) %collective-permute-start.2) | collective-permute-done | bytes 524320 | tf_op jit(solution)/shard_map/ppermute | solution.py:25
  25.1 2.0 %collective-permute-done.3 = bf16[512,512]{1,0:T(8,128)(2,1)S(1)} collective-permute-done((bf16[512,512]{1,0:T(8,128)(2,1)S(1)}, bf16[512,512]{1,0:T(8,128)(2,1)S(1)}, u32[]{:S(2)}, u32[]{:S(2)}) %collective-permute-start.3) | collective-permute-done | bytes 524320 | tf_op jit(solution)/shard_map/ppermute | solution.py:25
  31.5 2.3 %collective-permute-start.11 = (f16[512,1024]{1,0:T(8,128)(2,1)S(1)}, f16[512,1024]{1,0:T(8,128)(2,1)S(1)}, u32[]{:S(2)}, u32[]{:S(2)}) collective-permute-start(f16[512,1024]{1,0:T(8,128)(2,1)S(1)} %multiply_convert_fusion), channel_id=1, source_target_pairs={{0,48},{1,17},{16,32},{17,1},{32,16},{33,49},{48,0},{49,33},{2,50}... | collective-permute-start | bytes 3145736 | tf_op jit(solution)/shard_map/ppermute | solution.py:25
  33.8 7.0 %collective-permute-done.6 = bf16[512,512]{1,0:T(8,128)(2,1)S(1)} collective-permute-done((bf16[512,512]{1,0:T(8,128)(2,1)S(1)}, bf16[512,512]{1,0:T(8,128)(2,1)S(1)}, u32[]{:S(2)}, u32[]{:S(2)}) %collective-permute-start.6) | collective-permute-done | bytes 524320 | tf_op jit(solution)/shard_map/ppermute | solution.py:25
  42.8 3.1 %collective-permute-done.7 = f16[512,1024]{1,0:T(8,128)(2,1)S(1)} collective-permute-done((f16[512,1024]{1,0:T(8,128)(2,1)S(1)}, f16[512,1024]{1,0:T(8,128)(2,1)S(1)}, u32[]{:S(2)}, u32[]{:S(2)}) %collective-permute-start.7) | collective-permute-done | bytes 1048608 | tf_op jit(solution)/shard_map/ppermute | solution.py:25
  47.2 4.1 %collective-permute-done.11 = f16[512,1024]{1,0:T(8,128)(2,1)S(1)} collective-permute-done((f16[512,1024]{1,0:T(8,128)(2,1)S(1)}, f16[512,1024]{1,0:T(8,128)(2,1)S(1)}, u32[]{:S(2)}, u32[]{:S(2)}) %collective-permute-start.11) | collective-permute-done | bytes 1048608 | tf_op jit(solution)/shard_map/ppermute | solution.py:25
  52.3 3.5 %collective-permute-done.8 = f16[256,1024]{1,0:T(8,128)(2,1)S(1)} collective-permute-done((f16[256,1024]{1,0:T(8,128)(2,1)S(1)}, f16[256,1024]{1,0:T(8,128)(2,1)S(1)}, u32[]{:S(2)}, u32[]{:S(2)}) %collective-permute-start.8) | collective-permute-done | bytes 524320 | tf_op jit(solution)/shard_map/ppermute | solution.py:25
  56.1 3.0 %collective-permute-start.9 = (f16[128,1024]{1,0:T(8,128)(2,1)S(1)}, f16[128,1024]{1,0:T(8,128)(2,1)S(1)}, u32[]{:S(2)}, u32[]{:S(2)}) collective-permute-start(f16[128,1024]{1,0:T(8,128)(2,1)S(1)} %fusion.8), channel_id=1, source_target_pairs={{0,48},{1,17},{16,32},{17,1},{32,16},{33,49},{48,0},{49,33},{2,50}... | collective-permute-start | bytes 786440 | tf_op jit(solution)/shard_map/ppermute | solution.py:25
  59.2 1.9 %collective-permute-done.12 = f16[256,1024]{1,0:T(8,128)(2,1)S(1)} collective-permute-done((f16[256,1024]{1,0:T(8,128)(2,1)S(1)}, f16[256,1024]{1,0:T(8,128)(2,1)S(1)}, u32[]{:S(2)}, u32[]{:S(2)}) %collective-permute-start.12) | collective-permute-done | bytes 524320 | tf_op jit(solution)/shard_map/ppermute | solution.py:25
  63.9 4.0 %collective-permute-done.13 = f16[128,1024]{1,0:T(8,128)(2,1)S(1)} collective-permute-done((f16[128,1024]{1,0:T(8,128)(2,1)S(1)}, f16[128,1024]{1,0:T(8,128)(2,1)S(1)}, u32[]{:S(2)}, u32[]{:S(2)}) %collective-permute-start.13) | collective-permute-done | bytes 262176 | tf_op jit(solution)/shard_map/ppermute | solution.py:25
  70.5 2.9 %collective-permute-done.14 = f16[256,256]{1,0:T(8,128)(2,1)S(1)} collective-permute-done((f16[256,256]{1,0:T(8,128)(2,1)S(1)}, f16[256,256]{1,0:T(8,128)(2,1)S(1)}, u32[]{:S(2)}, u32[]{:S(2)}) %collective-permute-start.14) | collective-permute-done | bytes 131104 | tf_op jit(solution)/shard_map/ppermute | solution.py:192
  73.3 3.5 %collective-permute-done.16 = f16[256,256]{1,0:T(8,128)(2,1)S(1)} collective-permute-done((f16[256,256]{1,0:T(8,128)(2,1)S(1)}, f16[256,256]{1,0:T(8,128)(2,1)S(1)}, u32[]{:S(2)}, u32[]{:S(2)}) %collective-permute-start.16) | collective-permute-done | bytes 131104 | tf_op jit(solution)/shard_map/ppermute | solution.py:192
  77.8 9.0 %collective-permute-done.17 = f32[256,256]{1,0:T(8,128)S(1)} collective-permute-done((f32[256,256]{1,0:T(8,128)S(1)}, f32[256,256]{1,0:T(8,128)S(1)}, u32[]{:S(2)}, u32[]{:S(2)}) %collective-permute-start.17) | collective-permute-done | bytes 262176 | tf_op jit(solution)/shard_map/ppermute | solution.py:25
  86.8 2.7 %collective-permute-start.18 = (f32[128,256]{1,0:T(8,128)S(1)}, f32[128,256]{1,0:T(8,128)S(1)}, u32[]{:S(2)}, u32[]{:S(2)}) collective-permute-start(f32[128,256]{1,0:T(8,128)S(1)} %slice_add_fusion.7), channel_id=1, source_target_pairs={{0,192},{1,65},{64,128},{65,1},{128,64},{129,193},{192,0},{193,129... | collective-permute-start | bytes 393224 | tf_op jit(solution)/shard_map/ppermute | solution.py:25
  89.5 5.8 %collective-permute-done.18 = f32[128,256]{1,0:T(8,128)S(1)} collective-permute-done((f32[128,256]{1,0:T(8,128)S(1)}, f32[128,256]{1,0:T(8,128)S(1)}, u32[]{:S(2)}, u32[]{:S(2)}) %collective-permute-start.18) | collective-permute-done | bytes 131104 | tf_op jit(solution)/shard_map/ppermute | solution.py:25
  96.9 2.5 %collective-permute-start.19 = (bf16[128,256]{1,0:T(8,128)(2,1)S(1)}, bf16[128,256]{1,0:T(8,128)(2,1)S(1)}, u32[]{:S(2)}, u32[]{:S(2)}) collective-permute-start(bf16[128,256]{1,0:T(8,128)(2,1)S(1)} %get-tuple-element.49), channel_id=1, source_target_pairs={{0,192},{1,65},{64,128},{65,1},{128,64},{129,193},{192,0},{193,129... | collective-permute-start | bytes 196616 | tf_op jit(solution)/shard_map/ppermute | solution.py:25
  99.3 3.4 %collective-permute-start.20 = (bf16[128,256]{1,0:T(8,128)(2,1)S(1)}, bf16[128,256]{1,0:T(8,128)(2,1)S(1)}, u32[]{:S(2)}, u32[]{:S(2)}) collective-permute-start(bf16[128,256]{1,0:T(8,128)(2,1)S(1)} %get-tuple-element.49), channel_id=1, source_target_pairs={{0,128},{1,129},{64,192},{65,193},{128,0},{129,1},{192,64},{193,65... | collective-permute-start | bytes 196616 | tf_op jit(solution)/shard_map/ppermute | solution.py:25
  103.0 2.9 %collective-permute-start.28 = (bf16[256,256]{1,0:T(8,128)(2,1)S(1)}, bf16[256,256]{1,0:T(8,128)(2,1)S(1)}, u32[]{:S(2)}, u32[]{:S(2)}) collective-permute-start(bf16[256,256]{1,0:T(8,128)(2,1)S(1)} %pad_maximum_fusion.4), channel_id=1, source_target_pairs={{0,48},{1,17},{16,32},{17,1},{32,16},{33,49},{48,0},{49,33},{2,50}... | collective-permute-start | bytes 393224 | tf_op jit(solution)/shard_map/ppermute | solution.py:25
  109.2 2.6 %collective-permute-start.23 = (bf16[256,256]{1,0:T(8,128)(2,1)S(1)}, bf16[256,256]{1,0:T(8,128)(2,1)S(1)}, u32[]{:S(2)}, u32[]{:S(2)}) collective-permute-start(bf16[256,256]{1,0:T(8,128)(2,1)S(1)} %pad_maximum_fusion.3), channel_id=1, source_target_pairs={{0,4},{1,13},{4,0},{5,9},{8,12},{9,5},{12,8},{13,1},{2,6},{3,15},{... | collective-permute-start | bytes 393224 | tf_op jit(solution)/shard_map/ppermute | solution.py:25
  114.0 2.2 %collective-permute-start.30 = (bf16[1024,256]{1,0:T(8,128)(2,1)S(1)}, bf16[1024,256]{1,0:T(8,128)(2,1)S(1)}, u32[]{:S(2)}, u32[]{:S(2)}) collective-permute-start(bf16[1024,256]{1,0:T(8,128)(2,1)S(1)} %constant_dynamic-update-slice_fusion.6.refs_0_), channel_id=1, source_target_pairs={{0,4},{1,13},{4,0},{5,9},{8,12},{9,5},{12,8},{13,1},{2,6},{3,15},{... | collective-permute-start | bytes 1572872 | tf_op jit(solution)/shard_map/ppermute | solution.py:25
  116.3 4.0 %collective-permute-done.24 = bf16[256,256]{1,0:T(8,128)(2,1)S(1)} collective-permute-done((bf16[256,256]{1,0:T(8,128)(2,1)S(1)}, bf16[256,256]{1,0:T(8,128)(2,1)S(1)}, u32[]{:S(2)}, u32[]{:S(2)}) %collective-permute-start.24) | collective-permute-done | bytes 131104 | tf_op jit(solution)/shard_map/ppermute | solution.py:25
  122.3 2.1 %collective-permute-start.33 = (bf16[1024,256]{1,0:T(8,128)(2,1)S(1)}, bf16[1024,256]{1,0:T(8,128)(2,1)S(1)}, u32[]{:S(2)}, u32[]{:S(2)}) collective-permute-start(bf16[1024,256]{1,0:T(8,128)(2,1)S(1)} %constant_dynamic-update-slice_fusion.2.refs_3_), channel_id=1, source_target_pairs={{0,48},{1,17},{16,32},{17,1},{32,16},{33,49},{48,0},{49,33},{2,50}... | collective-permute-start | bytes 1572872 | tf_op jit(solution)/shard_map/ppermute | solution.py:25
  124.4 3.5 %collective-permute-done.30.refs_1_ = bf16[1024,256]{1,0:T(8,128)(2,1)S(1)} collective-permute-done((bf16[1024,256]{1,0:T(8,128)(2,1)S(1)}, bf16[1024,256]{1,0:T(8,128)(2,1)S(1)}, u32[]{:S(2)}, u32[]{:S(2)}) %collective-permute-start.30) | collective-permute-done | bytes 524320 | tf_op jit(solution)/shard_map/ppermute | solution.py:25
  129.0 6.2 %collective-permute-done.26.refs_4_ = bf16[1024,256]{1,0:T(8,128)(2,1)S(1)} collective-permute-done((bf16[1024,256]{1,0:T(8,128)(2,1)S(1)}, bf16[1024,256]{1,0:T(8,128)(2,1)S(1)}, u32[]{:S(2)}, u32[]{:S(2)}) %collective-permute-start.26) | collective-permute-done | bytes 524320 | tf_op jit(solution)/shard_map/ppermute | solution.py:25
  135.2 2.5 %collective-permute-start.27 = (bf16[1024,256]{1,0:T(8,128)(2,1)S(1)}, bf16[1024,256]{1,0:T(8,128)(2,1)S(1)}, u32[]{:S(2)}, u32[]{:S(2)}) collective-permute-start(bf16[1024,256]{1,0:T(8,128)(2,1)S(1)} %collective-permute-done.26.refs_4_), channel_id=1, source_target_pairs={{0,48},{1,17},{16,32},{17,1},{32,16},{33,49},{48,0},{49,33},{2,50}... | collective-permute-start | bytes 1572872 | tf_op jit(solution)/shard_map/ppermute | solution.py:25
  137.7 2.2 %shard_map.89.refs_1_ = bf16[8192,256]{1,0:T(8,128)(2,1)} custom-call(s32[4]{0:T(128)S(1)} %pad_add_fusion.where_ref, bf16[1024,256]{1,0:T(8,128)(2,1)S(1)} %constant_dynamic-update-slice_fusion.6.refs_0_, bf16[1024,256]{1,0:T(8,128)(2,1)S(1)} %collective-permute-done.30.refs_1_, bf16[1024,256]{1,0:T(8,128)(2,1)S(1)} %collective-permute-done.32.refs_2_, ...), custom_call_target="tpu_custom_call" | custom-call | bytes 6291456 | tf_op jit(solution)/shard_map/pallas_call | solution.py:118
  141.3 4.4 %collective-permute-done.27.refs_0_ = bf16[1024,256]{1,0:T(8,128)(2,1)S(1)} collective-permute-done((bf16[1024,256]{1,0:T(8,128)(2,1)S(1)}, bf16[1024,256]{1,0:T(8,128)(2,1)S(1)}, u32[]{:S(2)}, u32[]{:S(2)}) %collective-permute-start.27) | collective-permute-done | bytes 524320 | tf_op jit(solution)/shard_map/ppermute | solution.py:25
  (95 shorter events, 37.4 us)
Async XLA Ops:
  4.4 15.1 %collective-permute-start.4 = (bf16[512,1024]{1,0:T(8,128)(2,1)S(1)}, bf16[512,1024]{1,0:T(8,128)(2,1)S(1)}, u32[]{:S(2)}, u32[]{:S(2)}) collective-permute-start(bf16[512,1024]{1,0:T(8,128)(2,1)S(1)} %constant_dynamic-update-slice_fusion), channel_id=1, source_target_pairs={{0,4},{1,13},{4,0},{5,9},{8,12},{9,5},{12,8},{13,1},{2,6},{3,15},{... | collective-permute-start | bytes 3145736 | tf_op jit(solution)/shard_map/ppermute | solution.py:25
  6.7 14.8 %collective-permute-start.5 = (bf16[512,1024]{1,0:T(8,128)(2,1)S(1)}, bf16[512,1024]{1,0:T(8,128)(2,1)S(1)}, u32[]{:S(2)}, u32[]{:S(2)}) collective-permute-start(bf16[512,1024]{1,0:T(8,128)(2,1)S(1)} %constant_dynamic-update-slice_fusion), channel_id=1, source_target_pairs={{0,16},{1,49},{16,0},{17,33},{32,48},{33,17},{48,32},{49,1},{2,18}... | collective-permute-start | bytes 3145736 | tf_op jit(solution)/shard_map/ppermute | solution.py:25
  8.9 16.2 %collective-permute-start.2 = (bf16[512,512]{1,0:T(8,128)(2,1)S(1)}, bf16[512,512]{1,0:T(8,128)(2,1)S(1)}, u32[]{:S(2)}, u32[]{:S(2)}) collective-permute-start(bf16[512,512]{1,0:T(8,128)(2,1)S(1)} %get-tuple-element.33), channel_id=1, source_target_pairs={{0,4},{1,13},{4,0},{5,9},{8,12},{9,5},{12,8},{13,1},{2,6},{3,15},{... | collective-permute-start | bytes 1572872 | tf_op jit(solution)/shard_map/ppermute | solution.py:25
  11.3 15.9 %collective-permute-start.3 = (bf16[512,512]{1,0:T(8,128)(2,1)S(1)}, bf16[512,512]{1,0:T(8,128)(2,1)S(1)}, u32[]{:S(2)}, u32[]{:S(2)}) collective-permute-start(bf16[512,512]{1,0:T(8,128)(2,1)S(1)} %get-tuple-element.34), channel_id=1, source_target_pairs={{0,16},{1,49},{16,0},{17,33},{32,48},{33,17},{48,32},{49,1},{2,18}... | collective-permute-start | bytes 1572872 | tf_op jit(solution)/shard_map/ppermute | solution.py:25
  27.1 13.7 %collective-permute-start.6 = (bf16[512,512]{1,0:T(8,128)(2,1)S(1)}, bf16[512,512]{1,0:T(8,128)(2,1)S(1)}, u32[]{:S(2)}, u32[]{:S(2)}) collective-permute-start(bf16[512,512]{1,0:T(8,128)(2,1)S(1)} %get-tuple-element.37), channel_id=1, source_target_pairs={{0,4},{1,13},{4,0},{5,9},{8,12},{9,5},{12,8},{13,1},{2,6},{3,15},{... | collective-permute-start | bytes 1572872 | tf_op jit(solution)/shard_map/ppermute | solution.py:25
  28.0 17.9 %collective-permute-start.7 = (f16[512,1024]{1,0:T(8,128)(2,1)S(1)}, f16[512,1024]{1,0:T(8,128)(2,1)S(1)}, u32[]{:S(2)}, u32[]{:S(2)}) collective-permute-start(f16[512,1024]{1,0:T(8,128)(2,1)S(1)} %multiply_convert_fusion.1), channel_id=1, source_target_pairs={{0,12},{1,5},{4,8},{5,1},{8,4},{9,13},{12,0},{13,9},{2,14},{3,7},{... | collective-permute-start | bytes 3145736 | tf_op jit(solution)/shard_map/ppermute | solution.py:25
  29.2 12.9 %collective-permute-start.10 = (bf16[512,512]{1,0:T(8,128)(2,1)S(1)}, bf16[512,512]{1,0:T(8,128)(2,1)S(1)}, u32[]{:S(2)}, u32[]{:S(2)}) collective-permute-start(bf16[512,512]{1,0:T(8,128)(2,1)S(1)} %get-tuple-element.42), channel_id=1, source_target_pairs={{0,16},{1,49},{16,0},{17,33},{32,48},{33,17},{48,32},{49,1},{2,18}... | collective-permute-start | bytes 1572872 | tf_op jit(solution)/shard_map/ppermute | solution.py:25
  31.5 19.8 %collective-permute-start.11 = (f16[512,1024]{1,0:T(8,128)(2,1)S(1)}, f16[512,1024]{1,0:T(8,128)(2,1)S(1)}, u32[]{:S(2)}, u32[]{:S(2)}) collective-permute-start(f16[512,1024]{1,0:T(8,128)(2,1)S(1)} %multiply_convert_fusion), channel_id=1, source_target_pairs={{0,48},{1,17},{16,32},{17,1},{32,16},{33,49},{48,0},{49,33},{2,50}... | collective-permute-start | bytes 3145736 | tf_op jit(solution)/shard_map/ppermute | solution.py:25
  46.4 9.4 %collective-permute-start.8 = (f16[256,1024]{1,0:T(8,128)(2,1)S(1)}, f16[256,1024]{1,0:T(8,128)(2,1)S(1)}, u32[]{:S(2)}, u32[]{:S(2)}) collective-permute-start(f16[256,1024]{1,0:T(8,128)(2,1)S(1)} %fusion.4), channel_id=1, source_target_pairs={{0,16},{1,49},{16,0},{17,33},{32,48},{33,17},{48,32},{49,1},{2,18}... | collective-permute-start | bytes 1572872 | tf_op jit(solution)/shard_map/ppermute | solution.py:25
  51.8 9.3 %collective-permute-start.12 = (f16[256,1024]{1,0:T(8,128)(2,1)S(1)}, f16[256,1024]{1,0:T(8,128)(2,1)S(1)}, u32[]{:S(2)}, u32[]{:S(2)}) collective-permute-start(f16[256,1024]{1,0:T(8,128)(2,1)S(1)} %fusion.1), channel_id=1, source_target_pairs={{0,4},{1,13},{4,0},{5,9},{8,12},{9,5},{12,8},{13,1},{2,6},{3,15},{... | collective-permute-start | bytes 1572872 | tf_op jit(solution)/shard_map/ppermute | solution.py:25
  56.1 7.7 %collective-permute-start.9 = (f16[128,1024]{1,0:T(8,128)(2,1)S(1)}, f16[128,1024]{1,0:T(8,128)(2,1)S(1)}, u32[]{:S(2)}, u32[]{:S(2)}) collective-permute-start(f16[128,1024]{1,0:T(8,128)(2,1)S(1)} %fusion.8), channel_id=1, source_target_pairs={{0,48},{1,17},{16,32},{17,1},{32,16},{33,49},{48,0},{49,33},{2,50}... | collective-permute-start | bytes 786440 | tf_op jit(solution)/shard_map/ppermute | solution.py:25
  61.4 6.5 %collective-permute-start.13 = (f16[128,1024]{1,0:T(8,128)(2,1)S(1)}, f16[128,1024]{1,0:T(8,128)(2,1)S(1)}, u32[]{:S(2)}, u32[]{:S(2)}) collective-permute-start(f16[128,1024]{1,0:T(8,128)(2,1)S(1)} %fusion.7), channel_id=1, source_target_pairs={{0,12},{1,5},{4,8},{5,1},{8,4},{9,13},{12,0},{13,9},{2,14},{3,7},{... | collective-permute-start | bytes 786440 | tf_op jit(solution)/shard_map/ppermute | solution.py:25
  68.1 8.7 %collective-permute-start.15 = (f32[256,256]{1,0:T(8,128)S(1)}, f32[256,256]{1,0:T(8,128)S(1)}, u32[]{:S(2)}, u32[]{:S(2)}) collective-permute-start(f32[256,256]{1,0:T(8,128)S(1)} %slice_select_fusion), channel_id=1, source_target_pairs={{0,1},{1,0},{2,3},{3,2},{4,5},{5,4},{6,7},{7,6},{8,9},{9,8},{10,11... | collective-permute-start | bytes 786440 | tf_op jit(solution)/shard_map/ppermute | solution.py:29
  68.3 5.1 %collective-permute-start.14 = (f16[256,256]{1,0:T(8,128)(2,1)S(1)}, f16[256,256]{1,0:T(8,128)(2,1)S(1)}, u32[]{:S(2)}, u32[]{:S(2)}) collective-permute-start(f16[256,256]{1,0:T(8,128)(2,1)S(1)} %get-tuple-element.59), channel_id=1, source_target_pairs={{0,2},{1,195},{2,0},{3,65},{64,66},{65,3},{66,64},{67,129},{128,13... | collective-permute-start | bytes 393224 | tf_op jit(solution)/shard_map/ppermute | solution.py:192
  68.7 8.1 %collective-permute-start.16 = (f16[256,256]{1,0:T(8,128)(2,1)S(1)}, f16[256,256]{1,0:T(8,128)(2,1)S(1)}, u32[]{:S(2)}, u32[]{:S(2)}) collective-permute-start(f16[256,256]{1,0:T(8,128)(2,1)S(1)} %get-tuple-element.60), channel_id=1, source_target_pairs={{0,3},{1,194},{2,1},{3,64},{64,67},{65,2},{66,65},{67,128},{128,13... | collective-permute-start | bytes 393224 | tf_op jit(solution)/shard_map/ppermute | solution.py:192
  77.1 9.7 %collective-permute-start.17 = (f32[256,256]{1,0:T(8,128)S(1)}, f32[256,256]{1,0:T(8,128)S(1)}, u32[]{:S(2)}, u32[]{:S(2)}) collective-permute-start(f32[256,256]{1,0:T(8,128)S(1)} %pad_maximum_fusion.2), channel_id=1, source_target_pairs={{0,64},{1,193},{64,0},{65,129},{128,192},{129,65},{192,128},{193,1... | collective-permute-start | bytes 786440 | tf_op jit(solution)/shard_map/ppermute | solution.py:25
  86.8 8.6 %collective-permute-start.18 = (f32[128,256]{1,0:T(8,128)S(1)}, f32[128,256]{1,0:T(8,128)S(1)}, u32[]{:S(2)}, u32[]{:S(2)}) collective-permute-start(f32[128,256]{1,0:T(8,128)S(1)} %slice_add_fusion.7), channel_id=1, source_target_pairs={{0,192},{1,65},{64,128},{65,1},{128,64},{129,193},{192,0},{193,129... | collective-permute-start | bytes 393224 | tf_op jit(solution)/shard_map/ppermute | solution.py:25
  96.2 6.5 %collective-permute-start.21 = (bf16[128,256]{1,0:T(8,128)(2,1)S(1)}, bf16[128,256]{1,0:T(8,128)(2,1)S(1)}, u32[]{:S(2)}, u32[]{:S(2)}) collective-permute-start(bf16[128,256]{1,0:T(8,128)(2,1)S(1)} %get-tuple-element.49), channel_id=1, source_target_pairs={{0,64},{1,193},{64,0},{65,129},{128,192},{129,65},{192,128},{193,1... | collective-permute-start | bytes 196616 | tf_op jit(solution)/shard_map/ppermute | solution.py:25
  96.9 10.4 %collective-permute-start.19 = (bf16[128,256]{1,0:T(8,128)(2,1)S(1)}, bf16[128,256]{1,0:T(8,128)(2,1)S(1)}, u32[]{:S(2)}, u32[]{:S(2)}) collective-permute-start(bf16[128,256]{1,0:T(8,128)(2,1)S(1)} %get-tuple-element.49), channel_id=1, source_target_pairs={{0,192},{1,65},{64,128},{65,1},{128,64},{129,193},{192,0},{193,129... | collective-permute-start | bytes 196616 | tf_op jit(solution)/shard_map/ppermute | solution.py:25
  99.3 8.3 %collective-permute-start.20 = (bf16[128,256]{1,0:T(8,128)(2,1)S(1)}, bf16[128,256]{1,0:T(8,128)(2,1)S(1)}, u32[]{:S(2)}, u32[]{:S(2)}) collective-permute-start(bf16[128,256]{1,0:T(8,128)(2,1)S(1)} %get-tuple-element.49), channel_id=1, source_target_pairs={{0,128},{1,129},{64,192},{65,193},{128,0},{129,1},{192,64},{193,65... | collective-permute-start | bytes 196616 | tf_op jit(solution)/shard_map/ppermute | solution.py:25
  102.7 6.4 %collective-permute-start.22 = (bf16[256,256]{1,0:T(8,128)(2,1)S(1)}, bf16[256,256]{1,0:T(8,128)(2,1)S(1)}, u32[]{:S(2)}, u32[]{:S(2)}) collective-permute-start(bf16[256,256]{1,0:T(8,128)(2,1)S(1)} %pad_maximum_fusion.4), channel_id=1, source_target_pairs={{0,16},{1,49},{16,0},{17,33},{32,48},{33,17},{48,32},{49,1},{2,18}... | collective-permute-start | bytes 393224 | tf_op jit(solution)/shard_map/ppermute | solution.py:25
  103.0 11.0 %collective-permute-start.28 = (bf16[256,256]{1,0:T(8,128)(2,1)S(1)}, bf16[256,256]{1,0:T(8,128)(2,1)S(1)}, u32[]{:S(2)}, u32[]{:S(2)}) collective-permute-start(bf16[256,256]{1,0:T(8,128)(2,1)S(1)} %pad_maximum_fusion.4), channel_id=1, source_target_pairs={{0,48},{1,17},{16,32},{17,1},{32,16},{33,49},{48,0},{49,33},{2,50}... | collective-permute-start | bytes 393224 | tf_op jit(solution)/shard_map/ppermute | solution.py:25
  105.9 8.1 %collective-permute-start.29 = (bf16[256,256]{1,0:T(8,128)(2,1)S(1)}, bf16[256,256]{1,0:T(8,128)(2,1)S(1)}, u32[]{:S(2)}, u32[]{:S(2)}) collective-permute-start(bf16[256,256]{1,0:T(8,128)(2,1)S(1)} %pad_maximum_fusion.4), channel_id=1, source_target_pairs={{0,32},{1,33},{16,48},{17,49},{32,0},{33,1},{48,16},{49,17},{2,34}... | collective-permute-start | bytes 393224 | tf_op jit(solution)/shard_map/ppermute | solution.py:25
  109.2 7.1 %collective-permute-start.23 = (bf16[256,256]{1,0:T(8,128)(2,1)S(1)}, bf16[256,256]{1,0:T(8,128)(2,1)S(1)}, u32[]{:S(2)}, u32[]{:S(2)}) collective-permute-start(bf16[256,256]{1,0:T(8,128)(2,1)S(1)} %pad_maximum_fusion.3), channel_id=1, source_target_pairs={{0,4},{1,13},{4,0},{5,9},{8,12},{9,5},{12,8},{13,1},{2,6},{3,15},{... | collective-permute-start | bytes 393224 | tf_op jit(solution)/shard_map/ppermute | solution.py:25
  111.8 8.5 %collective-permute-start.24 = (bf16[256,256]{1,0:T(8,128)(2,1)S(1)}, bf16[256,256]{1,0:T(8,128)(2,1)S(1)}, u32[]{:S(2)}, u32[]{:S(2)}) collective-permute-start(bf16[256,256]{1,0:T(8,128)(2,1)S(1)} %pad_maximum_fusion.3), channel_id=1, source_target_pairs={{0,12},{1,5},{4,8},{5,1},{8,4},{9,13},{12,0},{13,9},{2,14},{3,7},{... | collective-permute-start | bytes 393224 | tf_op jit(solution)/shard_map/ppermute | solution.py:25
  113.0 7.3 %collective-permute-start.25 = (bf16[256,256]{1,0:T(8,128)(2,1)S(1)}, bf16[256,256]{1,0:T(8,128)(2,1)S(1)}, u32[]{:S(2)}, u32[]{:S(2)}) collective-permute-start(bf16[256,256]{1,0:T(8,128)(2,1)S(1)} %pad_maximum_fusion.3), channel_id=1, source_target_pairs={{0,8},{1,9},{4,12},{5,13},{8,0},{9,1},{12,4},{13,5},{2,10},{3,11},... | collective-permute-start | bytes 393224 | tf_op jit(solution)/shard_map/ppermute | solution.py:25
  114.0 13.8 %collective-permute-start.30 = (bf16[1024,256]{1,0:T(8,128)(2,1)S(1)}, bf16[1024,256]{1,0:T(8,128)(2,1)S(1)}, u32[]{:S(2)}, u32[]{:S(2)}) collective-permute-start(bf16[1024,256]{1,0:T(8,128)(2,1)S(1)} %constant_dynamic-update-slice_fusion.6.refs_0_), channel_id=1, source_target_pairs={{0,4},{1,13},{4,0},{5,9},{8,12},{9,5},{12,8},{13,1},{2,6},{3,15},{... | collective-permute-start | bytes 1572872 | tf_op jit(solution)/shard_map/ppermute | solution.py:25
  120.3 14.9 %collective-permute-start.26 = (bf16[1024,256]{1,0:T(8,128)(2,1)S(1)}, bf16[1024,256]{1,0:T(8,128)(2,1)S(1)}, u32[]{:S(2)}, u32[]{:S(2)}) collective-permute-start(bf16[1024,256]{1,0:T(8,128)(2,1)S(1)} %constant_dynamic-update-slice_fusion.2.refs_3_), channel_id=1, source_target_pairs={{0,16},{1,49},{16,0},{17,33},{32,48},{33,17},{48,32},{49,1},{2,18}... | collective-permute-start | bytes 1572872 | tf_op jit(solution)/shard_map/ppermute | solution.py:25
  120.7 17.0 %collective-permute-start.32 = (bf16[1024,256]{1,0:T(8,128)(2,1)S(1)}, bf16[1024,256]{1,0:T(8,128)(2,1)S(1)}, u32[]{:S(2)}, u32[]{:S(2)}) collective-permute-start(bf16[1024,256]{1,0:T(8,128)(2,1)S(1)} %constant_dynamic-update-slice_fusion.6.refs_0_), channel_id=1, source_target_pairs={{0,12},{1,5},{4,8},{5,1},{8,4},{9,13},{12,0},{13,9},{2,14},{3,7},{... | collective-permute-start | bytes 1572872 | tf_op jit(solution)/shard_map/ppermute | solution.py:25
  122.3 15.4 %collective-permute-start.33 = (bf16[1024,256]{1,0:T(8,128)(2,1)S(1)}, bf16[1024,256]{1,0:T(8,128)(2,1)S(1)}, u32[]{:S(2)}, u32[]{:S(2)}) collective-permute-start(bf16[1024,256]{1,0:T(8,128)(2,1)S(1)} %constant_dynamic-update-slice_fusion.2.refs_3_), channel_id=1, source_target_pairs={{0,48},{1,17},{16,32},{17,1},{32,16},{33,49},{48,0},{49,33},{2,50}... | collective-permute-start | bytes 1572872 | tf_op jit(solution)/shard_map/ppermute | solution.py:25
  127.8 12.1 %collective-permute-start.31 = (bf16[1024,256]{1,0:T(8,128)(2,1)S(1)}, bf16[1024,256]{1,0:T(8,128)(2,1)S(1)}, u32[]{:S(2)}, u32[]{:S(2)}) collective-permute-start(bf16[1024,256]{1,0:T(8,128)(2,1)S(1)} %collective-permute-done.30.refs_1_), channel_id=1, source_target_pairs={{0,12},{1,5},{4,8},{5,1},{8,4},{9,13},{12,0},{13,9},{2,14},{3,7},{... | collective-permute-start | bytes 1572872 | tf_op jit(solution)/shard_map/ppermute | solution.py:25
  135.2 10.4 %collective-permute-start.27 = (bf16[1024,256]{1,0:T(8,128)(2,1)S(1)}, bf16[1024,256]{1,0:T(8,128)(2,1)S(1)}, u32[]{:S(2)}, u32[]{:S(2)}) collective-permute-start(bf16[1024,256]{1,0:T(8,128)(2,1)S(1)} %collective-permute-done.26.refs_4_), channel_id=1, source_target_pairs={{0,48},{1,17},{16,32},{17,1},{32,16},{33,49},{48,0},{49,33},{2,50}... | collective-permute-start | bytes 1572872 | tf_op jit(solution)/shard_map/ppermute | solution.py:25
  (7 other events, 66.4 us)

commit v6 on v5

--- a/solution.py
+++ b/solution.py
@@ -88,7 +88,7 @@
     )(where, acts, peer)
 
 
-def place(pieces, where, parts, firsts, into=None):
+def place(pieces, where, specs, into=None):
     many = len(pieces)
 
     def kernel(where_ref, *refs):
@@ -96,19 +96,18 @@
         x, y, zh, core = (where_ref[i] for i in range(4))
         distances = (0, GATHER_NEAR[0] + (GATHER_NEAR[1] - GATHER_NEAR[0]) * core, GATHER_NEXT[0] + (GATHER_NEXT[1] - GATHER_NEXT[0]) * core, 2)
         copies = []
-        for index, part in enumerate(parts):
-            for i, first in enumerate(firsts):
-                for j in range(4):
-                    for k in range(2):
-                        block = lax.bitwise_xor(zh, distances[2 * part + k]) * 16
-                        block += owner(part, distances[first], distances[j], x, y)
-                        copies.append(
-                            pltpu.make_async_copy(
-                                ins[index * len(firsts) + i].at[pl.ds((j * 2 + k) * BLOCK, BLOCK), :],
-                                out_ref.at[pl.ds(pl.multiple_of(block * BLOCK, BLOCK), BLOCK), :],
-                                sem,
-                            )
+        for index, (part, first, seconds) in enumerate(specs):
+            for j, second in enumerate(seconds):
+                for k in range(2):
+                    block = lax.bitwise_xor(zh, distances[2 * part + k]) * 16
+                    block += owner(part, distances[first], distances[second], x, y)
+                    copies.append(
+                        pltpu.make_async_copy(
+                            ins[index].at[pl.ds((j * 2 + k) * BLOCK, BLOCK), :],
+                            out_ref.at[pl.ds(pl.multiple_of(block * BLOCK, BLOCK), BLOCK), :],
+                            sem,
                         )
+                    )
         for copy in copies:
             copy.start()
         for copy in copies:
@@ -216,14 +215,19 @@
     far = [swap(pieces[0], SECOND[0], by) for by in every]
     pieces[1], far[0] = lax.optimization_barrier((pieces[1], far[0]))
     pieces[0] = jnp.concatenate([pieces[0]] + far, 0)
-    pieces[1] = jnp.concatenate([pieces[1]] + [swap(pieces[1], SECOND[1], by) for by in every], 0)
+    far = [swap(pieces[1], SECOND[1], by) for by in every]
+    pieces[0], far[0] = lax.optimization_barrier((pieces[0], far[0]))
+    pieces[1] = jnp.concatenate([pieces[1]] + far, 0)
     near = [swap(pieces[p], FIRST[p], GATHER_NEAR) for p in parts]
     following = [swap(pieces[p], FIRST[p], GATHER_NEXT) for p in parts]
-    last = [swap(near[p], FIRST[p], GATHER_NEXT) for p in parts]
+    last = [
+        [swap(near[p][:512], FIRST[p], GATHER_NEXT), swap(following[p][512:], FIRST[p], GATHER_NEAR)]
+        for p in parts
+    ]
     first = [array for p in parts for array in (pieces[p], near[p], following[p])]
-    new_weights = place(first, where, parts, (0, 1, 2))
+    new_weights = place(first, where, [(p, i, range(4)) for p in parts for i in range(3)])
     for p in parts:
-        new_weights = place([last[p]], where, (p,), (3,), new_weights)
+        new_weights = place(last[p], where, [(p, 3, (0, 1)), (p, 3, (2, 3))], new_weights)
     return (new_master, new_moment1, new_moment2, new_weights)
 
 

time: 148 us -> 143 us (0.966)
  waiting for transfers between devices: 78.9 us -> 71.9 us
  starting transfers between devices: 47 us -> 48.9 us
    ppermute x29 -> x31, waiting for transfers between devices: 71.2 us -> 64.2 us  [swap(): return lax.ppermute(array, (axis, 'c'), pairs)]
    ppermute x29 -> x31, starting transfers between devices: 44 us -> 45.9 us  [swap(): return lax.ppermute(array, (axis, 'c'), pairs)]
  transfers between devices with their start and end apart: 34 -> 36, of which waited for: 23 -> 25; matrix products, arithmetic and copies ran while one was open for 5% -> 6% of each run, Pallas kernels for 5% -> 5%
where the time goes in v6:
time: 143 us; the launch traced here: 142 us
  waiting for transfers between devices  71.9 us (50%)
  starting transfers between devices  48.9 us (34%)
  Pallas kernels  8.83 us (6%)
  matrix products  5.84 us (4%)
  other arithmetic  2.95 us (2%)
  local copies, waits for them, and re-layouts  2.49 us (2%)
    ppermute x31, waiting for transfers between devices, swap(): return lax.ppermute(array, (axis, 'c'), pairs)  64.2 us
    ppermute x31, starting transfers between devices, swap(): return lax.ppermute(array, (axis, 'c'), pairs)  45.9 us
    ppermute x2, waiting for transfers between devices, along_z(): return lambda v: lax.ppermute(v, ('zh', 'zl', 'c'), pairs)  6.35 us
    dot_general x8, matrix products, dot(): lax.dot_general(a, b, (((0,), (0,)), ((), ())), preferred_element_type=F32)  5.84 us
    pallas_call x3, Pallas kernels, place(): pl.pallas_call(kernel, out_shape=jax.ShapeDtypeStruct((8192, 256), BF16),...  4.84 us
    pallas_call x4, Pallas kernels, arrange(): pl.pallas_call(kernel, out_shape=[out] * 2, in_specs=[pl.BlockSpec(memory...  3.31 us
  transfers between devices with their start and end apart: 36, of which 25 were waited for; matrix products, arithmetic and copies ran while one was open for 6% of the time, Pallas kernels for 5%

profile of v6, /device:TPU:2, one launch (start us, length us, event | category | flops | bytes accessed | tf_op | source)
XLA Modules:
  0.0 142.1 jit_solution(11881765280910961298)
XLA Ops:
  0.8 2.2 %copy-done = bf16[256,8192]{1,0:T(8,128)(2,1)S(1)} copy-done((bf16[256,8192]{1,0:T(8,128)(2,1)S(1)}, bf16[256,8192]{1,0:T(8,128)(2,1)}, u32[]{:S(2)}) %copy-start) | copy-done | bytes 4194328
  4.4 2.4 %collective-permute-start.4 = (bf16[512,1024]{1,0:T(8,128)(2,1)S(1)}, bf16[512,1024]{1,0:T(8,128)(2,1)S(1)}, u32[]{:S(2)}, u32[]{:S(2)}) collective-permute-start(bf16[512,1024]{1,0:T(8,128)(2,1)S(1)} %constant_dynamic-update-slice_fusion), channel_id=1, source_target_pairs={{0,4},{1,13},{4,0},{5,9},{8,12},{9,5},{12,8},{13,1},{2,6},{3,15},{... | collective-permute-start | bytes 3145736 | tf_op jit(solution)/shard_map/ppermute | solution.py:25
  8.9 2.4 %collective-permute-start.2 = (bf16[512,512]{1,0:T(8,128)(2,1)S(1)}, bf16[512,512]{1,0:T(8,128)(2,1)S(1)}, u32[]{:S(2)}, u32[]{:S(2)}) collective-permute-start(bf16[512,512]{1,0:T(8,128)(2,1)S(1)} %get-tuple-element.35), channel_id=1, source_target_pairs={{0,4},{1,13},{4,0},{5,9},{8,12},{9,5},{12,8},{13,1},{2,6},{3,15},{... | collective-permute-start | bytes 1572872 | tf_op jit(solution)/shard_map/ppermute | solution.py:25
  16.7 2.8 %collective-permute-done.4 = bf16[512,1024]{1,0:T(8,128)(2,1)S(1)} collective-permute-done((bf16[512,1024]{1,0:T(8,128)(2,1)S(1)}, bf16[512,1024]{1,0:T(8,128)(2,1)S(1)}, u32[]{:S(2)}, u32[]{:S(2)}) %collective-permute-start.4) | collective-permute-done | bytes 1048608 | tf_op jit(solution)/shard_map/ppermute | solution.py:25
  19.5 2.0 %collective-permute-done.5 = bf16[512,1024]{1,0:T(8,128)(2,1)S(1)} collective-permute-done((bf16[512,1024]{1,0:T(8,128)(2,1)S(1)}, bf16[512,1024]{1,0:T(8,128)(2,1)S(1)}, u32[]{:S(2)}, u32[]{:S(2)}) %collective-permute-start.5) | collective-permute-done | bytes 1048608 | tf_op jit(solution)/shard_map/ppermute | solution.py:25
  21.5 3.6 %collective-permute-done.2 = bf16[512,512]{1,0:T(8,128)(2,1)S(1)} collective-permute-done((bf16[512,512]{1,0:T(8,128)(2,1)S(1)}, bf16[512,512]{1,0:T(8,128)(2,1)S(1)}, u32[]{:S(2)}, u32[]{:S(2)}) %collective-permute-start.2) | collective-permute-done | bytes 524320 | tf_op jit(solution)/shard_map/ppermute | solution.py:25
  25.1 2.0 %collective-permute-done.3 = bf16[512,512]{1,0:T(8,128)(2,1)S(1)} collective-permute-done((bf16[512,512]{1,0:T(8,128)(2,1)S(1)}, bf16[512,512]{1,0:T(8,128)(2,1)S(1)}, u32[]{:S(2)}, u32[]{:S(2)}) %collective-permute-start.3) | collective-permute-done | bytes 524320 | tf_op jit(solution)/shard_map/ppermute | solution.py:25
  31.5 2.3 %collective-permute-start.11 = (f16[512,1024]{1,0:T(8,128)(2,1)S(1)}, f16[512,1024]{1,0:T(8,128)(2,1)S(1)}, u32[]{:S(2)}, u32[]{:S(2)}) collective-permute-start(f16[512,1024]{1,0:T(8,128)(2,1)S(1)} %multiply_convert_fusion), channel_id=1, source_target_pairs={{0,48},{1,17},{16,32},{17,1},{32,16},{33,49},{48,0},{49,33},{2,50}... | collective-permute-start | bytes 3145736 | tf_op jit(solution)/shard_map/ppermute | solution.py:25
  33.8 7.0 %collective-permute-done.6 = bf16[512,512]{1,0:T(8,128)(2,1)S(1)} collective-permute-done((bf16[512,512]{1,0:T(8,128)(2,1)S(1)}, bf16[512,512]{1,0:T(8,128)(2,1)S(1)}, u32[]{:S(2)}, u32[]{:S(2)}) %collective-permute-start.6) | collective-permute-done | bytes 524320 | tf_op jit(solution)/shard_map/ppermute | solution.py:25
  42.8 3.1 %collective-permute-done.7 = f16[512,1024]{1,0:T(8,128)(2,1)S(1)} collective-permute-done((f16[512,1024]{1,0:T(8,128)(2,1)S(1)}, f16[512,1024]{1,0:T(8,128)(2,1)S(1)}, u32[]{:S(2)}, u32[]{:S(2)}) %collective-permute-start.7) | collective-permute-done | bytes 1048608 | tf_op jit(solution)/shard_map/ppermute | solution.py:25
  47.2 4.1 %collective-permute-done.11 = f16[512,1024]{1,0:T(8,128)(2,1)S(1)} collective-permute-done((f16[512,1024]{1,0:T(8,128)(2,1)S(1)}, f16[512,1024]{1,0:T(8,128)(2,1)S(1)}, u32[]{:S(2)}, u32[]{:S(2)}) %collective-permute-start.11) | collective-permute-done | bytes 1048608 | tf_op jit(solution)/shard_map/ppermute | solution.py:25
  52.3 3.5 %collective-permute-done.8 = f16[256,1024]{1,0:T(8,128)(2,1)S(1)} collective-permute-done((f16[256,1024]{1,0:T(8,128)(2,1)S(1)}, f16[256,1024]{1,0:T(8,128)(2,1)S(1)}, u32[]{:S(2)}, u32[]{:S(2)}) %collective-permute-start.8) | collective-permute-done | bytes 524320 | tf_op jit(solution)/shard_map/ppermute | solution.py:25
  56.1 3.0 %collective-permute-start.9 = (f16[128,1024]{1,0:T(8,128)(2,1)S(1)}, f16[128,1024]{1,0:T(8,128)(2,1)S(1)}, u32[]{:S(2)}, u32[]{:S(2)}) collective-permute-start(f16[128,1024]{1,0:T(8,128)(2,1)S(1)} %fusion.8), channel_id=1, source_target_pairs={{0,48},{1,17},{16,32},{17,1},{32,16},{33,49},{48,0},{49,33},{2,50}... | collective-permute-start | bytes 786440 | tf_op jit(solution)/shard_map/ppermute | solution.py:25
  59.2 1.9 %collective-permute-done.12 = f16[256,1024]{1,0:T(8,128)(2,1)S(1)} collective-permute-done((f16[256,1024]{1,0:T(8,128)(2,1)S(1)}, f16[256,1024]{1,0:T(8,128)(2,1)S(1)}, u32[]{:S(2)}, u32[]{:S(2)}) %collective-permute-start.12) | collective-permute-done | bytes 524320 | tf_op jit(solution)/shard_map/ppermute | solution.py:25
  62.0 1.8 %collective-permute-done.9 = f16[128,1024]{1,0:T(8,128)(2,1)S(1)} collective-permute-done((f16[128,1024]{1,0:T(8,128)(2,1)S(1)}, f16[128,1024]{1,0:T(8,128)(2,1)S(1)}, u32[]{:S(2)}, u32[]{:S(2)}) %collective-permute-start.9) | collective-permute-done | bytes 262176 | tf_op jit(solution)/shard_map/ppermute | solution.py:25
  63.9 4.0 %collective-permute-done.13 = f16[128,1024]{1,0:T(8,128)(2,1)S(1)} collective-permute-done((f16[128,1024]{1,0:T(8,128)(2,1)S(1)}, f16[128,1024]{1,0:T(8,128)(2,1)S(1)}, u32[]{:S(2)}, u32[]{:S(2)}) %collective-permute-start.13) | collective-permute-done | bytes 262176 | tf_op jit(solution)/shard_map/ppermute | solution.py:25
  70.5 2.9 %collective-permute-done.14 = f16[256,256]{1,0:T(8,128)(2,1)S(1)} collective-permute-done((f16[256,256]{1,0:T(8,128)(2,1)S(1)}, f16[256,256]{1,0:T(8,128)(2,1)S(1)}, u32[]{:S(2)}, u32[]{:S(2)}) %collective-permute-start.14) | collective-permute-done | bytes 131104 | tf_op jit(solution)/shard_map/ppermute | solution.py:191
  73.3 3.5 %collective-permute-done.16 = f16[256,256]{1,0:T(8,128)(2,1)S(1)} collective-permute-done((f16[256,256]{1,0:T(8,128)(2,1)S(1)}, f16[256,256]{1,0:T(8,128)(2,1)S(1)}, u32[]{:S(2)}, u32[]{:S(2)}) %collective-permute-start.16) | collective-permute-done | bytes 131104 | tf_op jit(solution)/shard_map/ppermute | solution.py:191
  77.8 9.0 %collective-permute-done.17 = f32[256,256]{1,0:T(8,128)S(1)} collective-permute-done((f32[256,256]{1,0:T(8,128)S(1)}, f32[256,256]{1,0:T(8,128)S(1)}, u32[]{:S(2)}, u32[]{:S(2)}) %collective-permute-start.17) | collective-permute-done | bytes 262176 | tf_op jit(solution)/shard_map/ppermute | solution.py:25
  86.8 2.7 %collective-permute-start.18 = (f32[128,256]{1,0:T(8,128)S(1)}, f32[128,256]{1,0:T(8,128)S(1)}, u32[]{:S(2)}, u32[]{:S(2)}) collective-permute-start(f32[128,256]{1,0:T(8,128)S(1)} %slice_add_fusion.7), channel_id=1, source_target_pairs={{0,192},{1,65},{64,128},{65,1},{128,64},{129,193},{192,0},{193,129... | collective-permute-start | bytes 393224 | tf_op jit(solution)/shard_map/ppermute | solution.py:25
  89.5 5.8 %collective-permute-done.18 = f32[128,256]{1,0:T(8,128)S(1)} collective-permute-done((f32[128,256]{1,0:T(8,128)S(1)}, f32[128,256]{1,0:T(8,128)S(1)}, u32[]{:S(2)}, u32[]{:S(2)}) %collective-permute-start.18) | collective-permute-done | bytes 131104 | tf_op jit(solution)/shard_map/ppermute | solution.py:25
  96.9 2.5 %collective-permute-start.19 = (bf16[128,256]{1,0:T(8,128)(2,1)S(1)}, bf16[128,256]{1,0:T(8,128)(2,1)S(1)}, u32[]{:S(2)}, u32[]{:S(2)}) collective-permute-start(bf16[128,256]{1,0:T(8,128)(2,1)S(1)} %get-tuple-element.53), channel_id=1, source_target_pairs={{0,192},{1,65},{64,128},{65,1},{128,64},{129,193},{192,0},{193,129... | collective-permute-start | bytes 196616 | tf_op jit(solution)/shard_map/ppermute | solution.py:25
  99.3 3.4 %collective-permute-start.20 = (bf16[128,256]{1,0:T(8,128)(2,1)S(1)}, bf16[128,256]{1,0:T(8,128)(2,1)S(1)}, u32[]{:S(2)}, u32[]{:S(2)}) collective-permute-start(bf16[128,256]{1,0:T(8,128)(2,1)S(1)} %get-tuple-element.53), channel_id=1, source_target_pairs={{0,128},{1,129},{64,192},{65,193},{128,0},{129,1},{192,64},{193,65... | collective-permute-start | bytes 196616 | tf_op jit(solution)/shard_map/ppermute | solution.py:25
  103.0 2.9 %collective-permute-start.23 = (bf16[256,256]{1,0:T(8,128)(2,1)S(1)}, bf16[256,256]{1,0:T(8,128)(2,1)S(1)}, u32[]{:S(2)}, u32[]{:S(2)}) collective-permute-start(bf16[256,256]{1,0:T(8,128)(2,1)S(1)} %pad_maximum_fusion.4), channel_id=1, source_target_pairs={{0,48},{1,17},{16,32},{17,1},{32,16},{33,49},{48,0},{49,33},{2,50}... | collective-permute-start | bytes 393224 | tf_op jit(solution)/shard_map/ppermute | solution.py:25
  109.1 2.5 %collective-permute-start.25 = (bf16[256,256]{1,0:T(8,128)(2,1)S(1)}, bf16[256,256]{1,0:T(8,128)(2,1)S(1)}, u32[]{:S(2)}, u32[]{:S(2)}) collective-permute-start(bf16[256,256]{1,0:T(8,128)(2,1)S(1)} %pad_maximum_fusion.3), channel_id=1, source_target_pairs={{0,4},{1,13},{4,0},{5,9},{8,12},{9,5},{12,8},{13,1},{2,6},{3,15},{... | collective-permute-start | bytes 393224 | tf_op jit(solution)/shard_map/ppermute | solution.py:25
  115.0 2.5 %collective-permute-start.32 = (bf16[1024,256]{1,0:T(8,128)(2,1)S(1)}, bf16[1024,256]{1,0:T(8,128)(2,1)S(1)}, u32[]{:S(2)}, u32[]{:S(2)}) collective-permute-start(bf16[1024,256]{1,0:T(8,128)(2,1)S(1)} %constant_dynamic-update-slice_fusion.2.refs_0_), channel_id=1, source_target_pairs={{0,4},{1,13},{4,0},{5,9},{8,12},{9,5},{12,8},{13,1},{2,6},{3,15},{... | collective-permute-start | bytes 1572872 | tf_op jit(solution)/shard_map/ppermute | solution.py:25
  117.5 1.8 %collective-permute-start.34 = (bf16[1024,256]{1,0:T(8,128)(2,1)S(1)}, bf16[1024,256]{1,0:T(8,128)(2,1)S(1)}, u32[]{:S(2)}, u32[]{:S(2)}) collective-permute-start(bf16[1024,256]{1,0:T(8,128)(2,1)S(1)} %constant_dynamic-update-slice_fusion.2.refs_0_), channel_id=1, source_target_pairs={{0,12},{1,5},{4,8},{5,1},{8,4},{9,13},{12,0},{13,9},{2,14},{3,7},{... | collective-permute-start | bytes 1572872 | tf_op jit(solution)/shard_map/ppermute | solution.py:25
  121.0 2.1 %collective-permute-start.30 = (bf16[1024,256]{1,0:T(8,128)(2,1)S(1)}, bf16[1024,256]{1,0:T(8,128)(2,1)S(1)}, u32[]{:S(2)}, u32[]{:S(2)}) collective-permute-start(bf16[1024,256]{1,0:T(8,128)(2,1)S(1)} %constant_dynamic-update-slice_fusion.7.refs_3_), channel_id=1, source_target_pairs={{0,48},{1,17},{16,32},{17,1},{32,16},{33,49},{48,0},{49,33},{2,50}... | collective-permute-start | bytes 1572872 | tf_op jit(solution)/shard_map/ppermute | solution.py:25
  123.1 6.1 %collective-permute-done.32.refs_1_ = bf16[1024,256]{1,0:T(8,128)(2,1)S(1)} collective-permute-done((bf16[1024,256]{1,0:T(8,128)(2,1)S(1)}, bf16[1024,256]{1,0:T(8,128)(2,1)S(1)}, u32[]{:S(2)}, u32[]{:S(2)}) %collective-permute-start.32) | collective-permute-done | bytes 524320 | tf_op jit(solution)/shard_map/ppermute | solution.py:25
  129.1 2.8 %collective-permute-start.33 = (bf16[512,256]{1,0:T(8,128)(2,1)S(1)}, bf16[512,256]{1,0:T(8,128)(2,1)S(1)}, u32[]{:S(2)}, u32[]{:S(2)}) collective-permute-start(bf16[512,256]{1,0:T(8,128)(2,1)S(1)} %slice.138), channel_id=1, source_target_pairs={{0,12},{1,5},{4,8},{5,1},{8,4},{9,13},{12,0},{13,9},{2,14},{3,7},{... | collective-permute-start | bytes 786440 | tf_op jit(solution)/shard_map/ppermute | solution.py:25
  134.7 2.2 %shard_map.89.refs_2_ = bf16[8192,256]{1,0:T(8,128)(2,1)} custom-call(s32[4]{0:T(128)S(1)} %pad_add_fusion.where_ref, bf16[1024,256]{1,0:T(8,128)(2,1)S(1)} %constant_dynamic-update-slice_fusion.2.refs_0_, bf16[1024,256]{1,0:T(8,128)(2,1)S(1)} %collective-permute-done.32.refs_1_, bf16[1024,256]{1,0:T(8,128)(2,1)S(1)} %collective-permute-done.34.refs_2_, ...), custom_call_target="tpu_custom_call" | custom-call | bytes 6291456 | tf_op jit(solution)/shard_map/pallas_call | solution.py:117
  136.9 1.8 %collective-permute-done.33.refs_0_ = bf16[512,256]{1,0:T(8,128)(2,1)S(1)} collective-permute-done((bf16[512,256]{1,0:T(8,128)(2,1)S(1)}, bf16[512,256]{1,0:T(8,128)(2,1)S(1)}, u32[]{:S(2)}, u32[]{:S(2)}) %collective-permute-start.33) | collective-permute-done | bytes 262176 | tf_op jit(solution)/shard_map/ppermute | solution.py:25
  (103 shorter events, 38.4 us)
Async XLA Ops:
  4.4 15.1 %collective-permute-start.4 = (bf16[512,1024]{1,0:T(8,128)(2,1)S(1)}, bf16[512,1024]{1,0:T(8,128)(2,1)S(1)}, u32[]{:S(2)}, u32[]{:S(2)}) collective-permute-start(bf16[512,1024]{1,0:T(8,128)(2,1)S(1)} %constant_dynamic-update-slice_fusion), channel_id=1, source_target_pairs={{0,4},{1,13},{4,0},{5,9},{8,12},{9,5},{12,8},{13,1},{2,6},{3,15},{... | collective-permute-start | bytes 3145736 | tf_op jit(solution)/shard_map/ppermute | solution.py:25
  6.7 14.8 %collective-permute-start.5 = (bf16[512,1024]{1,0:T(8,128)(2,1)S(1)}, bf16[512,1024]{1,0:T(8,128)(2,1)S(1)}, u32[]{:S(2)}, u32[]{:S(2)}) collective-permute-start(bf16[512,1024]{1,0:T(8,128)(2,1)S(1)} %constant_dynamic-update-slice_fusion), channel_id=1, source_target_pairs={{0,16},{1,49},{16,0},{17,33},{32,48},{33,17},{48,32},{49,1},{2,18}... | collective-permute-start | bytes 3145736 | tf_op jit(solution)/shard_map/ppermute | solution.py:25
  8.9 16.2 %collective-permute-start.2 = (bf16[512,512]{1,0:T(8,128)(2,1)S(1)}, bf16[512,512]{1,0:T(8,128)(2,1)S(1)}, u32[]{:S(2)}, u32[]{:S(2)}) collective-permute-start(bf16[512,512]{1,0:T(8,128)(2,1)S(1)} %get-tuple-element.35), channel_id=1, source_target_pairs={{0,4},{1,13},{4,0},{5,9},{8,12},{9,5},{12,8},{13,1},{2,6},{3,15},{... | collective-permute-start | bytes 1572872 | tf_op jit(solution)/shard_map/ppermute | solution.py:25
  11.3 15.9 %collective-permute-start.3 = (bf16[512,512]{1,0:T(8,128)(2,1)S(1)}, bf16[512,512]{1,0:T(8,128)(2,1)S(1)}, u32[]{:S(2)}, u32[]{:S(2)}) collective-permute-start(bf16[512,512]{1,0:T(8,128)(2,1)S(1)} %get-tuple-element.36), channel_id=1, source_target_pairs={{0,16},{1,49},{16,0},{17,33},{32,48},{33,17},{48,32},{49,1},{2,18}... | collective-permute-start | bytes 1572872 | tf_op jit(solution)/shard_map/ppermute | solution.py:25
  27.1 13.7 %collective-permute-start.6 = (bf16[512,512]{1,0:T(8,128)(2,1)S(1)}, bf16[512,512]{1,0:T(8,128)(2,1)S(1)}, u32[]{:S(2)}, u32[]{:S(2)}) collective-permute-start(bf16[512,512]{1,0:T(8,128)(2,1)S(1)} %get-tuple-element.39), channel_id=1, source_target_pairs={{0,4},{1,13},{4,0},{5,9},{8,12},{9,5},{12,8},{13,1},{2,6},{3,15},{... | collective-permute-start | bytes 1572872 | tf_op jit(solution)/shard_map/ppermute | solution.py:25
  28.0 17.9 %collective-permute-start.7 = (f16[512,1024]{1,0:T(8,128)(2,1)S(1)}, f16[512,1024]{1,0:T(8,128)(2,1)S(1)}, u32[]{:S(2)}, u32[]{:S(2)}) collective-permute-start(f16[512,1024]{1,0:T(8,128)(2,1)S(1)} %multiply_convert_fusion.1), channel_id=1, source_target_pairs={{0,12},{1,5},{4,8},{5,1},{8,4},{9,13},{12,0},{13,9},{2,14},{3,7},{... | collective-permute-start | bytes 3145736 | tf_op jit(solution)/shard_map/ppermute | solution.py:25
  29.2 12.9 %collective-permute-start.10 = (bf16[512,512]{1,0:T(8,128)(2,1)S(1)}, bf16[512,512]{1,0:T(8,128)(2,1)S(1)}, u32[]{:S(2)}, u32[]{:S(2)}) collective-permute-start(bf16[512,512]{1,0:T(8,128)(2,1)S(1)} %get-tuple-element.44), channel_id=1, source_target_pairs={{0,16},{1,49},{16,0},{17,33},{32,48},{33,17},{48,32},{49,1},{2,18}... | collective-permute-start | bytes 1572872 | tf_op jit(solution)/shard_map/ppermute | solution.py:25
  31.5 19.8 %collective-permute-start.11 = (f16[512,1024]{1,0:T(8,128)(2,1)S(1)}, f16[512,1024]{1,0:T(8,128)(2,1)S(1)}, u32[]{:S(2)}, u32[]{:S(2)}) collective-permute-start(f16[512,1024]{1,0:T(8,128)(2,1)S(1)} %multiply_convert_fusion), channel_id=1, source_target_pairs={{0,48},{1,17},{16,32},{17,1},{32,16},{33,49},{48,0},{49,33},{2,50}... | collective-permute-start | bytes 3145736 | tf_op jit(solution)/shard_map/ppermute | solution.py:25
  46.4 9.4 %collective-permute-start.8 = (f16[256,1024]{1,0:T(8,128)(2,1)S(1)}, f16[256,1024]{1,0:T(8,128)(2,1)S(1)}, u32[]{:S(2)}, u32[]{:S(2)}) collective-permute-start(f16[256,1024]{1,0:T(8,128)(2,1)S(1)} %fusion.4), channel_id=1, source_target_pairs={{0,16},{1,49},{16,0},{17,33},{32,48},{33,17},{48,32},{49,1},{2,18}... | collective-permute-start | bytes 1572872 | tf_op jit(solution)/shard_map/ppermute | solution.py:25
  51.8 9.3 %collective-permute-start.12 = (f16[256,1024]{1,0:T(8,128)(2,1)S(1)}, f16[256,1024]{1,0:T(8,128)(2,1)S(1)}, u32[]{:S(2)}, u32[]{:S(2)}) collective-permute-start(f16[256,1024]{1,0:T(8,128)(2,1)S(1)} %fusion.1), channel_id=1, source_target_pairs={{0,4},{1,13},{4,0},{5,9},{8,12},{9,5},{12,8},{13,1},{2,6},{3,15},{... | collective-permute-start | bytes 1572872 | tf_op jit(solution)/shard_map/ppermute | solution.py:25
  56.1 7.7 %collective-permute-start.9 = (f16[128,1024]{1,0:T(8,128)(2,1)S(1)}, f16[128,1024]{1,0:T(8,128)(2,1)S(1)}, u32[]{:S(2)}, u32[]{:S(2)}) collective-permute-start(f16[128,1024]{1,0:T(8,128)(2,1)S(1)} %fusion.8), channel_id=1, source_target_pairs={{0,48},{1,17},{16,32},{17,1},{32,16},{33,49},{48,0},{49,33},{2,50}... | collective-permute-start | bytes 786440 | tf_op jit(solution)/shard_map/ppermute | solution.py:25
  61.4 6.5 %collective-permute-start.13 = (f16[128,1024]{1,0:T(8,128)(2,1)S(1)}, f16[128,1024]{1,0:T(8,128)(2,1)S(1)}, u32[]{:S(2)}, u32[]{:S(2)}) collective-permute-start(f16[128,1024]{1,0:T(8,128)(2,1)S(1)} %fusion.7), channel_id=1, source_target_pairs={{0,12},{1,5},{4,8},{5,1},{8,4},{9,13},{12,0},{13,9},{2,14},{3,7},{... | collective-permute-start | bytes 786440 | tf_op jit(solution)/shard_map/ppermute | solution.py:25
  68.1 8.7 %collective-permute-start.15 = (f32[256,256]{1,0:T(8,128)S(1)}, f32[256,256]{1,0:T(8,128)S(1)}, u32[]{:S(2)}, u32[]{:S(2)}) collective-permute-start(f32[256,256]{1,0:T(8,128)S(1)} %slice_select_fusion), channel_id=1, source_target_pairs={{0,1},{1,0},{2,3},{3,2},{4,5},{5,4},{6,7},{7,6},{8,9},{9,8},{10,11... | collective-permute-start | bytes 786440 | tf_op jit(solution)/shard_map/ppermute | solution.py:29
  68.7 8.1 %collective-permute-start.16 = (f16[256,256]{1,0:T(8,128)(2,1)S(1)}, f16[256,256]{1,0:T(8,128)(2,1)S(1)}, u32[]{:S(2)}, u32[]{:S(2)}) collective-permute-start(f16[256,256]{1,0:T(8,128)(2,1)S(1)} %get-tuple-element.64), channel_id=1, source_target_pairs={{0,3},{1,194},{2,1},{3,64},{64,67},{65,2},{66,65},{67,128},{128,13... | collective-permute-start | bytes 393224 | tf_op jit(solution)/shard_map/ppermute | solution.py:191
  77.1 9.7 %collective-permute-start.17 = (f32[256,256]{1,0:T(8,128)S(1)}, f32[256,256]{1,0:T(8,128)S(1)}, u32[]{:S(2)}, u32[]{:S(2)}) collective-permute-start(f32[256,256]{1,0:T(8,128)S(1)} %pad_maximum_fusion.2), channel_id=1, source_target_pairs={{0,64},{1,193},{64,0},{65,129},{128,192},{129,65},{192,128},{193,1... | collective-permute-start | bytes 786440 | tf_op jit(solution)/shard_map/ppermute | solution.py:25
  86.8 8.6 %collective-permute-start.18 = (f32[128,256]{1,0:T(8,128)S(1)}, f32[128,256]{1,0:T(8,128)S(1)}, u32[]{:S(2)}, u32[]{:S(2)}) collective-permute-start(f32[128,256]{1,0:T(8,128)S(1)} %slice_add_fusion.7), channel_id=1, source_target_pairs={{0,192},{1,65},{64,128},{65,1},{128,64},{129,193},{192,0},{193,129... | collective-permute-start | bytes 393224 | tf_op jit(solution)/shard_map/ppermute | solution.py:25
  96.2 6.5 %collective-permute-start.21 = (bf16[128,256]{1,0:T(8,128)(2,1)S(1)}, bf16[128,256]{1,0:T(8,128)(2,1)S(1)}, u32[]{:S(2)}, u32[]{:S(2)}) collective-permute-start(bf16[128,256]{1,0:T(8,128)(2,1)S(1)} %get-tuple-element.53), channel_id=1, source_target_pairs={{0,64},{1,193},{64,0},{65,129},{128,192},{129,65},{192,128},{193,1... | collective-permute-start | bytes 196616 | tf_op jit(solution)/shard_map/ppermute | solution.py:25
  96.9 10.4 %collective-permute-start.19 = (bf16[128,256]{1,0:T(8,128)(2,1)S(1)}, bf16[128,256]{1,0:T(8,128)(2,1)S(1)}, u32[]{:S(2)}, u32[]{:S(2)}) collective-permute-start(bf16[128,256]{1,0:T(8,128)(2,1)S(1)} %get-tuple-element.53), channel_id=1, source_target_pairs={{0,192},{1,65},{64,128},{65,1},{128,64},{129,193},{192,0},{193,129... | collective-permute-start | bytes 196616 | tf_op jit(solution)/shard_map/ppermute | solution.py:25
  99.3 8.3 %collective-permute-start.20 = (bf16[128,256]{1,0:T(8,128)(2,1)S(1)}, bf16[128,256]{1,0:T(8,128)(2,1)S(1)}, u32[]{:S(2)}, u32[]{:S(2)}) collective-permute-start(bf16[128,256]{1,0:T(8,128)(2,1)S(1)} %get-tuple-element.53), channel_id=1, source_target_pairs={{0,128},{1,129},{64,192},{65,193},{128,0},{129,1},{192,64},{193,65... | collective-permute-start | bytes 196616 | tf_op jit(solution)/shard_map/ppermute | solution.py:25
  102.7 6.4 %collective-permute-start.22 = (bf16[256,256]{1,0:T(8,128)(2,1)S(1)}, bf16[256,256]{1,0:T(8,128)(2,1)S(1)}, u32[]{:S(2)}, u32[]{:S(2)}) collective-permute-start(bf16[256,256]{1,0:T(8,128)(2,1)S(1)} %pad_maximum_fusion.4), channel_id=1, source_target_pairs={{0,16},{1,49},{16,0},{17,33},{32,48},{33,17},{48,32},{49,1},{2,18}... | collective-permute-start | bytes 393224 | tf_op jit(solution)/shard_map/ppermute | solution.py:25
  103.0 10.9 %collective-permute-start.23 = (bf16[256,256]{1,0:T(8,128)(2,1)S(1)}, bf16[256,256]{1,0:T(8,128)(2,1)S(1)}, u32[]{:S(2)}, u32[]{:S(2)}) collective-permute-start(bf16[256,256]{1,0:T(8,128)(2,1)S(1)} %pad_maximum_fusion.4), channel_id=1, source_target_pairs={{0,48},{1,17},{16,32},{17,1},{32,16},{33,49},{48,0},{49,33},{2,50}... | collective-permute-start | bytes 393224 | tf_op jit(solution)/shard_map/ppermute | solution.py:25
  105.9 8.0 %collective-permute-start.24 = (bf16[256,256]{1,0:T(8,128)(2,1)S(1)}, bf16[256,256]{1,0:T(8,128)(2,1)S(1)}, u32[]{:S(2)}, u32[]{:S(2)}) collective-permute-start(bf16[256,256]{1,0:T(8,128)(2,1)S(1)} %pad_maximum_fusion.4), channel_id=1, source_target_pairs={{0,32},{1,33},{16,48},{17,49},{32,0},{33,1},{48,16},{49,17},{2,34}... | collective-permute-start | bytes 393224 | tf_op jit(solution)/shard_map/ppermute | solution.py:25
  111.7 8.3 %collective-permute-start.26 = (bf16[256,256]{1,0:T(8,128)(2,1)S(1)}, bf16[256,256]{1,0:T(8,128)(2,1)S(1)}, u32[]{:S(2)}, u32[]{:S(2)}) collective-permute-start(bf16[256,256]{1,0:T(8,128)(2,1)S(1)} %pad_maximum_fusion.3), channel_id=1, source_target_pairs={{0,12},{1,5},{4,8},{5,1},{8,4},{9,13},{12,0},{13,9},{2,14},{3,7},{... | collective-permute-start | bytes 393224 | tf_op jit(solution)/shard_map/ppermute | solution.py:25
  113.0 7.9 %collective-permute-start.27 = (bf16[256,256]{1,0:T(8,128)(2,1)S(1)}, bf16[256,256]{1,0:T(8,128)(2,1)S(1)}, u32[]{:S(2)}, u32[]{:S(2)}) collective-permute-start(bf16[256,256]{1,0:T(8,128)(2,1)S(1)} %pad_maximum_fusion.3), channel_id=1, source_target_pairs={{0,8},{1,9},{4,12},{5,13},{8,0},{9,1},{12,4},{13,5},{2,10},{3,11},... | collective-permute-start | bytes 393224 | tf_op jit(solution)/shard_map/ppermute | solution.py:25
  115.0 14.1 %collective-permute-start.32 = (bf16[1024,256]{1,0:T(8,128)(2,1)S(1)}, bf16[1024,256]{1,0:T(8,128)(2,1)S(1)}, u32[]{:S(2)}, u32[]{:S(2)}) collective-permute-start(bf16[1024,256]{1,0:T(8,128)(2,1)S(1)} %constant_dynamic-update-slice_fusion.2.refs_0_), channel_id=1, source_target_pairs={{0,4},{1,13},{4,0},{5,9},{8,12},{9,5},{12,8},{13,1},{2,6},{3,15},{... | collective-permute-start | bytes 1572872 | tf_op jit(solution)/shard_map/ppermute | solution.py:25
  117.5 14.4 %collective-permute-start.34 = (bf16[1024,256]{1,0:T(8,128)(2,1)S(1)}, bf16[1024,256]{1,0:T(8,128)(2,1)S(1)}, u32[]{:S(2)}, u32[]{:S(2)}) collective-permute-start(bf16[1024,256]{1,0:T(8,128)(2,1)S(1)} %constant_dynamic-update-slice_fusion.2.refs_0_), channel_id=1, source_target_pairs={{0,12},{1,5},{4,8},{5,1},{8,4},{9,13},{12,0},{13,9},{2,14},{3,7},{... | collective-permute-start | bytes 1572872 | tf_op jit(solution)/shard_map/ppermute | solution.py:25
  120.9 12.0 %collective-permute-start.28 = (bf16[1024,256]{1,0:T(8,128)(2,1)S(1)}, bf16[1024,256]{1,0:T(8,128)(2,1)S(1)}, u32[]{:S(2)}, u32[]{:S(2)}) collective-permute-start(bf16[1024,256]{1,0:T(8,128)(2,1)S(1)} %constant_dynamic-update-slice_fusion.7.refs_3_), channel_id=1, source_target_pairs={{0,16},{1,49},{16,0},{17,33},{32,48},{33,17},{48,32},{49,1},{2,18}... | collective-permute-start | bytes 1572872 | tf_op jit(solution)/shard_map/ppermute | solution.py:25
  121.0 13.1 %collective-permute-start.30 = (bf16[1024,256]{1,0:T(8,128)(2,1)S(1)}, bf16[1024,256]{1,0:T(8,128)(2,1)S(1)}, u32[]{:S(2)}, u32[]{:S(2)}) collective-permute-start(bf16[1024,256]{1,0:T(8,128)(2,1)S(1)} %constant_dynamic-update-slice_fusion.7.refs_3_), channel_id=1, source_target_pairs={{0,48},{1,17},{16,32},{17,1},{32,16},{33,49},{48,0},{49,33},{2,50}... | collective-permute-start | bytes 1572872 | tf_op jit(solution)/shard_map/ppermute | solution.py:25
  129.1 9.5 %collective-permute-start.33 = (bf16[512,256]{1,0:T(8,128)(2,1)S(1)}, bf16[512,256]{1,0:T(8,128)(2,1)S(1)}, u32[]{:S(2)}, u32[]{:S(2)}) collective-permute-start(bf16[512,256]{1,0:T(8,128)(2,1)S(1)} %slice.138), channel_id=1, source_target_pairs={{0,12},{1,5},{4,8},{5,1},{8,4},{9,13},{12,0},{13,9},{2,14},{3,7},{... | collective-permute-start | bytes 786440 | tf_op jit(solution)/shard_map/ppermute | solution.py:25
  132.0 6.7 %collective-permute-start.35 = (bf16[512,256]{1,0:T(8,128)(2,1)S(1)}, bf16[512,256]{1,0:T(8,128)(2,1)S(1)}, u32[]{:S(2)}, u32[]{:S(2)}) collective-permute-start(bf16[512,256]{1,0:T(8,128)(2,1)S(1)} %slice.139), channel_id=1, source_target_pairs={{0,4},{1,13},{4,0},{5,9},{8,12},{9,5},{12,8},{13,1},{2,6},{3,15},{... | collective-permute-start | bytes 786440 | tf_op jit(solution)/shard_map/ppermute | solution.py:25
  132.9 7.7 %collective-permute-start.29 = (bf16[512,256]{1,0:T(8,128)(2,1)S(1)}, bf16[512,256]{1,0:T(8,128)(2,1)S(1)}, u32[]{:S(2)}, u32[]{:S(2)}) collective-permute-start(bf16[512,256]{1,0:T(8,128)(2,1)S(1)} %slice.136), channel_id=1, source_target_pairs={{0,48},{1,17},{16,32},{17,1},{32,16},{33,49},{48,0},{49,33},{2,50}... | collective-permute-start | bytes 786440 | tf_op jit(solution)/shard_map/ppermute | solution.py:25
  134.1 6.5 %collective-permute-start.31 = (bf16[512,256]{1,0:T(8,128)(2,1)S(1)}, bf16[512,256]{1,0:T(8,128)(2,1)S(1)}, u32[]{:S(2)}, u32[]{:S(2)}) collective-permute-start(bf16[512,256]{1,0:T(8,128)(2,1)S(1)} %slice.137), channel_id=1, source_target_pairs={{0,16},{1,49},{16,0},{17,33},{32,48},{33,17},{48,32},{49,1},{2,18}... | collective-permute-start | bytes 786440 | tf_op jit(solution)/shard_map/ppermute | solution.py:25
  (9 other events, 77.3 us)

commit v7 on v6

--- a/solution.py
+++ b/solution.py
@@ -151,7 +151,7 @@
     sent, rest = arrange(acts, peer, where, 3), arrange(acts, peer, where, 2)
     kept = [arrange(acts, peer, where, i) for i in range(2)]
     far = [swap(sent[p], FIRST[p], NEAR) for p in parts]
-    far, far_grad, rest = lax.optimization_barrier((far, far_grad, rest))
+    far_grad, rest = lax.optimization_barrier((far_grad, rest))
     far_acts = [(swap(rest[p], FIRST[p], NEAR), far[p]) for p in parts]
 
     near_sums = [[dot(kept[i][p], chip_grad) for i in range(2)] for p in parts]
@@ -213,10 +213,9 @@
     z = [own] + [swap(own, "zh", by) for by in every]
     pieces = [jnp.concatenate(z[:2], 0), jnp.concatenate(z[2:], 0)]
     far = [swap(pieces[0], SECOND[0], by) for by in every]
-    pieces[1], far[0] = lax.optimization_barrier((pieces[1], far[0]))
     pieces[0] = jnp.concatenate([pieces[0]] + far, 0)
     far = [swap(pieces[1], SECOND[1], by) for by in every]
-    pieces[0], far[0] = lax.optimization_barrier((pieces[0], far[0]))
+    pieces[0], far[2] = lax.optimization_barrier((pieces[0], far[2]))
     pieces[1] = jnp.concatenate([pieces[1]] + far, 0)
     near = [swap(pieces[p], FIRST[p], GATHER_NEAR) for p in parts]
     following = [swap(pieces[p], FIRST[p], GATHER_NEXT) for p in parts]

time: 143 us -> 145 us (1.014)
    ppermute x2, starting transfers between devices: 2.19 us -> 3.74 us  [along_z(): return lambda v: lax.ppermute(v, ('zh', 'zl', 'c'), pairs)]
  transfers between devices with their start and end apart: 36 -> 36, of which waited for: 25 -> 21; matrix products, arithmetic and copies ran while one was open for 6% -> 5% of each run, Pallas kernels for 5% -> 5%
where the time goes in v7:
time: 145 us; the launch traced here: 143 us
  waiting for transfers between devices  72.5 us (50%)
  starting transfers between devices  49.1 us (34%)
  Pallas kernels  8.81 us (6%)
  matrix products  5.84 us (4%)
  other arithmetic  2.91 us (2%)
  local copies, waits for them, and re-layouts  2.51 us (2%)
    ppermute x31, waiting for transfers between devices, swap(): return lax.ppermute(array, (axis, 'c'), pairs)  64.9 us
    ppermute x31, starting transfers between devices, swap(): return lax.ppermute(array, (axis, 'c'), pairs)  44.6 us
    ppermute x2, waiting for transfers between devices, along_z(): return lambda v: lax.ppermute(v, ('zh', 'zl', 'c'), pairs)  6.35 us
    dot_general x8, matrix products, dot(): lax.dot_general(a, b, (((0,), (0,)), ((), ())), preferred_element_type=F32)  5.84 us
    pallas_call x3, Pallas kernels, place(): pl.pallas_call(kernel, out_shape=jax.ShapeDtypeStruct((8192, 256), BF16),...  4.84 us
    ppermute x2, starting transfers between devices, along_z(): return lambda v: lax.ppermute(v, ('zh', 'zl', 'c'), pairs)  3.74 us
    pallas_call x4, Pallas kernels, arrange(): pl.pallas_call(kernel, out_shape=[out] * 2, in_specs=[pl.BlockSpec(memory...  3.3 us
  transfers between devices with their start and end apart: 36, of which 21 were waited for; matrix products, arithmetic and copies ran while one was open for 5% of the time, Pallas kernels for 5%

profile of v7, /device:TPU:2, one launch (start us, length us, event | category | flops | bytes accessed | tf_op | source)
XLA Modules:
  0.0 143.0 jit_solution(6579254857834295271)
XLA Ops:
  0.8 2.2 %copy-done = bf16[256,8192]{1,0:T(8,128)(2,1)S(1)} copy-done((bf16[256,8192]{1,0:T(8,128)(2,1)S(1)}, bf16[256,8192]{1,0:T(8,128)(2,1)}, u32[]{:S(2)}) %copy-start) | copy-done | bytes 4194328
  4.4 1.7 %collective-permute-start.3 = (bf16[512,1024]{1,0:T(8,128)(2,1)S(1)}, bf16[512,1024]{1,0:T(8,128)(2,1)S(1)}, u32[]{:S(2)}, u32[]{:S(2)}) collective-permute-start(bf16[512,1024]{1,0:T(8,128)(2,1)S(1)} %constant_dynamic-update-slice_fusion), channel_id=1, source_target_pairs={{0,16},{1,49},{16,0},{17,33},{32,48},{33,17},{48,32},{49,1},{2,18}... | collective-permute-start | bytes 3145736 | tf_op jit(solution)/shard_map/ppermute | solution.py:25
  8.9 2.4 %collective-permute-start.5 = (bf16[512,512]{1,0:T(8,128)(2,1)S(1)}, bf16[512,512]{1,0:T(8,128)(2,1)S(1)}, u32[]{:S(2)}, u32[]{:S(2)}) collective-permute-start(bf16[512,512]{1,0:T(8,128)(2,1)S(1)} %get-tuple-element.36), channel_id=1, source_target_pairs={{0,4},{1,13},{4,0},{5,9},{8,12},{9,5},{12,8},{13,1},{2,6},{3,15},{... | collective-permute-start | bytes 1572872 | tf_op jit(solution)/shard_map/ppermute | solution.py:25
  12.1 7.2 %collective-permute-done.3 = bf16[512,1024]{1,0:T(8,128)(2,1)S(1)} collective-permute-done((bf16[512,1024]{1,0:T(8,128)(2,1)S(1)}, bf16[512,1024]{1,0:T(8,128)(2,1)S(1)}, u32[]{:S(2)}, u32[]{:S(2)}) %collective-permute-start.3) | collective-permute-done | bytes 1048608 | tf_op jit(solution)/shard_map/ppermute | solution.py:25
  19.3 1.6 %collective-permute-done.2 = bf16[512,1024]{1,0:T(8,128)(2,1)S(1)} collective-permute-done((bf16[512,1024]{1,0:T(8,128)(2,1)S(1)}, bf16[512,1024]{1,0:T(8,128)(2,1)S(1)}, u32[]{:S(2)}, u32[]{:S(2)}) %collective-permute-start.2) | collective-permute-done | bytes 1048608 | tf_op jit(solution)/shard_map/ppermute | solution.py:25
  21.6 1.9 %collective-permute-start.9 = (bf16[512,512]{1,0:T(8,128)(2,1)S(1)}, bf16[512,512]{1,0:T(8,128)(2,1)S(1)}, u32[]{:S(2)}, u32[]{:S(2)}) collective-permute-start(bf16[512,512]{1,0:T(8,128)(2,1)S(1)} %get-tuple-element.38), channel_id=1, source_target_pairs={{0,16},{1,49},{16,0},{17,33},{32,48},{33,17},{48,32},{49,1},{2,18}... | collective-permute-start | bytes 1572872 | tf_op jit(solution)/shard_map/ppermute | solution.py:25
  31.0 2.2 %collective-permute-start.6 = (f16[512,1024]{1,0:T(8,128)(2,1)S(1)}, f16[512,1024]{1,0:T(8,128)(2,1)S(1)}, u32[]{:S(2)}, u32[]{:S(2)}) collective-permute-start(f16[512,1024]{1,0:T(8,128)(2,1)S(1)} %multiply_convert_fusion.1), channel_id=1, source_target_pairs={{0,12},{1,5},{4,8},{5,1},{8,4},{9,13},{12,0},{13,9},{2,14},{3,7},{... | collective-permute-start | bytes 3145736 | tf_op jit(solution)/shard_map/ppermute | solution.py:25
  34.7 10.3 %collective-permute-done.11 = f16[512,1024]{1,0:T(8,128)(2,1)S(1)} collective-permute-done((f16[512,1024]{1,0:T(8,128)(2,1)S(1)}, f16[512,1024]{1,0:T(8,128)(2,1)S(1)}, u32[]{:S(2)}, u32[]{:S(2)}) %collective-permute-start.11) | collective-permute-done | bytes 1048608 | tf_op jit(solution)/shard_map/ppermute | solution.py:25
  47.3 7.6 %collective-permute-done.12 = f16[256,1024]{1,0:T(8,128)(2,1)S(1)} collective-permute-done((f16[256,1024]{1,0:T(8,128)(2,1)S(1)}, f16[256,1024]{1,0:T(8,128)(2,1)S(1)}, u32[]{:S(2)}, u32[]{:S(2)}) %collective-permute-start.12) | collective-permute-done | bytes 524320 | tf_op jit(solution)/shard_map/ppermute | solution.py:25
  56.8 2.4 %collective-permute-start.8 = (f16[128,1024]{1,0:T(8,128)(2,1)S(1)}, f16[128,1024]{1,0:T(8,128)(2,1)S(1)}, u32[]{:S(2)}, u32[]{:S(2)}) collective-permute-start(f16[128,1024]{1,0:T(8,128)(2,1)S(1)} %fusion.8), channel_id=1, source_target_pairs={{0,48},{1,17},{16,32},{17,1},{32,16},{33,49},{48,0},{49,33},{2,50}... | collective-permute-start | bytes 786440 | tf_op jit(solution)/shard_map/ppermute | solution.py:25
  59.1 2.5 %collective-permute-done.13 = f16[128,1024]{1,0:T(8,128)(2,1)S(1)} collective-permute-done((f16[128,1024]{1,0:T(8,128)(2,1)S(1)}, f16[128,1024]{1,0:T(8,128)(2,1)S(1)}, u32[]{:S(2)}, u32[]{:S(2)}) %collective-permute-start.13) | collective-permute-done | bytes 262176 | tf_op jit(solution)/shard_map/ppermute | solution.py:25
  61.8 2.7 %collective-permute-done.8 = f16[128,1024]{1,0:T(8,128)(2,1)S(1)} collective-permute-done((f16[128,1024]{1,0:T(8,128)(2,1)S(1)}, f16[128,1024]{1,0:T(8,128)(2,1)S(1)}, u32[]{:S(2)}, u32[]{:S(2)}) %collective-permute-start.8) | collective-permute-done | bytes 262176 | tf_op jit(solution)/shard_map/ppermute | solution.py:25
  64.8 2.0 %collective-permute-start.14 = (f16[256,256]{1,0:T(8,128)(2,1)S(1)}, f16[256,256]{1,0:T(8,128)(2,1)S(1)}, u32[]{:S(2)}, u32[]{:S(2)}) collective-permute-start(f16[256,256]{1,0:T(8,128)(2,1)S(1)} %get-tuple-element.55), channel_id=1, source_target_pairs={{0,2},{1,195},{2,0},{3,65},{64,66},{65,3},{66,64},{67,129},{128,13... | collective-permute-start | bytes 393224 | tf_op jit(solution)/shard_map/ppermute | solution.py:191
  66.8 1.7 %collective-permute-start.16 = (f16[256,256]{1,0:T(8,128)(2,1)S(1)}, f16[256,256]{1,0:T(8,128)(2,1)S(1)}, u32[]{:S(2)}, u32[]{:S(2)}) collective-permute-start(f16[256,256]{1,0:T(8,128)(2,1)S(1)} %get-tuple-element.56), channel_id=1, source_target_pairs={{0,3},{1,194},{2,1},{3,64},{64,67},{65,2},{66,65},{67,128},{128,13... | collective-permute-start | bytes 393224 | tf_op jit(solution)/shard_map/ppermute | solution.py:191
  69.9 5.0 %collective-permute-done.16 = f16[256,256]{1,0:T(8,128)(2,1)S(1)} collective-permute-done((f16[256,256]{1,0:T(8,128)(2,1)S(1)}, f16[256,256]{1,0:T(8,128)(2,1)S(1)}, u32[]{:S(2)}, u32[]{:S(2)}) %collective-permute-start.16) | collective-permute-done | bytes 131104 | tf_op jit(solution)/shard_map/ppermute | solution.py:191
  75.9 9.0 %collective-permute-done.17 = f32[256,256]{1,0:T(8,128)S(1)} collective-permute-done((f32[256,256]{1,0:T(8,128)S(1)}, f32[256,256]{1,0:T(8,128)S(1)}, u32[]{:S(2)}, u32[]{:S(2)}) %collective-permute-start.17) | collective-permute-done | bytes 262176 | tf_op jit(solution)/shard_map/ppermute | solution.py:25
  84.9 2.7 %collective-permute-start.18 = (f32[128,256]{1,0:T(8,128)S(1)}, f32[128,256]{1,0:T(8,128)S(1)}, u32[]{:S(2)}, u32[]{:S(2)}) collective-permute-start(f32[128,256]{1,0:T(8,128)S(1)} %slice_add_fusion.7), channel_id=1, source_target_pairs={{0,192},{1,65},{64,128},{65,1},{128,64},{129,193},{192,0},{193,129... | collective-permute-start | bytes 393224 | tf_op jit(solution)/shard_map/ppermute | solution.py:25
  87.7 5.8 %collective-permute-done.18 = f32[128,256]{1,0:T(8,128)S(1)} collective-permute-done((f32[128,256]{1,0:T(8,128)S(1)}, f32[128,256]{1,0:T(8,128)S(1)}, u32[]{:S(2)}, u32[]{:S(2)}) %collective-permute-start.18) | collective-permute-done | bytes 131104 | tf_op jit(solution)/shard_map/ppermute | solution.py:25
  95.0 3.5 %collective-permute-start.20 = (bf16[128,256]{1,0:T(8,128)(2,1)S(1)}, bf16[128,256]{1,0:T(8,128)(2,1)S(1)}, u32[]{:S(2)}, u32[]{:S(2)}) collective-permute-start(bf16[128,256]{1,0:T(8,128)(2,1)S(1)} %get-tuple-element.45), channel_id=1, source_target_pairs={{0,128},{1,129},{64,192},{65,193},{128,0},{129,1},{192,64},{193,65... | collective-permute-start | bytes 196616 | tf_op jit(solution)/shard_map/ppermute | solution.py:25
  98.5 2.3 %collective-permute-start.19 = (bf16[128,256]{1,0:T(8,128)(2,1)S(1)}, bf16[128,256]{1,0:T(8,128)(2,1)S(1)}, u32[]{:S(2)}, u32[]{:S(2)}) collective-permute-start(bf16[128,256]{1,0:T(8,128)(2,1)S(1)} %get-tuple-element.45), channel_id=1, source_target_pairs={{0,192},{1,65},{64,128},{65,1},{128,64},{129,193},{192,0},{193,129... | collective-permute-start | bytes 196616 | tf_op jit(solution)/shard_map/ppermute | solution.py:25
  101.2 2.3 %collective-permute-start.25 = (bf16[256,256]{1,0:T(8,128)(2,1)S(1)}, bf16[256,256]{1,0:T(8,128)(2,1)S(1)}, u32[]{:S(2)}, u32[]{:S(2)}) collective-permute-start(bf16[256,256]{1,0:T(8,128)(2,1)S(1)} %pad_maximum_fusion.3), channel_id=1, source_target_pairs={{0,48},{1,17},{16,32},{17,1},{32,16},{33,49},{48,0},{49,33},{2,50}... | collective-permute-start | bytes 393224 | tf_op jit(solution)/shard_map/ppermute | solution.py:25
  105.0 3.5 %collective-permute-start.27 = (bf16[256,256]{1,0:T(8,128)(2,1)S(1)}, bf16[256,256]{1,0:T(8,128)(2,1)S(1)}, u32[]{:S(2)}, u32[]{:S(2)}) collective-permute-start(bf16[256,256]{1,0:T(8,128)(2,1)S(1)} %get-tuple-element.61), channel_id=1, source_target_pairs={{0,8},{1,9},{4,12},{5,13},{8,0},{9,1},{12,4},{13,5},{2,10},{3,11},... | collective-permute-start | bytes 393224 | tf_op jit(solution)/shard_map/ppermute | solution.py:25
  110.2 1.5 %collective-permute-done.27 = bf16[256,256]{1,0:T(8,128)(2,1)S(1)} collective-permute-done((bf16[256,256]{1,0:T(8,128)(2,1)S(1)}, bf16[256,256]{1,0:T(8,128)(2,1)S(1)}, u32[]{:S(2)}, u32[]{:S(2)}) %collective-permute-start.27) | collective-permute-done | bytes 131104 | tf_op jit(solution)/shard_map/ppermute | solution.py:25
  111.7 1.9 %collective-permute-done.21 = bf16[256,256]{1,0:T(8,128)(2,1)S(1)} collective-permute-done((bf16[256,256]{1,0:T(8,128)(2,1)S(1)}, bf16[256,256]{1,0:T(8,128)(2,1)S(1)}, u32[]{:S(2)}, u32[]{:S(2)}) %collective-permute-start.21) | collective-permute-done | bytes 131104 | tf_op jit(solution)/shard_map/ppermute | solution.py:25
  113.7 2.0 %collective-permute-start.30 = (bf16[1024,256]{1,0:T(8,128)(2,1)S(1)}, bf16[1024,256]{1,0:T(8,128)(2,1)S(1)}, u32[]{:S(2)}, u32[]{:S(2)}) collective-permute-start(bf16[1024,256]{1,0:T(8,128)(2,1)S(1)} %constant_dynamic-update-slice_fusion.9.refs_3_), channel_id=1, source_target_pairs={{0,48},{1,17},{16,32},{17,1},{32,16},{33,49},{48,0},{49,33},{2,50}... | collective-permute-start | bytes 1572872 | tf_op jit(solution)/shard_map/ppermute | solution.py:25
  116.9 2.8 %collective-permute-start.32 = (bf16[1024,256]{1,0:T(8,128)(2,1)S(1)}, bf16[1024,256]{1,0:T(8,128)(2,1)S(1)}, u32[]{:S(2)}, u32[]{:S(2)}) collective-permute-start(bf16[1024,256]{1,0:T(8,128)(2,1)S(1)} %constant_dynamic-update-slice_fusion.4.refs_0_), channel_id=1, source_target_pairs={{0,4},{1,13},{4,0},{5,9},{8,12},{9,5},{12,8},{13,1},{2,6},{3,15},{... | collective-permute-start | bytes 1572872 | tf_op jit(solution)/shard_map/ppermute | solution.py:25
  119.7 9.3 %collective-permute-done.30.refs_5_ = bf16[1024,256]{1,0:T(8,128)(2,1)S(1)} collective-permute-done((bf16[1024,256]{1,0:T(8,128)(2,1)S(1)}, bf16[1024,256]{1,0:T(8,128)(2,1)S(1)}, u32[]{:S(2)}, u32[]{:S(2)}) %collective-permute-start.30) | collective-permute-done | bytes 524320 | tf_op jit(solution)/shard_map/ppermute | solution.py:25
  129.1 1.4 %collective-permute-done.34.refs_2_ = bf16[1024,256]{1,0:T(8,128)(2,1)S(1)} collective-permute-done((bf16[1024,256]{1,0:T(8,128)(2,1)S(1)}, bf16[1024,256]{1,0:T(8,128)(2,1)S(1)}, u32[]{:S(2)}, u32[]{:S(2)}) %collective-permute-start.34) | collective-permute-done | bytes 524320 | tf_op jit(solution)/shard_map/ppermute | solution.py:25
  131.8 2.0 %collective-permute-start.33 = (bf16[512,256]{1,0:T(8,128)(2,1)S(1)}, bf16[512,256]{1,0:T(8,128)(2,1)S(1)}, u32[]{:S(2)}, u32[]{:S(2)}) collective-permute-start(bf16[512,256]{1,0:T(8,128)(2,1)S(1)} %slice.138), channel_id=1, source_target_pairs={{0,12},{1,5},{4,8},{5,1},{8,4},{9,13},{12,0},{13,9},{2,14},{3,7},{... | collective-permute-start | bytes 786440 | tf_op jit(solution)/shard_map/ppermute | solution.py:25
  133.8 1.6 %collective-permute-start.29 = (bf16[512,256]{1,0:T(8,128)(2,1)S(1)}, bf16[512,256]{1,0:T(8,128)(2,1)S(1)}, u32[]{:S(2)}, u32[]{:S(2)}) collective-permute-start(bf16[512,256]{1,0:T(8,128)(2,1)S(1)} %slice.136), channel_id=1, source_target_pairs={{0,48},{1,17},{16,32},{17,1},{32,16},{33,49},{48,0},{49,33},{2,50}... | collective-permute-start | bytes 786440 | tf_op jit(solution)/shard_map/ppermute | solution.py:25
  135.4 2.2 %shard_map.89.refs_2_ = bf16[8192,256]{1,0:T(8,128)(2,1)} custom-call(s32[4]{0:T(128)S(1)} %pad_add_fusion.where_ref, bf16[1024,256]{1,0:T(8,128)(2,1)S(1)} %constant_dynamic-update-slice_fusion.4.refs_0_, bf16[1024,256]{1,0:T(8,128)(2,1)S(1)} %collective-permute-done.32.refs_1_, bf16[1024,256]{1,0:T(8,128)(2,1)S(1)} %collective-permute-done.34.refs_2_, ...), custom_call_target="tpu_custom_call" | custom-call | bytes 6291456 | tf_op jit(solution)/shard_map/pallas_call | solution.py:117
  139.6 1.8 %collective-permute-done.29.refs_0_ = bf16[512,256]{1,0:T(8,128)(2,1)S(1)} collective-permute-done((bf16[512,256]{1,0:T(8,128)(2,1)S(1)}, bf16[512,256]{1,0:T(8,128)(2,1)S(1)}, u32[]{:S(2)}, u32[]{:S(2)}) %collective-permute-start.29) | collective-permute-done | bytes 262176 | tf_op jit(solution)/shard_map/ppermute | solution.py:25
  (103 shorter events, 32.5 us)
Async XLA Ops:
  4.4 14.9 %collective-permute-start.3 = (bf16[512,1024]{1,0:T(8,128)(2,1)S(1)}, bf16[512,1024]{1,0:T(8,128)(2,1)S(1)}, u32[]{:S(2)}, u32[]{:S(2)}) collective-permute-start(bf16[512,1024]{1,0:T(8,128)(2,1)S(1)} %constant_dynamic-update-slice_fusion), channel_id=1, source_target_pairs={{0,16},{1,49},{16,0},{17,33},{32,48},{33,17},{48,32},{49,1},{2,18}... | collective-permute-start | bytes 3145736 | tf_op jit(solution)/shard_map/ppermute | solution.py:25
  6.0 14.8 %collective-permute-start.2 = (bf16[512,1024]{1,0:T(8,128)(2,1)S(1)}, bf16[512,1024]{1,0:T(8,128)(2,1)S(1)}, u32[]{:S(2)}, u32[]{:S(2)}) collective-permute-start(bf16[512,1024]{1,0:T(8,128)(2,1)S(1)} %constant_dynamic-update-slice_fusion), channel_id=1, source_target_pairs={{0,4},{1,13},{4,0},{5,9},{8,12},{9,5},{12,8},{13,1},{2,6},{3,15},{... | collective-permute-start | bytes 3145736 | tf_op jit(solution)/shard_map/ppermute | solution.py:25
  8.9 21.4 %collective-permute-start.5 = (bf16[512,512]{1,0:T(8,128)(2,1)S(1)}, bf16[512,512]{1,0:T(8,128)(2,1)S(1)}, u32[]{:S(2)}, u32[]{:S(2)}) collective-permute-start(bf16[512,512]{1,0:T(8,128)(2,1)S(1)} %get-tuple-element.36), channel_id=1, source_target_pairs={{0,4},{1,13},{4,0},{5,9},{8,12},{9,5},{12,8},{13,1},{2,6},{3,15},{... | collective-permute-start | bytes 1572872 | tf_op jit(solution)/shard_map/ppermute | solution.py:25
  11.3 16.9 %collective-permute-start.10 = (bf16[512,512]{1,0:T(8,128)(2,1)S(1)}, bf16[512,512]{1,0:T(8,128)(2,1)S(1)}, u32[]{:S(2)}, u32[]{:S(2)}) collective-permute-start(bf16[512,512]{1,0:T(8,128)(2,1)S(1)} %get-tuple-element.41), channel_id=1, source_target_pairs={{0,16},{1,49},{16,0},{17,33},{32,48},{33,17},{48,32},{49,1},{2,18}... | collective-permute-start | bytes 1572872 | tf_op jit(solution)/shard_map/ppermute | solution.py:25
  20.8 12.4 %collective-permute-start.4 = (bf16[512,512]{1,0:T(8,128)(2,1)S(1)}, bf16[512,512]{1,0:T(8,128)(2,1)S(1)}, u32[]{:S(2)}, u32[]{:S(2)}) collective-permute-start(bf16[512,512]{1,0:T(8,128)(2,1)S(1)} %get-tuple-element.33), channel_id=1, source_target_pairs={{0,4},{1,13},{4,0},{5,9},{8,12},{9,5},{12,8},{13,1},{2,6},{3,15},{... | collective-permute-start | bytes 1572872 | tf_op jit(solution)/shard_map/ppermute | solution.py:25
  21.6 12.4 %collective-permute-start.9 = (bf16[512,512]{1,0:T(8,128)(2,1)S(1)}, bf16[512,512]{1,0:T(8,128)(2,1)S(1)}, u32[]{:S(2)}, u32[]{:S(2)}) collective-permute-start(bf16[512,512]{1,0:T(8,128)(2,1)S(1)} %get-tuple-element.38), channel_id=1, source_target_pairs={{0,16},{1,49},{16,0},{17,33},{32,48},{33,17},{48,32},{49,1},{2,18}... | collective-permute-start | bytes 1572872 | tf_op jit(solution)/shard_map/ppermute | solution.py:25
  28.9 16.1 %collective-permute-start.11 = (f16[512,1024]{1,0:T(8,128)(2,1)S(1)}, f16[512,1024]{1,0:T(8,128)(2,1)S(1)}, u32[]{:S(2)}, u32[]{:S(2)}) collective-permute-start(f16[512,1024]{1,0:T(8,128)(2,1)S(1)} %multiply_convert_fusion), channel_id=1, source_target_pairs={{0,48},{1,17},{16,32},{17,1},{32,16},{33,49},{48,0},{49,33},{2,50}... | collective-permute-start | bytes 3145736 | tf_op jit(solution)/shard_map/ppermute | solution.py:25
  31.0 15.7 %collective-permute-start.6 = (f16[512,1024]{1,0:T(8,128)(2,1)S(1)}, f16[512,1024]{1,0:T(8,128)(2,1)S(1)}, u32[]{:S(2)}, u32[]{:S(2)}) collective-permute-start(f16[512,1024]{1,0:T(8,128)(2,1)S(1)} %multiply_convert_fusion.1), channel_id=1, source_target_pairs={{0,12},{1,5},{4,8},{5,1},{8,4},{9,13},{12,0},{13,9},{2,14},{3,7},{... | collective-permute-start | bytes 3145736 | tf_op jit(solution)/shard_map/ppermute | solution.py:25
  45.5 9.4 %collective-permute-start.12 = (f16[256,1024]{1,0:T(8,128)(2,1)S(1)}, f16[256,1024]{1,0:T(8,128)(2,1)S(1)}, u32[]{:S(2)}, u32[]{:S(2)}) collective-permute-start(f16[256,1024]{1,0:T(8,128)(2,1)S(1)} %fusion.1), channel_id=1, source_target_pairs={{0,4},{1,13},{4,0},{5,9},{8,12},{9,5},{12,8},{13,1},{2,6},{3,15},{... | collective-permute-start | bytes 1572872 | tf_op jit(solution)/shard_map/ppermute | solution.py:25
  47.2 9.3 %collective-permute-start.7 = (f16[256,1024]{1,0:T(8,128)(2,1)S(1)}, f16[256,1024]{1,0:T(8,128)(2,1)S(1)}, u32[]{:S(2)}, u32[]{:S(2)}) collective-permute-start(f16[256,1024]{1,0:T(8,128)(2,1)S(1)} %fusion.4), channel_id=1, source_target_pairs={{0,16},{1,49},{16,0},{17,33},{32,48},{33,17},{48,32},{49,1},{2,18}... | collective-permute-start | bytes 1572872 | tf_op jit(solution)/shard_map/ppermute | solution.py:25
  55.2 6.5 %collective-permute-start.13 = (f16[128,1024]{1,0:T(8,128)(2,1)S(1)}, f16[128,1024]{1,0:T(8,128)(2,1)S(1)}, u32[]{:S(2)}, u32[]{:S(2)}) collective-permute-start(f16[128,1024]{1,0:T(8,128)(2,1)S(1)} %fusion.7), channel_id=1, source_target_pairs={{0,12},{1,5},{4,8},{5,1},{8,4},{9,13},{12,0},{13,9},{2,14},{3,7},{... | collective-permute-start | bytes 786440 | tf_op jit(solution)/shard_map/ppermute | solution.py:25
  56.8 7.7 %collective-permute-start.8 = (f16[128,1024]{1,0:T(8,128)(2,1)S(1)}, f16[128,1024]{1,0:T(8,128)(2,1)S(1)}, u32[]{:S(2)}, u32[]{:S(2)}) collective-permute-start(f16[128,1024]{1,0:T(8,128)(2,1)S(1)} %fusion.8), channel_id=1, source_target_pairs={{0,48},{1,17},{16,32},{17,1},{32,16},{33,49},{48,0},{49,33},{2,50}... | collective-permute-start | bytes 786440 | tf_op jit(solution)/shard_map/ppermute | solution.py:25
  64.7 10.3 %collective-permute-start.15 = (f32[256,256]{1,0:T(8,128)S(1)}, f32[256,256]{1,0:T(8,128)S(1)}, u32[]{:S(2)}, u32[]{:S(2)}) collective-permute-start(f32[256,256]{1,0:T(8,128)S(1)} %slice_select_fusion), channel_id=1, source_target_pairs={{0,1},{1,0},{2,3},{3,2},{4,5},{5,4},{6,7},{7,6},{8,9},{9,8},{10,11... | collective-permute-start | bytes 786440 | tf_op jit(solution)/shard_map/ppermute | solution.py:29
  66.8 8.1 %collective-permute-start.16 = (f16[256,256]{1,0:T(8,128)(2,1)S(1)}, f16[256,256]{1,0:T(8,128)(2,1)S(1)}, u32[]{:S(2)}, u32[]{:S(2)}) collective-permute-start(f16[256,256]{1,0:T(8,128)(2,1)S(1)} %get-tuple-element.56), channel_id=1, source_target_pairs={{0,3},{1,194},{2,1},{3,64},{64,67},{65,2},{66,65},{67,128},{128,13... | collective-permute-start | bytes 393224 | tf_op jit(solution)/shard_map/ppermute | solution.py:191
  75.2 9.7 %collective-permute-start.17 = (f32[256,256]{1,0:T(8,128)S(1)}, f32[256,256]{1,0:T(8,128)S(1)}, u32[]{:S(2)}, u32[]{:S(2)}) collective-permute-start(f32[256,256]{1,0:T(8,128)S(1)} %pad_maximum_fusion.2), channel_id=1, source_target_pairs={{0,64},{1,193},{64,0},{65,129},{128,192},{129,65},{192,128},{193,1... | collective-permute-start | bytes 786440 | tf_op jit(solution)/shard_map/ppermute | solution.py:25
  84.9 8.6 %collective-permute-start.18 = (f32[128,256]{1,0:T(8,128)S(1)}, f32[128,256]{1,0:T(8,128)S(1)}, u32[]{:S(2)}, u32[]{:S(2)}) collective-permute-start(f32[128,256]{1,0:T(8,128)S(1)} %slice_add_fusion.7), channel_id=1, source_target_pairs={{0,192},{1,65},{64,128},{65,1},{128,64},{129,193},{192,0},{193,129... | collective-permute-start | bytes 393224 | tf_op jit(solution)/shard_map/ppermute | solution.py:25
  94.3 6.7 %collective-permute-start.23 = (bf16[128,256]{1,0:T(8,128)(2,1)S(1)}, bf16[128,256]{1,0:T(8,128)(2,1)S(1)}, u32[]{:S(2)}, u32[]{:S(2)}) collective-permute-start(bf16[128,256]{1,0:T(8,128)(2,1)S(1)} %get-tuple-element.45), channel_id=1, source_target_pairs={{0,64},{1,193},{64,0},{65,129},{128,192},{129,65},{192,128},{193,1... | collective-permute-start | bytes 196616 | tf_op jit(solution)/shard_map/ppermute | solution.py:25
  95.0 10.0 %collective-permute-start.20 = (bf16[128,256]{1,0:T(8,128)(2,1)S(1)}, bf16[128,256]{1,0:T(8,128)(2,1)S(1)}, u32[]{:S(2)}, u32[]{:S(2)}) collective-permute-start(bf16[128,256]{1,0:T(8,128)(2,1)S(1)} %get-tuple-element.45), channel_id=1, source_target_pairs={{0,128},{1,129},{64,192},{65,193},{128,0},{129,1},{192,64},{193,65... | collective-permute-start | bytes 196616 | tf_op jit(solution)/shard_map/ppermute | solution.py:25
  98.5 6.5 %collective-permute-start.19 = (bf16[128,256]{1,0:T(8,128)(2,1)S(1)}, bf16[128,256]{1,0:T(8,128)(2,1)S(1)}, u32[]{:S(2)}, u32[]{:S(2)}) collective-permute-start(bf16[128,256]{1,0:T(8,128)(2,1)S(1)} %get-tuple-element.45), channel_id=1, source_target_pairs={{0,192},{1,65},{64,128},{65,1},{128,64},{129,193},{192,0},{193,129... | collective-permute-start | bytes 196616 | tf_op jit(solution)/shard_map/ppermute | solution.py:25
  101.0 9.1 %collective-permute-start.26 = (bf16[256,256]{1,0:T(8,128)(2,1)S(1)}, bf16[256,256]{1,0:T(8,128)(2,1)S(1)}, u32[]{:S(2)}, u32[]{:S(2)}) collective-permute-start(bf16[256,256]{1,0:T(8,128)(2,1)S(1)} %pad_maximum_fusion.3), channel_id=1, source_target_pairs={{0,32},{1,33},{16,48},{17,49},{32,0},{33,1},{48,16},{49,17},{2,34}... | collective-permute-start | bytes 393224 | tf_op jit(solution)/shard_map/ppermute | solution.py:25
  101.2 8.9 %collective-permute-start.25 = (bf16[256,256]{1,0:T(8,128)(2,1)S(1)}, bf16[256,256]{1,0:T(8,128)(2,1)S(1)}, u32[]{:S(2)}, u32[]{:S(2)}) collective-permute-start(bf16[256,256]{1,0:T(8,128)(2,1)S(1)} %pad_maximum_fusion.3), channel_id=1, source_target_pairs={{0,48},{1,17},{16,32},{17,1},{32,16},{33,49},{48,0},{49,33},{2,50}... | collective-permute-start | bytes 393224 | tf_op jit(solution)/shard_map/ppermute | solution.py:25
  103.5 5.2 %collective-permute-start.24 = (bf16[256,256]{1,0:T(8,128)(2,1)S(1)}, bf16[256,256]{1,0:T(8,128)(2,1)S(1)}, u32[]{:S(2)}, u32[]{:S(2)}) collective-permute-start(bf16[256,256]{1,0:T(8,128)(2,1)S(1)} %pad_maximum_fusion.3), channel_id=1, source_target_pairs={{0,16},{1,49},{16,0},{17,33},{32,48},{33,17},{48,32},{49,1},{2,18}... | collective-permute-start | bytes 393224 | tf_op jit(solution)/shard_map/ppermute | solution.py:25
  105.0 6.7 %collective-permute-start.27 = (bf16[256,256]{1,0:T(8,128)(2,1)S(1)}, bf16[256,256]{1,0:T(8,128)(2,1)S(1)}, u32[]{:S(2)}, u32[]{:S(2)}) collective-permute-start(bf16[256,256]{1,0:T(8,128)(2,1)S(1)} %get-tuple-element.61), channel_id=1, source_target_pairs={{0,8},{1,9},{4,12},{5,13},{8,0},{9,1},{12,4},{13,5},{2,10},{3,11},... | collective-permute-start | bytes 393224 | tf_op jit(solution)/shard_map/ppermute | solution.py:25
  108.5 5.2 %collective-permute-start.22 = (bf16[256,256]{1,0:T(8,128)(2,1)S(1)}, bf16[256,256]{1,0:T(8,128)(2,1)S(1)}, u32[]{:S(2)}, u32[]{:S(2)}) collective-permute-start(bf16[256,256]{1,0:T(8,128)(2,1)S(1)} %get-tuple-element.61), channel_id=1, source_target_pairs={{0,12},{1,5},{4,8},{5,1},{8,4},{9,13},{12,0},{13,9},{2,14},{3,7},{... | collective-permute-start | bytes 393224 | tf_op jit(solution)/shard_map/ppermute | solution.py:25
  113.7 15.3 %collective-permute-start.30 = (bf16[1024,256]{1,0:T(8,128)(2,1)S(1)}, bf16[1024,256]{1,0:T(8,128)(2,1)S(1)}, u32[]{:S(2)}, u32[]{:S(2)}) collective-permute-start(bf16[1024,256]{1,0:T(8,128)(2,1)S(1)} %constant_dynamic-update-slice_fusion.9.refs_3_), channel_id=1, source_target_pairs={{0,48},{1,17},{16,32},{17,1},{32,16},{33,49},{48,0},{49,33},{2,50}... | collective-permute-start | bytes 1572872 | tf_op jit(solution)/shard_map/ppermute | solution.py:25
  115.7 14.9 %collective-permute-start.34 = (bf16[1024,256]{1,0:T(8,128)(2,1)S(1)}, bf16[1024,256]{1,0:T(8,128)(2,1)S(1)}, u32[]{:S(2)}, u32[]{:S(2)}) collective-permute-start(bf16[1024,256]{1,0:T(8,128)(2,1)S(1)} %constant_dynamic-update-slice_fusion.4.refs_0_), channel_id=1, source_target_pairs={{0,12},{1,5},{4,8},{5,1},{8,4},{9,13},{12,0},{13,9},{2,14},{3,7},{... | collective-permute-start | bytes 1572872 | tf_op jit(solution)/shard_map/ppermute | solution.py:25
  116.9 14.9 %collective-permute-start.32 = (bf16[1024,256]{1,0:T(8,128)(2,1)S(1)}, bf16[1024,256]{1,0:T(8,128)(2,1)S(1)}, u32[]{:S(2)}, u32[]{:S(2)}) collective-permute-start(bf16[1024,256]{1,0:T(8,128)(2,1)S(1)} %constant_dynamic-update-slice_fusion.4.refs_0_), channel_id=1, source_target_pairs={{0,4},{1,13},{4,0},{5,9},{8,12},{9,5},{12,8},{13,1},{2,6},{3,15},{... | collective-permute-start | bytes 1572872 | tf_op jit(solution)/shard_map/ppermute | solution.py:25
  119.7 14.1 %collective-permute-start.28 = (bf16[1024,256]{1,0:T(8,128)(2,1)S(1)}, bf16[1024,256]{1,0:T(8,128)(2,1)S(1)}, u32[]{:S(2)}, u32[]{:S(2)}) collective-permute-start(bf16[1024,256]{1,0:T(8,128)(2,1)S(1)} %constant_dynamic-update-slice_fusion.9.refs_3_), channel_id=1, source_target_pairs={{0,16},{1,49},{16,0},{17,33},{32,48},{33,17},{48,32},{49,1},{2,18}... | collective-permute-start | bytes 1572872 | tf_op jit(solution)/shard_map/ppermute | solution.py:25
  129.0 10.6 %collective-permute-start.31 = (bf16[512,256]{1,0:T(8,128)(2,1)S(1)}, bf16[512,256]{1,0:T(8,128)(2,1)S(1)}, u32[]{:S(2)}, u32[]{:S(2)}) collective-permute-start(bf16[512,256]{1,0:T(8,128)(2,1)S(1)} %slice.137), channel_id=1, source_target_pairs={{0,16},{1,49},{16,0},{17,33},{32,48},{33,17},{48,32},{49,1},{2,18}... | collective-permute-start | bytes 786440 | tf_op jit(solution)/shard_map/ppermute | solution.py:25
  130.6 6.9 %collective-permute-start.35 = (bf16[512,256]{1,0:T(8,128)(2,1)S(1)}, bf16[512,256]{1,0:T(8,128)(2,1)S(1)}, u32[]{:S(2)}, u32[]{:S(2)}) collective-permute-start(bf16[512,256]{1,0:T(8,128)(2,1)S(1)} %slice.139), channel_id=1, source_target_pairs={{0,4},{1,13},{4,0},{5,9},{8,12},{9,5},{12,8},{13,1},{2,6},{3,15},{... | collective-permute-start | bytes 786440 | tf_op jit(solution)/shard_map/ppermute | solution.py:25
  131.8 6.5 %collective-permute-start.33 = (bf16[512,256]{1,0:T(8,128)(2,1)S(1)}, bf16[512,256]{1,0:T(8,128)(2,1)S(1)}, u32[]{:S(2)}, u32[]{:S(2)}) collective-permute-start(bf16[512,256]{1,0:T(8,128)(2,1)S(1)} %slice.138), channel_id=1, source_target_pairs={{0,12},{1,5},{4,8},{5,1},{8,4},{9,13},{12,0},{13,9},{2,14},{3,7},{... | collective-permute-start | bytes 786440 | tf_op jit(solution)/shard_map/ppermute | solution.py:25
  133.8 7.7 %collective-permute-start.29 = (bf16[512,256]{1,0:T(8,128)(2,1)S(1)}, bf16[512,256]{1,0:T(8,128)(2,1)S(1)}, u32[]{:S(2)}, u32[]{:S(2)}) collective-permute-start(bf16[512,256]{1,0:T(8,128)(2,1)S(1)} %slice.136), channel_id=1, source_target_pairs={{0,48},{1,17},{16,32},{17,1},{32,16},{33,49},{48,0},{49,33},{2,50}... | collective-permute-start | bytes 786440 | tf_op jit(solution)/shard_map/ppermute | solution.py:25
  (9 other events, 76.4 us)
